TPU v7x, 32 devices: a whole 2x2x4 slice. The times are simulated.
32 devices in a mesh: group: 2 (over x), shard: 8 (over z, y), dp: 2 (over core).
Axes of the slice: x: 2, y: 2, z: 4, core: 2. Of those that a mesh axis runs over, the one named last changes fastest.
Arguments:
- held_rows: bfloat16 [24576, 8192], P(('group', 'shard', 'dp')), parts along dimension 0, may hold values from -6 to 6
- block_home: int32 [192], P(('group', 'shard', 'dp')), parts along dimension 0, may hold values from -1 to 1, as said below
- block_len: int32 [192], P(('group', 'shard', 'dp')), parts along dimension 0, may hold values from 1 to 128
- block_adapter: int32 [192], P(('group', 'shard', 'dp')), parts along dimension 0, may hold values from 0 to 7
- adapter_down: bfloat16 [16, 16, 8192], P('group'), parts along dimension 0, may hold values from -0.0625 to 0.0625
- adapter_up: bfloat16 [16, 16, 1024], P('group'), parts along dimension 0, may hold values from -0.1875 to 0.1875
- value_weight: bfloat16 [8192, 1024], P('shard'), may hold values from -0.0625 to 0.0625
- adapter_owner: int32 [16], P('group'), parts along dimension 0, may hold values from 0 to 7, each once
- value_grad: bfloat16 [12288, 1024], P(('group', 'shard', 'dp')), parts along dimension 0, may hold values from -1.5 to 1.5
Outputs:
- value_projection_output: bfloat16 [12288, 1024], P(('group', 'shard', 'dp')), parts along dimension 0
- input_grad: bfloat16 [12288, 8192], P(('group', 'shard', 'dp')), parts along dimension 0
- grad_down: float32 [16, 16, 8192], P(('group', 'shard'), None, 'dp'), parts along dimension 0
- up_map_gradient: float32 [16, 16, 1024], P(('group', 'shard'), None, 'dp'), parts along dimension 0
There are 2 independent parts, one for each index of `group`. A program takes and returns all parts, laid end to end along the dimension named above; an argument that names none is the same for every part. Nothing has to cross between parts.
Inputs may be any that keep to these rules, and one draw needn't show every extreme that they name: `block_home`: slots p of chip s = p // 12 hold exactly 3 blocks with value 0 and 3 with value 1 on every chip; -1 marks an empty slot. One device (index along shard times 2 plus index along dp) holds at most 3 blocks for the other core of its chip, and in some chip of every draw each of its two devices holds exactly 3 blocks for the other. `adapter_owner`: A permutation.
All inputs are finite; a program needn't handle non-finite values.
Results may differ from a plain program's by a relative error of at most 0.0034.
Values may be sent and summed in bfloat16 or wider, within the bound.
No kernel may reach another device: no remote copies, remote signals or barrier semaphores. Data moves between devices by JAX's collectives and lax.ppermute only.
A program may use at most 192 MiB of HBM per device.

v0:
```python
import jax
import jax.numpy as jnp
from jax import lax
from jax.sharding import PartitionSpec as P

adapter_scale = 2.0


def pick_rows(live_flags, wanted):
    running = jnp.cumsum(live_flags)
    target = jnp.arange(1, wanted + 1, dtype=jnp.int32)
    matched = (live_flags[None, :] == 1) & (running[None, :] == target[:, None])
    positions = jnp.arange(live_flags.shape[0], dtype=jnp.int32)
    row_index = jnp.sum(jnp.where(matched, positions[None, :], 0), axis=1)
    present = jnp.any(matched, axis=1)
    return (row_index, present)


def body(
    held_rows,
    block_home,
    block_len,
    block_adapter,
    adapter_down,
    adapter_up,
    value_weight,
    adapter_owner,
    value_grad,
):
    hold_slots = block_home.shape[0]
    per_core = hold_slots // 2
    model_width = held_rows.shape[1]
    value_head_width = value_weight.shape[1]
    block_tokens = held_rows.shape[0] // hold_slots
    held_blocks = held_rows.reshape(hold_slots, block_tokens, model_width)
    outgoing_rows = []
    outgoing_len = []
    outgoing_adapter = []
    outgoing_live = []
    for target_core in range(2):
        wanted_flags = (block_home == target_core).astype(jnp.int32)
        slot_index, present = pick_rows(wanted_flags, per_core)
        outgoing_rows.append(jnp.take(held_blocks, slot_index, axis=0))
        outgoing_len.append(jnp.where(present, jnp.take(block_len, slot_index), 0))
        outgoing_adapter.append(jnp.where(present, jnp.take(block_adapter, slot_index), 0))
        outgoing_live.append(present.astype(jnp.int32))
    got_rows, got_len, got_adapter, got_live = (
        lax.all_to_all(jnp.stack(outgoing_rows), "dp", split_axis=0, concat_axis=0, tiled=True),
        lax.all_to_all(jnp.stack(outgoing_len), "dp", split_axis=0, concat_axis=0, tiled=True),
        lax.all_to_all(jnp.stack(outgoing_adapter), "dp", split_axis=0, concat_axis=0, tiled=True),
        lax.all_to_all(jnp.stack(outgoing_live), "dp", split_axis=0, concat_axis=0, tiled=True),
    )
    work_index, filled = pick_rows(got_live.reshape(-1), per_core)
    work_rows = jnp.take(
        got_rows.reshape(2 * per_core, block_tokens, model_width), work_index, axis=0
    )
    work_len = jnp.take(got_len.reshape(-1), work_index)
    work_adapter = jnp.take(got_adapter.reshape(-1), work_index)
    full_weight = lax.all_gather(value_weight, "shard", axis=0, tiled=True)
    flat_rows = work_rows.reshape(-1, model_width)
    down_rows = jnp.take(adapter_down, work_adapter, axis=0)
    up_weight_rows = jnp.take(adapter_up, work_adapter, axis=0)
    low_rank = jnp.einsum(
        "btd,brd->btr", work_rows, down_rows, preferred_element_type=jnp.float32
    ).astype(jnp.bfloat16)
    raised_rows = jnp.einsum(
        "btr,brk->btk", low_rank, up_weight_rows, preferred_element_type=jnp.float32
    )
    frozen_output = jnp.dot(flat_rows, full_weight, preferred_element_type=jnp.float32)
    value_projection_output = (
        frozen_output + adapter_scale * raised_rows.reshape(-1, value_head_width)
    ).astype(jnp.bfloat16)
    positions = jnp.arange(block_tokens, dtype=jnp.int32)
    live_mask = positions[None, :] < work_len[:, None]
    masked_tokens = jnp.where(
        live_mask[:, :, None],
        value_grad.reshape(per_core, block_tokens, value_head_width),
        jnp.zeros((), jnp.bfloat16),
    )
    returned_rank_rows = (
        adapter_scale
        * jnp.einsum(
            "uyc,uvc->uyv", masked_tokens, up_weight_rows, preferred_element_type=jnp.float32
        )
    ).astype(jnp.bfloat16)
    flattened_gradient = masked_tokens.reshape(-1, value_head_width)
    through_base = lax.dot_general(
        flattened_gradient,
        full_weight,
        (((1,), (1,)), ((), ())),
        preferred_element_type=jnp.float32,
    )
    through_low = jnp.einsum(
        "btr,brd->btd", returned_rank_rows, down_rows, preferred_element_type=jnp.float32
    )
    input_grad = (through_base + through_low.reshape(-1, model_width)).astype(jnp.bfloat16)
    shards = lax.axis_size("shard")
    core_count = lax.axis_size("dp")
    adapters = adapter_down.shape[0]
    per_shard = adapters // shards
    rank_size = adapter_down.shape[1]
    owner_slot = jnp.take(adapter_owner, work_adapter)
    one_hot = (owner_slot[:, None] == jnp.arange(adapters, dtype=jnp.int32)[None, :]).astype(
        jnp.bfloat16
    )
    spread_back = (returned_rank_rows[:, :, None, :] * one_hot[:, None, :, None]).reshape(
        -1, shards, per_shard, rank_size
    )
    scattered_rank_rows = (low_rank[:, :, None, :] * one_hot[:, None, :, None]).reshape(
        -1, shards, per_shard, rank_size
    )
    grad_down = jnp.einsum(
        "tsar,tch->scarh",
        spread_back,
        flat_rows.reshape(-1, core_count, model_width // core_count),
        preferred_element_type=jnp.float32,
    )
    up_map_gradient = adapter_scale * jnp.einsum(
        "tsar,tch->scarh",
        scattered_rank_rows,
        flattened_gradient.reshape(-1, core_count, value_head_width // core_count),
        preferred_element_type=jnp.float32,
    )
    own_down, own_up = (
        lax.psum_scatter(
            grad_down.reshape(shards * core_count, per_shard, rank_size, -1),
            ("shard", "dp"),
            scatter_dimension=0,
            tiled=True,
        ),
        lax.psum_scatter(
            up_map_gradient.reshape(shards * core_count, per_shard, rank_size, -1),
            ("shard", "dp"),
            scatter_dimension=0,
            tiled=True,
        ),
    )
    return (
        value_projection_output,
        input_grad,
        own_down.reshape(per_shard, rank_size, -1),
        own_up.reshape(per_shard, rank_size, -1),
    )


def solution(mesh):
    placed = (
        P(("group", "shard", "dp"), None),
        P(("group", "shard", "dp")),
        P(("group", "shard", "dp")),
        P(("group", "shard", "dp")),
        P("group", None, None),
        P("group", None, None),
        P("shard", None),
        P("group"),
        P(("group", "shard", "dp"), None),
    )
    return jax.shard_map(
        body,
        mesh=mesh,
        in_specs=placed,
        out_specs=(
            P(("group", "shard", "dp"), None),
            P(("group", "shard", "dp"), None),
            P(("group", "shard"), None, "dp"),
            P(("group", "shard"), None, "dp"),
        ),
        check_vma=False,
    )
```

profile of v0, /device:TPU:0, one launch (start us, length us, event | category | flops | bytes accessed | tf_op | source)
XLA Modules:
  0.0 346.6 jit_solution(5675665066893408685)
XLA Ops:
  10.0 3.7 %all_to_all.37 = s32[2,1,3]{2,1,0:T(1,128)S(1)} all-to-all(s32[2,1,3]{2,1,0:T(1,128)S(1)} %bitcast.99), channel_id=1, replica_groups=mesh['group'=2,'shard'=8,'dp'=2] {'dp'}, dimensions={0} | all-to-all | bytes 48 | tf_op jit(solution)/shard_map/all_to_all | solution.py:51
  18.0 11.0 %fusion.51 = (bf16[6,128,4096]{2,1,0:T(8,128)(2,1)}, bf16[6,128,4096]{2,1,0:T(8,128)(2,1)}) fusion(bf16[6,128,8192]{2,1,0:T(8,128)(2,1)} %bitcast.94), kind=kLoop, calls=%fused_computation.111 | loop fusion | bytes 25165824 | tf_op jit(solution)/shard_map/jit(_take)/gather | solution.py:43
  29.0 5.3 %gather_fusion.3 = bf16[3,128,4096]{2,1,0:T(8,128)(2,1)} fusion(bf16[6,128,4096]{2,1,0:T(8,128)(2,1)} %get-tuple-element.21, s32[1024]{0:T(1024)S(1)} %pad_clamp_fusion.3), kind=kCustom, calls=%fused_computation.clone | custom fusion | bytes 6291468 | tf_op jit(solution)/shard_map/jit(_take)/gather | solution.py:43
  34.3 5.4 %gather_fusion.5 = bf16[3,128,4096]{2,1,0:T(8,128)(2,1)} fusion(bf16[6,128,4096]{2,1,0:T(8,128)(2,1)} %get-tuple-element.21, s32[1024]{0:T(1024)S(1)} %pad_clamp_fusion.2), kind=kCustom, calls=%fused_computation.3.clone | custom fusion | bytes 6291468 | tf_op jit(solution)/shard_map/jit(_take)/gather | solution.py:43
  39.7 5.3 %gather_fusion.4 = bf16[3,128,4096]{2,1,0:T(8,128)(2,1)} fusion(bf16[6,128,4096]{2,1,0:T(8,128)(2,1)} %get-tuple-element.22, s32[1024]{0:T(1024)S(1)} %pad_clamp_fusion.3), kind=kCustom, calls=%fused_computation.1.clone | custom fusion | bytes 6291468 | tf_op jit(solution)/shard_map/jit(_take)/gather | solution.py:43
  45.0 5.3 %gather_fusion.6 = bf16[3,128,4096]{2,1,0:T(8,128)(2,1)} fusion(bf16[6,128,4096]{2,1,0:T(8,128)(2,1)} %get-tuple-element.22, s32[1024]{0:T(1024)S(1)} %pad_clamp_fusion.2), kind=kCustom, calls=%fused_computation.4.clone | custom fusion | bytes 6291468 | tf_op jit(solution)/shard_map/jit(_take)/gather | solution.py:43
  50.4 5.1 %fusion.1 = bf16[1,3,128,8192]{3,2,1,0:T(8,128)(2,1)S(1)} fusion(bf16[3,128,4096]{2,1,0:T(8,128)(2,1)} %gather_fusion.4, bf16[3,128,4096]{2,1,0:T(8,128)(2,1)} %gather_fusion.3, pred[3]{0:T(512)(128)(4,1)S(1)} %get-tuple-element.30), kind=kLoop, calls=%fused_computation.19 | loop fusion | flops 15728640 | bytes 12582915 | tf_op jit(solution)/shard_map/stack | solution.py:48
  57.0 5.2 %pad_maximum_fusion = bf16[2,3,128,8192]{3,2,1,0:T(8,128)(2,1)} fusion(bf16[1,3,128,8192]{3,2,1,0:T(8,128)(2,1)S(1)} %fusion.2, bf16[1,3,128,8192]{3,2,1,0:T(8,128)(2,1)S(1)} %fusion.1), kind=kLoop, calls=%fused_computation.15 | loop fusion | flops 6291456 | bytes 25165824 | tf_op jit(solution)/shard_map/stack | solution.py:48
  62.2 8.6 %all-to-all-start = ((bf16[2,3,128,8192]{3,2,1,0:T(8,128)(2,1)}), bf16[2,3,128,8192]{3,2,1,0:T(8,128)(2,1)}, u32[]{:S(2)}, u32[]{:S(2)}) async-start(bf16[2,3,128,8192]{3,2,1,0:T(8,128)(2,1)} %pad_maximum_fusion), calls=%async_computation | async-start | bytes 25165824 | tf_op jit(solution)/shard_map/all_to_all | solution.py:48
  72.7 8.6 %all-to-all-done = bf16[2,3,128,8192]{3,2,1,0:T(8,128)(2,1)} async-done(((bf16[2,3,128,8192]{3,2,1,0:T(8,128)(2,1)}), bf16[2,3,128,8192]{3,2,1,0:T(8,128)(2,1)}, u32[]{:S(2)}, u32[]{:S(2)}) %all-to-all-start) | async-done | bytes 12582944 | tf_op jit(solution)/shard_map/all_to_all | solution.py:48
  81.3 3.2 all-to-all-start.3
  84.5 10.5 %fusion.50 = (bf16[6,128,4096]{2,1,0:T(8,128)(2,1)}, bf16[6,128,4096]{2,1,0:T(8,128)(2,1)}) fusion(bf16[6,128,8192]{2,1,0:T(8,128)(2,1)} %bitcast.12), kind=kLoop, calls=%fused_computation.110 | loop fusion | bytes 25165824 | tf_op jit(solution)/shard_map/jit(_take)/gather | solution.py:54
  95.0 5.3 %gather_fusion.7 = bf16[3,128,4096]{2,1,0:T(8,128)(2,1)} fusion(bf16[6,128,4096]{2,1,0:T(8,128)(2,1)} %get-tuple-element.19, s32[1024]{0:T(1024)S(1)} %pad_clamp_fusion.1), kind=kCustom, calls=%fused_computation.5.clone | custom fusion | bytes 6291468 | tf_op jit(solution)/shard_map/jit(_take)/gather | solution.py:54
  100.3 6.6 %gather_fusion.8 = bf16[3,128,4096]{2,1,0:T(8,128)(2,1)} fusion(bf16[6,128,4096]{2,1,0:T(8,128)(2,1)} %get-tuple-element.20, s32[1024]{0:T(1024)S(1)} %pad_clamp_fusion.1), kind=kCustom, calls=%fused_computation.6.clone | custom fusion | bytes 6291468 | tf_op jit(solution)/shard_map/jit(_take)/gather | solution.py:54
  107.4 3.2 all-to-all-start.2
  115.0 4.1 %maximum_select_fusion.2 = bf16[3,128,8192]{2,1,0:T(8,128)(2,1)S(1)} fusion(bf16[3,128,4096]{2,1,0:T(8,128)(2,1)} %gather_fusion.8, bf16[3,128,4096]{2,1,0:T(8,128)(2,1)} %gather_fusion.7, pred[3]{0:T(512)(128)(4,1)S(1)} %get-tuple-element.12), kind=kLoop, calls=%fused_computation.22 | loop fusion | flops 15728640 | bytes 12582915 | tf_op jit(solution)/shard_map/jit(_take)/select_n | solution.py:54
  119.1 2.6 copy-done.4
  126.9 11.2 %reshape_reshape.4 = bf16[384,2,4096]{2,1,0:T(2,128)(2,1)} reshape(bf16[3,128,8192]{2,1,0:T(8,128)(2,1)} %copy-done.4) | data formatting | bytes 12582912 | tf_op jit(solution)/shard_map/reshape;reshape | solution.py:115
  138.1 7.0 %fusion.5 = f32[8,2,1,16,4096]{4,3,0,1,2:T(8,128)S(1)} fusion(bf16[384,2,4096,1]{2,1,0,3:T(2,128)(2,1)} %bitcast.95, bf16[384,8]{0,1:T(8,128)(2,1)S(1)} %broadcast_bitcast_fusion, bf16[384,16]{0,1:T(8,128)(2,1)S(1)} %copy_bitcast_fusion.1), kind=kOutput, calls=%fused_computation.25 | convolution fusion | flops 805502976 | bytes 10504192 | tf_op jit(solution)/shard_map/tsar,tch->scarh/dot_general | solution.py:112
  148.9 6.4 %fusion.22 = f32[3,128,8192]{2,1,0:T(8,128)} fusion(bf16[3,128,16]{1,2,0:T(8,128)(2,1)S(1)} %fusion.10, bf16[3,16,8192]{2,1,0:T(8,128)(2,1)S(1)} %gather_fusion, pred[3]{0:T(512)(128)(4,1)S(1)} %get-tuple-element.17), kind=kOutput, calls=%fused_computation.46 | convolution fusion | flops 101056512 | bytes 13381635 | tf_op jit(solution)/shard_map/btr,brd->btd/dot_general | solution.py:93
  155.3 86.5 %all-gather.2.cloned.1.call-done = bf16[8192,1024]{1,0:T(8,128)(2,1)} async-done(((bf16[1024,1024]{1,0:T(8,128)(2,1)}), bf16[8192,1024]{1,0:T(8,128)(2,1)}) %all-gather.2.cloned.1.call-update) | async-done | bytes 16777232 | tf_op jit(solution)/shard_map/all_gather | solution.py:59
  241.8 14.6 %fusion = bf16[384,8192]{1,0:T(8,128)(2,1)} fusion(f32[3,128,8192]{2,1,0:T(8,128)} %fusion.22, bf16[8192,1024]{1,0:T(8,128)(2,1)} %all-gather.2.cloned.1.call-done, bf16[384,1024]{1,0:T(8,128)(2,1)S(1)} %copy-done.7, pred[384]{0:T(512)(128)(4,1)S(1)} %get-tuple-element.23), kind=kOutput, calls=%fused_computation.17 | convolution fusion | flops 6449135616 | bytes 36438400 | tf_op jit(solution)/shard_map/dot_general | solution.py:87
  256.3 15.0 %fusion.8 = bf16[384,1024]{1,0:T(8,128)(2,1)} fusion(f32[3,128,1024]{2,1,0:T(8,128)} %convolution_multiply_fusion, bf16[384,8192]{1,0:T(8,128)(2,1)} %bitcast.92, bf16[8192,1024]{1,0:T(8,128)(2,1)} %all-gather.2.cloned.1.call-done), kind=kOutput, calls=%fused_computation.27 | convolution fusion | flops 6443237376 | bytes 25427968 | tf_op jit(solution)/shard_map/dot_general | solution.py:69
  271.3 67.9 %reduce-scatter.3.cloned.1.call-done = f32[1,1,16,4096]{3,2,0,1:T(8,128)} async-done(((f32[16,1,16,4096]{3,2,0,1:T(8,128)}), f32[1,1,16,4096]{3,2,0,1:T(8,128)}) %reduce-scatter.3.cloned.1.call-update) | async-done | bytes 262160 | tf_op jit(solution)/shard_map/reduce_scatter | solution.py:125
  (77 shorter events, 23.6 us)
Async XLA Ops:
  8.0 106.1 %copy-start = (bf16[8,16,8192]{2,1,0:T(8,128)(2,1)S(1)}, bf16[8,16,8192]{2,1,0:T(8,128)(2,1)}, u32[]{:S(2)}) copy-start(bf16[8,16,8192]{2,1,0:T(8,128)(2,1)} %param.17) | copy-start | bytes 6291460
  8.0 233.8 %all-gather.2.cloned.1.call-start = ((), (), s32[]{:S(2)}) async-start(), calls=%async_computation.6 | async-start | bytes 18874368 | tf_op jit(solution)/shard_map/all_gather | solution.py:59
  50.4 5.2 %copy-start.5 = (bf16[3,128,4096]{2,1,0:T(8,128)(2,1)S(1)}, bf16[3,128,4096]{2,1,0:T(8,128)(2,1)}, u32[]{:S(2)}) copy-start(bf16[3,128,4096]{2,1,0:T(8,128)(2,1)} %gather_fusion.5) | copy-start | bytes 9437188
  50.4 5.2 %copy-start.6 = (bf16[3,128,4096]{2,1,0:T(8,128)(2,1)S(1)}, bf16[3,128,4096]{2,1,0:T(8,128)(2,1)}, u32[]{:S(2)}) copy-start(bf16[3,128,4096]{2,1,0:T(8,128)(2,1)} %gather_fusion.6) | copy-start | bytes 9437188
  62.2 8.6 %copy-start.2 = (s32[6]{0:T(128)S(1)}, s32[6]{0:T(128)}, u32[]{:S(2)}) copy-start(s32[6]{0:T(128)} %param.16) | copy-start | bytes 76
  62.2 19.0 %all-to-all-start = ((bf16[2,3,128,8192]{3,2,1,0:T(8,128)(2,1)}), bf16[2,3,128,8192]{3,2,1,0:T(8,128)(2,1)}, u32[]{:S(2)}, u32[]{:S(2)}) async-start(bf16[2,3,128,8192]{3,2,1,0:T(8,128)(2,1)} %pad_maximum_fusion), calls=%async_computation | async-start | bytes 25165824 | tf_op jit(solution)/shard_map/all_to_all | solution.py:48
  81.3 26.1 %all-to-all-start.3 = ((s32[2,1,3]{2,1,0:T(1,128)}), s32[2,1,3]{2,1,0:T(1,128)S(1)}, u32[]{:S(2)}, u32[]{:S(2)}) async-start(s32[2,1,3]{2,1,0:T(1,128)} %bitcast.22), calls=%async_computation.3 | async-start | bytes 2048 | tf_op jit(solution)/shard_map/all_to_all | solution.py:49
  95.0 18.5 %copy-start.3 = (s32[8]{0:T(128)S(1)}, s32[8]{0:T(128)}, u32[]{:S(2)}) copy-start(s32[8]{0:T(128)} %param.20) | copy-start | bytes 100
  107.4 4.6 %all-to-all-start.2 = ((s32[2,1,3]{2,1,0:T(1,128)}), s32[2,1,3]{2,1,0:T(1,128)S(1)}, u32[]{:S(2)}, u32[]{:S(2)}) async-start(s32[2,1,3]{2,1,0:T(1,128)} %bitcast.17), calls=%async_computation.2 | async-start | bytes 2048 | tf_op jit(solution)/shard_map/all_to_all | solution.py:50
  110.6 160.7 %reduce-scatter.5.cloned.1.call-start = ((), (), s32[]{:S(2)}) async-start(), calls=%async_computation.8 | async-start | bytes 557056 | tf_op jit(solution)/shard_map/reduce_scatter | solution.py:131
  119.1 2.6 copy-start.4
  119.1 4.4 %copy-start.7 = (bf16[384,1024]{1,0:T(8,128)(2,1)S(1)}, bf16[384,1024]{1,0:T(8,128)(2,1)}, u32[]{:S(2)}) copy-start(bf16[384,1024]{1,0:T(8,128)(2,1)} %param.21) | copy-start | bytes 2359300
  124.8 214.4 %reduce-scatter.3.cloned.1.call-start = ((), (), s32[]{:S(2)}) async-start(), calls=%async_computation.7 | async-start | bytes 4456448 | tf_op jit(solution)/shard_map/reduce_scatter | solution.py:125
  256.3 82.9 %copy-start.1 = (bf16[8,16,8192]{2,1,0:T(8,128)(2,1)S(1)}, bf16[8,16,8192]{2,1,0:T(8,128)(2,1)}, u32[]{:S(2)}) copy-start(bf16[8,16,8192]{2,1,0:T(8,128)(2,1)} %param.17) | copy-start | bytes 6291460
Sparse Core Ops, SparseCore 0:
  11.0 230.7 all-gather.1
Sparse Core Ops, SparseCore 1:
  124.9 137.9 reduce-scatter.4
  267.6 71.5 reduce-scatter.2
where the time goes:
time: 348 us; the launch traced here: 347 us
  waiting for transfers between devices  164 us (47%)
  local copies, waits for them, and re-layouts  80.4 us (23%)
  matrix products  47 us (14%)
  other arithmetic  20.9 us (6%)
  between operations  15.7 us (5%)
  starting transfers between devices  15.3 us (4%)
  blocking collectives  3.66 us (1%)
    all_gather x1, waiting for transfers between devices, body(): full_weight = lax.all_gather(value_weight, 'shard', axis=0, tiled=True)  86.5 us
    reduce_scatter x1, waiting for transfers between devices, body(): lax.psum_scatter(grad_down.reshape(shards * core_count, per_shard, rank_s...  67.9 us
    gather x5, local copies, waits for them, and re-layouts, body(): outgoing_rows.append(jnp.take(held_blocks, slot_index, axis=0))  32.3 us
    gather x3, local copies, waits for them, and re-layouts, body(): jnp.take(got_rows.reshape(2 * per_core, block_tokens, model_width), work_...  22.3 us
    dot_general x1, matrix products, body(): jnp.dot(flat_rows, full_weight, preferred_element_type=jnp.float32)  15 us
    dot_general x1, matrix products, body(): lax.dot_general(flattened_gradient, full_weight, (((1,), (1,)), ((), ()))...  14.6 us
    another operation x3, other arithmetic, body(): jnp.stack(outgoing_rows)  11.8 us
    another operation x1, local copies, waits for them, and re-layouts, body(): flat_rows.reshape(-1, core_count, model_width // core_count)  11.2 us
  transfers between devices with their start and end apart: 6, of which 3 were waited for; matrix products, arithmetic and copies ran while one was open for 42% of the time, Pallas kernels for 0%

commit v1 on v0

v1 whole, which is shorter than its diff:
```python
import functools

import jax
import jax.numpy as jnp
import numpy as np
from jax import lax
from jax.experimental import pallas as pl
from jax.experimental.pallas import tpu as pltpu
from jax.sharding import PartitionSpec as P

adapter_scale = 2.0
ALL = ("group", "shard", "dp")
NT = (((1,), (1,)), ((), ()))
VMEM_LIMIT = 44 << 20
ANY = pl.BlockSpec(memory_space=pl.ANY)
SMEM = pl.BlockSpec(memory_space=pltpu.SMEM)


def ring_of(shards):
    if shards == 8:
        return [0, 2, 4, 6, 7, 5, 3, 1]
    return list(range(shards))


def dot(x, y):
    return jnp.dot(x, y, preferred_element_type=jnp.float32)


def dot_nt(x, y):
    return lax.dot_general(x, y, NT, preferred_element_type=jnp.float32)


def groups_of(shape, axis, rank):
    return lax.div(lax.broadcasted_iota(jnp.int32, shape, axis), jnp.int32(rank))


def ranks(home, wanted, slots):
    count = jnp.int32(0)
    places = []
    for i in range(slots):
        hit = home(i) == wanted
        places.append(jnp.where(hit, count, -1))
        count = count + hit.astype(jnp.int32)
    return places, count


def slot_at(places, place):
    found = jnp.int32(0)
    for i, here in enumerate(places):
        found = jnp.where(here == place, jnp.int32(i), found)
    return found


def head_kernel(
    dims, info, home, length, adapter, owner, held, grad, grad_sib, down, up,
    keep, send, packed,
    rows_v, grad_v, down_v, up_v, mask_v, low_v, sums_v, up_sums_v,
    row_sem, in_sem, down_sem, sum_sem, pack_sem, up_sem,
):
    slots, tokens, blk, shards, cols, rank, adapters, width = dims
    core = info[0]
    half_chunks = shards // 2
    half = half_chunks * cols
    live_rows = slots * tokens

    def row_copy(j):
        at = pl.ds(pl.multiple_of(j * cols, cols), cols)
        return pltpu.make_async_copy(held.at[:, at], rows_v.at[j], row_sem.at[j])

    def down_copy(j):
        at = pl.ds(pl.multiple_of(j * cols, cols), cols)
        return pltpu.make_async_copy(down.at[:, at], down_v.at[j], down_sem.at[j])

    inputs = [
        pltpu.make_async_copy(grad, grad_v.at[0], in_sem.at[0]),
        pltpu.make_async_copy(grad_sib, grad_v.at[1], in_sem.at[1]),
        pltpu.make_async_copy(up, up_v, in_sem.at[2]),
    ]
    for copy in inputs:
        copy.start()
    for j in range(shards):
        row_copy(j).start()
        down_copy(j).start()

    mine, mine_count = ranks(lambda i: home[i], core, slots)
    other, other_count = ranks(lambda i: home[i], 1 - core, slots)
    packs = [slot_at(other, k) for k in range(blk)]
    for copy in inputs:
        copy.wait()
    token = lax.broadcasted_iota(jnp.int32, (tokens, width), 0)
    for i in range(slots):
        is_mine = home[i] == core
        place = jnp.where(is_mine, mine[i], other[i])
        count = jnp.where(is_mine, mine_count, other_count)
        work = jnp.where(core == 0, place, blk - count + place)
        work = jnp.clip(work, 0, blk - 1)
        source = jnp.where(is_mine, 0, 1)
        live = jnp.where(home[i] >= 0, length[i], 0)
        at = pl.ds(pl.multiple_of(work * tokens, tokens), tokens)
        mask_v[pl.ds(i * tokens, tokens), :] = jnp.where(
            token < live, grad_v[source, at, :], jnp.zeros((), jnp.bfloat16)
        )

    flat = adapters * rank
    column_adapter = groups_of((tokens, flat), 1, rank)

    def own_columns(full):
        parts = []
        for i in range(slots):
            kept = column_adapter == adapter[i]
            parts.append(jnp.where(kept, full[i * tokens:(i + 1) * tokens, :], 0.0))
        return jnp.concatenate(parts, axis=0).astype(jnp.bfloat16)

    row_group = groups_of((flat, flat), 0, rank)
    column_group = groups_of((flat, flat), 1, rank)
    row_rank = lax.broadcasted_iota(jnp.int32, (flat, flat), 0) - row_group * rank
    column_rank = lax.broadcasted_iota(jnp.int32, (flat, flat), 1) - column_group * rank
    target = jnp.full((flat, flat), -1, jnp.int32)
    for a in range(adapters):
        target = jnp.where(column_group == a, owner[a], target)
    spread = jnp.where((target == row_group) & (row_rank == column_rank), 1.0, 0.0)
    spread = spread.astype(jnp.bfloat16)

    back = own_columns(adapter_scale * dot_nt(mask_v[...], up_v[...]))
    back_t = dot_nt(spread, back).astype(jnp.bfloat16)
    low_v[...] = jnp.zeros_like(low_v)

    def sum_copy(j, target_ref):
        at = pl.ds(pl.multiple_of(lax.rem(j, half_chunks) * cols, cols), cols)
        return pltpu.make_async_copy(sums_v.at[j], target_ref.at[:, at], sum_sem.at[j])

    def pack_copy(j, k):
        at = pl.ds(pl.multiple_of(j * cols, cols), cols)
        taken = pl.ds(pl.multiple_of(packs[k] * tokens, tokens), tokens)
        return pltpu.make_async_copy(
            rows_v.at[j, taken, :], packed.at[pl.ds(k * tokens, tokens), at], pack_sem.at[j, k]
        )

    def chunk(j, carry):
        row_copy(j).wait()
        down_copy(j).wait()
        sums_v[j] = dot(back_t, rows_v[j])
        here = lax.div(j, half_chunks) == core

        @pl.when(here)
        def _():
            sum_copy(j, keep).start()

        @pl.when(jnp.logical_not(here))
        def _():
            sum_copy(j, send).start()

        for k in range(blk):
            pack_copy(j, k).start()
        low_v[...] += dot_nt(rows_v[j], down_v[j])
        return carry

    lax.fori_loop(0, shards, chunk, 0)
    low = own_columns(low_v[...])
    low_t = dot_nt(spread, low).astype(jnp.bfloat16)
    up_sums_v[...] = adapter_scale * dot(low_t, mask_v[...])
    half_width = width // 2

    def up_copy(part, target_ref):
        return pltpu.make_async_copy(
            up_sums_v.at[:, pl.ds(part * half_width, half_width)],
            target_ref.at[:, pl.ds(half, half_width)],
            up_sem.at[part],
        )

    for part in range(2):

        @pl.when(core == part)
        def _():
            up_copy(part, keep).start()
            up_copy(1 - part, send).start()

    def drain(j, carry):
        sum_copy(j, keep).wait()
        for k in range(blk):
            pack_copy(j, k).wait()
        return carry

    lax.fori_loop(0, shards, drain, 0)
    for part in range(2):
        up_copy(part, keep).wait()


def backward_tiles(mask_v, back_v, weight_v, down_v, out_v):
    tile = min(256, weight_v.shape[0])

    def step(n, carry):
        at = pl.ds(pl.multiple_of(n * tile, tile), tile)
        out_v[:, at] = (
            dot_nt(mask_v[...], weight_v[at, :]) + dot(back_v[...], down_v[:, at])
        ).astype(out_v.dtype)
        return carry

    lax.fori_loop(0, weight_v.shape[0] // tile, step, 0)


def own_kernel(
    dims, info, home, length, adapter, sibling, grad, down, up, weight,
    table, masked, back, input_grad,
    grad_v, mask_v, back_v, up_v, weight_v, down_v, out_v, sem,
):
    slots, tokens, blk, shards, cols, rank, adapters, width = dims
    core = info[0]
    at = pl.ds(pl.multiple_of(info[2] * cols, cols), cols)
    grad_in = pltpu.make_async_copy(grad, grad_v, sem.at[0])
    up_in = pltpu.make_async_copy(up, up_v, sem.at[1])
    weight_in = pltpu.make_async_copy(weight, weight_v, sem.at[2])
    down_in = pltpu.make_async_copy(down.at[:, at], down_v, sem.at[3])
    for copy in (grad_in, up_in, weight_in, down_in):
        copy.start()
    mine, mine_count = ranks(lambda i: home[i], core, slots)
    theirs, _ = ranks(lambda i: sibling[0, i], core, slots)
    there_count = blk - mine_count
    chosen = []
    for w in range(blk):
        local = jnp.where(core == 0, w < mine_count, w >= there_count)
        local_place = jnp.where(core == 0, w, w - there_count)
        there_place = jnp.clip(jnp.where(core == 0, w - mine_count, w), 0, blk - 1)
        local_slot = slot_at(mine, local_place)
        there_slot = slot_at(theirs, there_place)
        adapter_w = jnp.where(local, adapter[local_slot], sibling[2, there_slot])
        length_w = jnp.where(local, length[local_slot], sibling[1, there_slot])
        table[0, w] = local.astype(jnp.int32)
        table[1, w] = jnp.where(local, local_slot, there_place)
        table[2, w] = adapter_w
        chosen.append((adapter_w, length_w))
    grad_in.wait()
    token = lax.broadcasted_iota(jnp.int32, (tokens, width), 0)
    for w, (_, length_w) in enumerate(chosen):
        own = pl.ds(w * tokens, tokens)
        mask_v[own, :] = jnp.where(
            token < length_w, grad_v[own, :], jnp.zeros((), jnp.bfloat16)
        )
    mask_out = pltpu.make_async_copy(mask_v, masked, sem.at[4])
    mask_out.start()
    up_in.wait()
    full = adapter_scale * dot_nt(mask_v[...], up_v[...])
    column_adapter = groups_of((tokens, adapters * rank), 1, rank)
    for w, (adapter_w, _) in enumerate(chosen):
        kept = jnp.where(column_adapter == adapter_w, full[w * tokens:(w + 1) * tokens, :], 0.0)
        back_v[pl.ds(w * tokens, tokens), :] = kept.astype(jnp.bfloat16)
    back_out = pltpu.make_async_copy(back_v, back, sem.at[5])
    back_out.start()
    weight_in.wait()
    down_in.wait()
    backward_tiles(mask_v, back_v, weight_v, down_v, out_v)
    out = pltpu.make_async_copy(out_v, input_grad.at[:, at], sem.at[6])
    out.start()
    mask_out.wait()
    back_out.wait()
    out.wait()


def weight_kernel(dims, jobs, first, last, *refs):
    slots, tokens, blk, shards, cols, rank, adapters, width = dims
    refs = list(refs)
    info, table, held, got, masked, back, down = refs[:7]
    del refs[:7]
    up = refs.pop(0) if last else None
    acc_in = None if first else refs.pop(0)
    refs.pop(0)
    n_pieces = sum(len(pieces) for _, pieces, _ in jobs)
    piece_refs = refs[:n_pieces]
    del refs[:n_pieces]
    input_grad, result = refs[:2]
    del refs[:2]
    mask_v, back_v, up_v, acc_v, final_v = refs[:5]
    per_job = refs[5:5 + 4 * len(jobs)]
    sem, row_sem, piece_sem, out_sem = refs[5 + 4 * len(jobs):]

    starts = [
        pltpu.make_async_copy(masked, mask_v, sem.at[0]),
        pltpu.make_async_copy(back, back_v, sem.at[1]),
    ]
    if not first:
        starts.append(pltpu.make_async_copy(acc_in, acc_v, sem.at[2]))
    if last:
        up_in = pltpu.make_async_copy(up, up_v, sem.at[3])
        up_in.start()
    work = []
    taken = 0
    for n, (shard_at, pieces, backward) in enumerate(jobs):
        weight_v, rows_v, down_v, out_v = per_job[4 * n:4 * n + 4]
        at = pl.ds(pl.multiple_of(info[shard_at] * cols, cols), cols)
        loads = []
        for row_at, row_add in pieces:
            piece = piece_refs[taken]
            size = piece.shape[0]
            row = 0 if row_at is None else pl.multiple_of(info[row_at] + info[row_add], 16)
            loads.append(
                pltpu.make_async_copy(piece, weight_v.at[pl.ds(row, size), :], piece_sem.at[taken])
            )
            taken += 1
        down_in = pltpu.make_async_copy(down.at[:, at], down_v, row_sem.at[n, blk])
        loads.append(down_in)
        for copy in loads:
            copy.start()
        for w in range(blk):
            to = rows_v.at[pl.ds(w * tokens, tokens), :]
            limit = jnp.where(table[0, w] == 1, slots - 1, blk - 1)
            row = pl.multiple_of(jnp.clip(table[1, w], 0, limit) * tokens, tokens)

            @pl.when(table[0, w] == 1)
            def _():
                pltpu.make_async_copy(
                    held.at[pl.ds(row, tokens), at], to, row_sem.at[n, w]
                ).start()

            @pl.when(table[0, w] != 1)
            def _():
                row_got = pl.multiple_of(jnp.clip(table[1, w], 0, blk - 1) * tokens, tokens)
                pltpu.make_async_copy(
                    got.at[pl.ds(row_got, tokens), at], to, row_sem.at[n, w]
                ).start()

            loads.append(pltpu.make_async_copy(held.at[pl.ds(0, tokens), at], to, row_sem.at[n, w]))
        work.append((loads, at, weight_v, rows_v, down_v, out_v, backward))
    for copy in starts:
        copy.start()
    for copy in starts:
        copy.wait()
    if first:
        acc_v[...] = jnp.zeros_like(acc_v)
    flat = adapters * rank
    tile = min(256, width)
    outs = []
    for n, (loads, at, weight_v, rows_v, down_v, out_v, backward) in enumerate(work):
        for copy in loads:
            copy.wait()

        def step(i, carry):
            cut = pl.ds(pl.multiple_of(i * tile, tile), tile)
            acc_v[:, cut] += dot(rows_v[...], weight_v[:, cut])
            return carry

        if backward:
            backward_tiles(mask_v, back_v, weight_v, down_v, out_v)
            out = pltpu.make_async_copy(out_v, input_grad.at[:, at], out_sem.at[n])
            out.start()
            outs.append(out)
        lax.fori_loop(0, width // tile, step, 0)
        acc_v[:, pl.ds(width, flat)] += dot_nt(rows_v[...], down_v[...])
    if last:
        up_in.wait()
        column_adapter = groups_of((tokens, flat), 1, rank)
        for w in range(blk):
            own = pl.ds(w * tokens, tokens)
            low = jnp.where(column_adapter == table[2, w], acc_v[own, pl.ds(width, flat)], 0.0)
            raised = dot(low.astype(jnp.bfloat16), up_v[...])
            final_v[own, :] = (acc_v[own, pl.ds(0, width)] + adapter_scale * raised).astype(
                jnp.bfloat16
            )
        finish = pltpu.make_async_copy(final_v, result, sem.at[4])
    else:
        finish = pltpu.make_async_copy(acc_v, result, sem.at[4])
    finish.start()
    for out in outs:
        out.wait()
    finish.wait()


def cost(us):
    return pl.CostEstimate(flops=int(us * 1e6), bytes_accessed=int(us * 1e5), transcendentals=0)


def body(
    held_rows,
    block_home,
    block_len,
    block_adapter,
    adapter_down,
    adapter_up,
    value_weight,
    adapter_owner,
    value_grad,
):
    groups, shards, cores = (lax.axis_size(name) for name in ALL)
    slots = block_home.shape[0]
    blk = slots // 2
    tokens = held_rows.shape[0] // slots
    model = held_rows.shape[1]
    cols, width = value_weight.shape
    adapters, rank = adapter_down.shape[:2]
    flat = adapters * rank
    work_rows = blk * tokens
    dims = (slots, tokens, blk, shards, cols, rank, adapters, width)
    f32, bf16 = jnp.float32, jnp.bfloat16
    sds = jax.ShapeDtypeStruct
    dma = pltpu.SemaphoreType.DMA
    params = pltpu.CompilerParams(vmem_limit_bytes=VMEM_LIMIT)

    pairs = groups > 1
    edge = (cols * 11 // 32 + 16) // 32 * 32 if pairs else 0
    middle = cols - 2 * edge
    steps = shards // 2
    ring = ring_of(shards)
    place = {shard: i for i, shard in enumerate(ring)}
    rows = []
    for parity in range(2):
        for core in range(2):
            for shard in range(shards):
                way = -1 if core == 0 else 1
                mine = [ring[(place[shard] + way * k) % shards] for k in range(1, steps + 1)]
                theirs = [ring[(place[shard] - way * k) % shards] for k in range(1, steps + 1)]
                rows.append(
                    [core, parity, shard, 0, parity * (cols - edge), edge, (1 - parity) * (cols - edge)]
                    + [core * edge // 2, (1 - core) * edge // 2]
                    + [core * middle // 2, (1 - core) * middle // 2]
                    + mine
                    + theirs
                )
    SHARD, ZERO, EDGE, MIDDLE, OTHER = 2, 3, 4, 5, 6
    EDGE_MINE, EDGE_SIB, MIDDLE_MINE, MIDDLE_SIB, MINE = 7, 8, 9, 10, 11
    group_at, shard_at, core_at = (lax.axis_index(name) for name in ALL)
    parity_at = lax.rem(group_at, 2)
    plan = jnp.asarray(np.array(rows, np.int32))
    info = lax.dynamic_slice(
        plan, ((parity_at * 2 + core_at) * shards + shard_at, 0), (1, plan.shape[1])
    ).reshape(-1)

    def index(g, s, c):
        return (g * shards + s) * cores + c

    ring_pairs = []
    for g in range(groups):
        for i in range(shards):
            ring_pairs.append((index(g, ring[i], 0), index(g, ring[(i + 1) % shards], 0)))
            ring_pairs.append((index(g, ring[i], 1), index(g, ring[(i - 1) % shards], 1)))

    def around(value):
        return lax.ppermute(value, ALL, ring_pairs)

    def partner(value):
        return lax.ppermute(value, "group", [(g, g ^ 1) for g in range(groups)])

    def swap(value):
        return lax.ppermute(value, "dp", [(0, 1), (1, 0)])

    def flip(value, bit):
        return lax.ppermute(value, "shard", [(s, s ^ bit) for s in range(shards)])

    down = adapter_down.reshape(flat, model)
    up = adapter_up.reshape(flat, width)
    grad_sib = swap(value_grad)
    sibling = swap(jnp.stack([block_home, block_len, block_adapter]))

    half = model // 2 + width // 2
    keep, send, packed = pl.pallas_call(
        functools.partial(head_kernel, dims),
        out_shape=(
            sds((flat, half), f32),
            sds((flat, half), f32),
            sds((work_rows, model), bf16),
        ),
        in_specs=[SMEM] * 5 + [ANY] * 5,
        out_specs=(ANY,) * 3,
        scratch_shapes=[
            pltpu.VMEM((shards, slots * tokens, cols), bf16),
            pltpu.VMEM((2, work_rows, width), bf16),
            pltpu.VMEM((shards, flat, cols), bf16),
            pltpu.VMEM((flat, width), bf16),
            pltpu.VMEM((slots * tokens, width), bf16),
            pltpu.VMEM((slots * tokens, flat), f32),
            pltpu.VMEM((shards, flat, cols), f32),
            pltpu.VMEM((flat, width), f32),
            dma((shards,)),
            dma((3,)),
            dma((shards,)),
            dma((shards,)),
            dma((shards, blk)),
            dma((2,)),
        ],
        compiler_params=params,
        cost_estimate=cost(7),
        name="head",
    )(info, block_home, block_len, block_adapter, adapter_owner, held_rows, value_grad, grad_sib, down, up)
    sent = swap(send)
    got = swap(packed)

    table, masked, back, input_grad = pl.pallas_call(
        functools.partial(own_kernel, dims),
        out_shape=(
            sds((3, blk), jnp.int32),
            sds((work_rows, width), bf16),
            sds((work_rows, flat), bf16),
            sds((work_rows, model), bf16),
        ),
        in_specs=[SMEM] * 5 + [ANY] * 4,
        out_specs=(SMEM, ANY, ANY, ANY),
        scratch_shapes=[
            pltpu.VMEM((work_rows, width), bf16),
            pltpu.VMEM((work_rows, width), bf16),
            pltpu.VMEM((work_rows, flat), bf16),
            pltpu.VMEM((flat, width), bf16),
            pltpu.VMEM((cols, width), bf16),
            pltpu.VMEM((flat, cols), bf16),
            pltpu.VMEM((work_rows, cols), bf16),
            dma((7,)),
        ],
        compiler_params=params,
        cost_estimate=cost(2),
        name="own_shard",
    )(info, block_home, block_len, block_adapter, sibling, value_grad, down, up, value_weight)

    def split(value, count, bit_value):
        parts = value.reshape(count // 2, 2, -1, half)
        return lax.dynamic_index_in_dim(parts, bit_value, 1, keepdims=False)

    bit, count, arrived = 1, shards, sent
    while count > 1:
        here = lax.rem(lax.div(shard_at, bit), 2)
        away = split(keep, count, 1 - here) + split(arrived, count, 1 - here).astype(f32)
        keep = split(keep, count, here) + split(arrived, count, here).astype(f32)
        arrived = flip(away.astype(bf16), bit)
        bit, count = bit * 2, count // 2
    total = keep.reshape(-1, half) + arrived.astype(f32).reshape(-1, half)

    def multiply(state, jobs, pieces, first=False, last=False):
        input_grad, acc = state
        operands = [info, table, held_rows, got, masked, back, down]
        if last:
            operands.append(up)
        if not first:
            operands.append(acc)
        aliases = {len(operands): 0}
        operands.append(input_grad)
        operands += pieces
        result = sds((work_rows, width), bf16) if last else sds((work_rows, width + flat), f32)
        return pl.pallas_call(
            functools.partial(weight_kernel, dims, jobs, first, last),
            out_shape=(sds(input_grad.shape, bf16), result),
            in_specs=[SMEM] * 2 + [ANY] * (len(operands) - 2),
            out_specs=(ANY, ANY),
            scratch_shapes=[
                pltpu.VMEM((work_rows, width), bf16),
                pltpu.VMEM((work_rows, flat), bf16),
                pltpu.VMEM((flat, width), bf16),
                pltpu.VMEM((work_rows, width + flat), f32),
                pltpu.VMEM((work_rows, width), bf16),
            ]
            + [
                pltpu.VMEM((cols, width), bf16),
                pltpu.VMEM((work_rows, cols), bf16),
                pltpu.VMEM((flat, cols), bf16),
                pltpu.VMEM((work_rows, cols), bf16),
            ] * len(jobs)
            + [dma((5,)), dma((len(jobs), blk + 1)), dma((len(pieces),)), dma((len(jobs),))],
            input_output_aliases=aliases,
            compiler_params=params,
            cost_estimate=cost(3),
            name="weights",
        )(*operands)

    edge_rows = lax.dynamic_slice(value_weight, (parity_at * (cols - edge), 0), (edge, width))
    middle_rows = value_weight[edge:edge + middle]
    state = (input_grad, None)
    for k in range(1, steps + 1):
        final = k == steps
        if final:
            edge_rows = lax.dynamic_slice(edge_rows, (core_at * (edge // 2), 0), (edge // 2, width))
            middle_rows = lax.dynamic_slice(
                middle_rows, (core_at * (middle // 2), 0), (middle // 2, width)
            )
        edge_rows = around(edge_rows)
        middle_rows = around(middle_rows)
        parts = [edge_rows, middle_rows, partner(edge_rows)]
        theirs = [swap(part) for part in parts]
        if final:
            jobs = [(
                MINE + k - 1,
                [(EDGE, EDGE_MINE), (MIDDLE, MIDDLE_MINE), (OTHER, EDGE_MINE)]
                + [(EDGE, EDGE_SIB), (MIDDLE, MIDDLE_SIB), (OTHER, EDGE_SIB)],
                True,
            )]
        else:
            whole = [(EDGE, ZERO), (MIDDLE, ZERO), (OTHER, ZERO)]
            jobs = [(MINE + k - 1, whole, True), (MINE + steps + k - 1, whole, True)]
        pieces = parts + theirs
        if k == 1:
            jobs = [(SHARD, [(None, None)], False)] + jobs
            pieces = [value_weight] + pieces
        state = multiply(state, jobs, pieces, first=k == 1, last=final)
    input_grad, value_projection_output = state
    per_shard = adapters // shards
    return (
        value_projection_output,
        input_grad,
        total[:, :model // 2].reshape(per_shard, rank, -1),
        total[:, model // 2:].reshape(per_shard, rank, -1),
    )


def solution(mesh):
    placed = (
        P(ALL, None),
        P(ALL),
        P(ALL),
        P(ALL),
        P("group", None, None),
        P("group", None, None),
        P("shard", None),
        P("group"),
        P(ALL, None),
    )
    return jax.shard_map(
        body,
        mesh=mesh,
        in_specs=placed,
        out_specs=(
            P(ALL, None),
            P(ALL, None),
            P(("group", "shard"), None, "dp"),
            P(("group", "shard"), None, "dp"),
        ),
        check_vma=False,
    )
```

time: 348 us -> 174 us (0.50)
  waiting for transfers between devices: 164 us -> 61.8 us
  local copies, waits for them, and re-layouts: 80.4 us -> 18.3 us
  Pallas kernels: 0 us -> 57.1 us
  matrix products: 47 us -> 0 us
  between operations: 15.7 us -> 1.07 us
  other arithmetic: 20.9 us -> 8.82 us
  starting transfers between devices: 15.3 us -> 25 us
  blocking collectives: 3.66 us -> 0 us
    all_gather x1 -> x0, waiting for transfers between devices: 86.5 us -> none  [body(): full_weight = lax.all_gather(value_weight, 'shard', axis=0, tiled=True)]
    reduce_scatter x2 -> x0, waiting for transfers between devices: 67.9 us -> none  [the longest x1 67.9 us: body(): lax.psum_scatter(grad_down.reshape(shards * core_count, per_shard, rank_s...]
    gather x17 -> x0, local copies, waits for them, and re-layouts: 62.6 us -> none  [the longest x5 32.3 us: body(): outgoing_rows.append(jnp.take(held_blocks, slot_index, axis=0))]
    ppermute x0 -> x31, waiting for transfers between devices: none -> 61.8 us  [the longest x4 34.5 us: partner(): return lax.ppermute(value, 'group', [(g, g ^ 1) for g in range(groups)])]
    pallas_call x0 -> x6, Pallas kernels: none -> 57.1 us  [the longest x4 40.6 us: multiply(): pl.pallas_call(functools.partial(weight_kernel, dims, jobs, first, last),...]
    dot_general x8 -> x0, matrix products: 47 us -> none  [the longest x1 15 us: body(): jnp.dot(flat_rows, full_weight, preferred_element_type=jnp.float32)]
    ppermute x0 -> x31, starting transfers between devices: none -> 25 us  [the longest x8 11.9 us: around(): return lax.ppermute(value, ALL, ring_pairs)]
    all_to_all x3 -> x0, starting transfers between devices: 14.9 us -> none  [the longest x1 8.55 us: body(): lax.all_to_all(jnp.stack(outgoing_rows), 'dp', split_axis=0, concat_axis=...]
  transfers between devices with their start and end apart: 6 -> 31, of which waited for: 3 -> 12; matrix products, arithmetic and copies ran while one was open for 42% -> 9% of each run, Pallas kernels for 0% -> 22%
where the time goes in v1:
time: 174 us; the launch traced here: 172 us
  waiting for transfers between devices  61.8 us (36%)
  Pallas kernels  57.1 us (33%)
  starting transfers between devices  25 us (14%)
  local copies, waits for them, and re-layouts  18.3 us (11%)
  other arithmetic  8.82 us (5%)
    pallas_call x4, Pallas kernels, multiply(): pl.pallas_call(functools.partial(weight_kernel, dims, jobs, first, last),...  40.6 us
    ppermute x4, waiting for transfers between devices, partner(): return lax.ppermute(value, 'group', [(g, g ^ 1) for g in range(groups)])  34.5 us
    ppermute x8, waiting for transfers between devices, around(): return lax.ppermute(value, ALL, ring_pairs)  17.4 us
    ppermute x8, starting transfers between devices, around(): return lax.ppermute(value, ALL, ring_pairs)  11.9 us
    pallas_call x1, Pallas kernels, body(): pl.pallas_call(functools.partial(head_kernel, dims), out_shape=(sds((flat...  11.7 us
    unnamed x54, local copies, waits for them, and re-layouts  11 us
    convert_element_type x3, other arithmetic, body(): arrived = flip(away.astype(bf16), bit)  7.78 us
    ppermute x4, starting transfers between devices, partner(): return lax.ppermute(value, 'group', [(g, g ^ 1) for g in range(groups)])  7.05 us
  transfers between devices with their start and end apart: 31, of which 12 were waited for; matrix products, arithmetic and copies ran while one was open for 9% of the time, Pallas kernels for 22%

profile of v1, /device:TPU:0, one launch (start us, length us, event | category | flops | bytes accessed | tf_op | source)
XLA Modules:
  0.0 172.0 jit_solution(14879896289396969045)
XLA Ops:
  9.6 11.7 %head.1 = (f32[128,4608]{1,0:T(8,128)S(1)}, f32[128,4608]{1,0:T(8,128)}, bf16[384,8192]{1,0:T(8,128)(2,1)}) custom-call(s32[19]{0:T(128)S(1)} %fusion.6.info.refs_0_, s32[6]{0:T(128)S(1)} %copy-done.18, s32[6]{0:T(128)S(1)} %copy-done.20, s32[6]{0:T(128)S(1)} %copy-done.22, s32[8]{0:T(128)S(1)} %copy-done.24, bf16[768,8192]{1,0:T(8,128)(2,1)} %refs_2_.7, ...), custom_call_target="tpu_custom_call" | custom-call | flops 7000000 | bytes 700000 | tf_op jit(solution)/shard_map/head/pallas_call | solution.py:453
  24.1 3.0 %collective-permute-start.4 = (bf16[320,1024]{1,0:T(8,128)(2,1)}, bf16[320,1024]{1,0:T(8,128)(2,1)S(1)}, u32[]{:S(2)}, u32[]{:S(2)}) collective-permute-start(bf16[320,1024]{1,0:T(8,128)(2,1)} %slice.9), channel_id=1, source_target_pairs={{0,4},{1,3},{4,8},{5,1},{8,12},{9,5},{12,14},{13,9},{14,10},{15,13... | collective-permute-start | bytes 1966088 | tf_op jit(solution)/shard_map/ppermute | solution.py:436
  29.5 6.2 %collective-permute-done.4.refs_10_ = bf16[320,1024]{1,0:T(8,128)(2,1)S(1)} collective-permute-done((bf16[320,1024]{1,0:T(8,128)(2,1)}, bf16[320,1024]{1,0:T(8,128)(2,1)S(1)}, u32[]{:S(2)}, u32[]{:S(2)}) %collective-permute-start.4) | collective-permute-done | bytes 655392 | tf_op jit(solution)/shard_map/ppermute | solution.py:436
  37.8 2.3 %collective-permute-start.10 = (bf16[320,1024]{1,0:T(8,128)(2,1)S(1)}, bf16[320,1024]{1,0:T(8,128)(2,1)}, u32[]{:S(2)}, u32[]{:S(2)}) collective-permute-start(bf16[320,1024]{1,0:T(8,128)(2,1)S(1)} %collective-permute-done.4.refs_10_), channel_id=1, source_target_pairs={{0,4},{1,3},{4,8},{5,1},{8,12},{9,5},{12,14},{13,9},{14,10},{15,13... | collective-permute-start | bytes 1966088 | tf_op jit(solution)/shard_map/ppermute | solution.py:436
  40.1 3.3 %collective-permute-done.3.refs_9_ = bf16[352,1024]{1,0:T(8,128)(2,1)S(1)} collective-permute-done((bf16[352,1024]{1,0:T(8,128)(2,1)}, bf16[352,1024]{1,0:T(8,128)(2,1)S(1)}, u32[]{:S(2)}, u32[]{:S(2)}) %collective-permute-start.3) | collective-permute-done | bytes 720928 | tf_op jit(solution)/shard_map/ppermute | solution.py:436
  43.4 2.0 %collective-permute-start.5 = (bf16[352,1024]{1,0:T(8,128)(2,1)S(1)}, bf16[352,1024]{1,0:T(8,128)(2,1)}, u32[]{:S(2)}, u32[]{:S(2)}) collective-permute-start(bf16[352,1024]{1,0:T(8,128)(2,1)S(1)} %collective-permute-done.3.refs_9_), channel_id=1, source_target_pairs={{0,16},{16,0},{1,17},{17,1},{2,18},{18,2},{3,19},{19,3},{4,20},{20... | collective-permute-start | bytes 2162696 | tf_op jit(solution)/shard_map/ppermute | solution.py:439
  47.1 3.6 %fusion.1 = (bf16[4,16,4608]{2,1,0:T(8,128)(2,1)S(1)}, f32[4,1,16,4608]{3,2,0,1:T(8,128)}) fusion(f32[4,2,16,4608]{3,2,1,0:T(8,128)} %bitcast.7, s32[]{:T(128)S(6)} %select_n.47, f32[4,2,16,4608]{3,2,1,0:T(8,128)} %bitcast.54, s32[]{:T(128)S(6)} %select_n.45), kind=kLoop, calls=%fused_computation.3 | loop fusion | flops 884736 | bytes 6488072 | tf_op jit(solution)/shard_map/convert_element_type | solution.py:519
  50.7 1.9 %collective-permute-start.28 = (bf16[4,16,4608]{2,1,0:T(8,128)(2,1)S(1)}, bf16[4,16,4608]{2,1,0:T(8,128)(2,1)S(1)}, u32[]{:S(2)}, u32[]{:S(2)}) collective-permute-start(bf16[4,16,4608]{2,1,0:T(8,128)(2,1)S(1)} %get-tuple-element.34), channel_id=1, source_target_pairs={{0,2},{2,0},{4,6},{6,4},{8,10},{10,8},{12,14},{14,12},{1,3},{3,1},... | collective-permute-start | bytes 1769480 | tf_op jit(solution)/shard_map/ppermute | solution.py:445
  52.6 8.6 %collective-permute-done.5.refs_11_ = bf16[352,1024]{1,0:T(8,128)(2,1)} collective-permute-done((bf16[352,1024]{1,0:T(8,128)(2,1)S(1)}, bf16[352,1024]{1,0:T(8,128)(2,1)}, u32[]{:S(2)}, u32[]{:S(2)}) %collective-permute-start.5) | collective-permute-done | bytes 720928 | tf_op jit(solution)/shard_map/ppermute | solution.py:439
  62.1 1.7 %collective-permute-start.16 = (bf16[320,1024]{1,0:T(8,128)(2,1)}, bf16[320,1024]{1,0:T(8,128)(2,1)}, u32[]{:S(2)}, u32[]{:S(2)}) collective-permute-start(bf16[320,1024]{1,0:T(8,128)(2,1)} %collective-permute-done.10.refs_10_), channel_id=1, source_target_pairs={{0,4},{1,3},{4,8},{5,1},{8,12},{9,5},{12,14},{13,9},{14,10},{15,13... | collective-permute-start | bytes 1966088 | tf_op jit(solution)/shard_map/ppermute | solution.py:436
  64.0 6.8 %collective-permute-done.28 = bf16[4,16,4608]{2,1,0:T(8,128)(2,1)S(1)} collective-permute-done((bf16[4,16,4608]{2,1,0:T(8,128)(2,1)S(1)}, bf16[4,16,4608]{2,1,0:T(8,128)(2,1)S(1)}, u32[]{:S(2)}, u32[]{:S(2)}) %collective-permute-start.28) | collective-permute-done | bytes 589856 | tf_op jit(solution)/shard_map/ppermute | solution.py:445
  71.6 2.5 %fusion.2 = (bf16[2,16,4608]{2,1,0:T(8,128)(2,1)S(1)}, f32[2,1,16,4608]{3,2,1,0:T(8,128)}) fusion(f32[2,2,16,4608]{3,2,1,0:T(8,128)} %bitcast.58, s32[]{:T(128)S(6)} %select_n.49, bf16[2,2,16,4608]{3,2,1,0:T(8,128)(2,1)} %bitcast.59, s32[]{:T(128)S(6)} %select_n.46), kind=kLoop, calls=%fused_computation.6 | loop fusion | flops 737280 | bytes 2654216 | tf_op jit(solution)/shard_map/convert_element_type | solution.py:519
  74.1 3.8 %collective-permute-done.16.refs_10_ = bf16[320,1024]{1,0:T(8,128)(2,1)} collective-permute-done((bf16[320,1024]{1,0:T(8,128)(2,1)}, bf16[320,1024]{1,0:T(8,128)(2,1)}, u32[]{:S(2)}, u32[]{:S(2)}) %collective-permute-start.16) | collective-permute-done | bytes 655392 | tf_op jit(solution)/shard_map/ppermute | solution.py:436
  77.9 2.0 %collective-permute-start.11 = (bf16[352,1024]{1,0:T(8,128)(2,1)}, bf16[352,1024]{1,0:T(8,128)(2,1)}, u32[]{:S(2)}, u32[]{:S(2)}) collective-permute-start(bf16[352,1024]{1,0:T(8,128)(2,1)} %collective-permute-done.9.refs_9_), channel_id=1, source_target_pairs={{0,16},{16,0},{1,17},{17,1},{2,18},{18,2},{3,19},{19,3},{4,20},{20... | collective-permute-start | bytes 2162696 | tf_op jit(solution)/shard_map/ppermute | solution.py:439
  81.6 4.0 %collective-permute-done.15.refs_9_ = bf16[352,1024]{1,0:T(8,128)(2,1)} collective-permute-done((bf16[352,1024]{1,0:T(8,128)(2,1)}, bf16[352,1024]{1,0:T(8,128)(2,1)}, u32[]{:S(2)}, u32[]{:S(2)}) %collective-permute-start.15) | collective-permute-done | bytes 720928 | tf_op jit(solution)/shard_map/ppermute | solution.py:436
  85.7 1.7 %constant_dynamic-slice_fusion.1 = bf16[176,1024]{1,0:T(8,128)(2,1)} fusion(bf16[352,1024]{1,0:T(8,128)(2,1)} %collective-permute-done.15.refs_9_, s32[]{:T(128)S(6)} %select_n.43), kind=kLoop, calls=%fused_computation.15 | loop fusion | bytes 720900 | tf_op jit(solution)/shard_map/dynamic_slice | solution.py:565
  90.8 4.3 %collective-permute-done.11.refs_11_ = bf16[352,1024]{1,0:T(8,128)(2,1)} collective-permute-done((bf16[352,1024]{1,0:T(8,128)(2,1)}, bf16[352,1024]{1,0:T(8,128)(2,1)}, u32[]{:S(2)}, u32[]{:S(2)}) %collective-permute-start.11) | collective-permute-done | bytes 720928 | tf_op jit(solution)/shard_map/ppermute | solution.py:439
  97.9 4.8 %own_shard.1 = (s32[3,3]{1,0:T(4,128)S(1)}, bf16[384,1024]{1,0:T(8,128)(2,1)S(1)}, bf16[384,128]{1,0:T(8,128)(2,1)S(1)}, bf16[384,8192]{1,0:T(8,128)(2,1)}) custom-call(s32[19]{0:T(128)S(1)} %fusion.6.info.refs_0_, s32[6]{0:T(128)S(1)} %copy-done.19, s32[6]{0:T(128)S(1)} %copy-done.21, s32[6]{0:T(128)S(1)} %copy-done.23, ...), custom_call_target="tpu_custom_call" | custom-call | flops 2000000 | bytes 200000 | tf_op jit(solution)/shard_map/own_shard/pallas_call | solution.py:485
  107.8 14.3 %collective-permute-done.17.refs_11_ = bf16[352,1024]{1,0:T(8,128)(2,1)S(1)} collective-permute-done((bf16[352,1024]{1,0:T(8,128)(2,1)}, bf16[352,1024]{1,0:T(8,128)(2,1)S(1)}, u32[]{:S(2)}, u32[]{:S(2)}) %collective-permute-start.17) | collective-permute-done | bytes 720928 | tf_op jit(solution)/shard_map/ppermute | solution.py:439
  122.0 7.3 %collective-permute-done.23.refs_12_ = bf16[176,1024]{1,0:T(8,128)(2,1)S(1)} collective-permute-done((bf16[176,1024]{1,0:T(8,128)(2,1)S(1)}, bf16[176,1024]{1,0:T(8,128)(2,1)S(1)}, u32[]{:S(2)}, u32[]{:S(2)}) %collective-permute-start.23) | collective-permute-done | bytes 360480 | tf_op jit(solution)/shard_map/ppermute | solution.py:439
  131.2 12.2 %weights.4 = (bf16[384,8192]{1,0:T(8,128)(2,1)}, f32[384,1152]{1,0:T(8,128)S(1)}) custom-call(s32[19]{0:T(128)S(1)} %fusion.6.info.refs_0_, s32[3,3]{1,0:T(4,128)S(1)} %get-tuple-element.19.refs_1_, bf16[768,8192]{1,0:T(8,128)(2,1)} %refs_2_.7, bf16[384,8192]{1,0:T(8,128)(2,1)} %collective-permute-done.2.refs_3_, ...), custom_call_target="tpu_custom_call", output_to_operand_aliasing={{0}: (7, {})} | custom-call | flops 3000000 | bytes 300000 | tf_op jit(solution)/shard_map/weights/pallas_call | solution.py:534
  143.3 10.7 %weights.5 = (bf16[384,8192]{1,0:T(8,128)(2,1)}, f32[384,1152]{1,0:T(8,128)S(1)}) custom-call(s32[19]{0:T(128)S(1)} %fusion.6.info.refs_0_, s32[3,3]{1,0:T(4,128)S(1)} %get-tuple-element.19.refs_1_, bf16[768,8192]{1,0:T(8,128)(2,1)} %refs_2_.7, bf16[384,8192]{1,0:T(8,128)(2,1)} %collective-permute-done.2.refs_3_, ...), custom_call_target="tpu_custom_call", output_to_operand_aliasing={{0}: (8, {})} | custom-call | flops 3000000 | bytes 300000 | tf_op jit(solution)/shard_map/weights/pallas_call | solution.py:534
  154.1 10.3 %weights.6 = (bf16[384,8192]{1,0:T(8,128)(2,1)}, f32[384,1152]{1,0:T(8,128)S(1)}) custom-call(s32[19]{0:T(128)S(1)} %fusion.6.info.refs_0_, s32[3,3]{1,0:T(4,128)S(1)} %get-tuple-element.19.refs_1_, bf16[768,8192]{1,0:T(8,128)(2,1)} %refs_2_.7, bf16[384,8192]{1,0:T(8,128)(2,1)} %collective-permute-done.2.refs_3_, ...), custom_call_target="tpu_custom_call", output_to_operand_aliasing={{0}: (8, {})} | custom-call | flops 3000000 | bytes 300000 | tf_op jit(solution)/shard_map/weights/pallas_call | solution.py:534
  164.4 7.5 %weights.7 = (bf16[384,8192]{1,0:T(8,128)(2,1)}, bf16[384,1024]{1,0:T(8,128)(2,1)}) custom-call(s32[19]{0:T(128)S(1)} %fusion.6.info.refs_0_, s32[3,3]{1,0:T(4,128)S(1)} %get-tuple-element.19.refs_1_, bf16[768,8192]{1,0:T(8,128)(2,1)} %refs_2_.7, bf16[384,8192]{1,0:T(8,128)(2,1)} %collective-permute-done.2.refs_3_, ...), custom_call_target="tpu_custom_call", output_to_operand_aliasing={{0}: (9, {})} | custom-call | flops 3000000 | bytes 300000 | tf_op jit(solution)/shard_map/weights/pallas_call | solution.py:534
  (110 shorter events, 34.5 us)
Async XLA Ops:
  22.7 106.6 %collective-permute-start.2 = (bf16[384,8192]{1,0:T(8,128)(2,1)}, bf16[384,8192]{1,0:T(8,128)(2,1)}, u32[]{:S(2)}, u32[]{:S(2)}) collective-permute-start(bf16[384,8192]{1,0:T(8,128)(2,1)} %get-tuple-element.20), channel_id=1, source_target_pairs={{0,1},{1,0},{2,3},{3,2},{4,5},{5,4},{6,7},{7,6},{8,9},{9,8},{10,11... | collective-permute-start | bytes 18874376 | tf_op jit(solution)/shard_map/ppermute | solution.py:442
  23.0 22.4 %collective-permute-start.27 = (f32[128,4608]{1,0:T(8,128)}, f32[128,4608]{1,0:T(8,128)}, u32[]{:S(2)}, u32[]{:S(2)}) collective-permute-start(f32[128,4608]{1,0:T(8,128)} %get-tuple-element.33), channel_id=1, source_target_pairs={{0,1},{1,0},{2,3},{3,2},{4,5},{5,4},{6,7},{7,6},{8,9},{9,8},{10,11... | collective-permute-start | bytes 7077896 | tf_op jit(solution)/shard_map/ppermute | solution.py:442
  27.9 15.5 %collective-permute-start.3 = (bf16[352,1024]{1,0:T(8,128)(2,1)}, bf16[352,1024]{1,0:T(8,128)(2,1)S(1)}, u32[]{:S(2)}, u32[]{:S(2)}) collective-permute-start(bf16[352,1024]{1,0:T(8,128)(2,1)} %constant_dynamic-slice_fusion.2), channel_id=1, source_target_pairs={{0,4},{1,3},{4,8},{5,1},{8,12},{9,5},{12,14},{13,9},{14,10},{15,13... | collective-permute-start | bytes 2162696 | tf_op jit(solution)/shard_map/ppermute | solution.py:436
  37.8 12.9 %collective-permute-start.10 = (bf16[320,1024]{1,0:T(8,128)(2,1)S(1)}, bf16[320,1024]{1,0:T(8,128)(2,1)}, u32[]{:S(2)}, u32[]{:S(2)}) collective-permute-start(bf16[320,1024]{1,0:T(8,128)(2,1)S(1)} %collective-permute-done.4.refs_10_), channel_id=1, source_target_pairs={{0,4},{1,3},{4,8},{5,1},{8,12},{9,5},{12,14},{13,9},{14,10},{15,13... | collective-permute-start | bytes 1966088 | tf_op jit(solution)/shard_map/ppermute | solution.py:436
  43.4 17.8 %collective-permute-start.5 = (bf16[352,1024]{1,0:T(8,128)(2,1)S(1)}, bf16[352,1024]{1,0:T(8,128)(2,1)}, u32[]{:S(2)}, u32[]{:S(2)}) collective-permute-start(bf16[352,1024]{1,0:T(8,128)(2,1)S(1)} %collective-permute-done.3.refs_9_), channel_id=1, source_target_pairs={{0,16},{16,0},{1,17},{17,1},{2,18},{18,2},{3,19},{19,3},{4,20},{20... | collective-permute-start | bytes 2162696 | tf_op jit(solution)/shard_map/ppermute | solution.py:439
  45.4 15.8 %collective-permute-start.6 = (bf16[352,1024]{1,0:T(8,128)(2,1)S(1)}, bf16[352,1024]{1,0:T(8,128)(2,1)S(1)}, u32[]{:S(2)}, u32[]{:S(2)}) collective-permute-start(bf16[352,1024]{1,0:T(8,128)(2,1)S(1)} %collective-permute-done.3.refs_9_), channel_id=1, source_target_pairs={{0,1},{1,0},{2,3},{3,2},{4,5},{5,4},{6,7},{7,6},{8,9},{9,8},{10,11... | collective-permute-start | bytes 2162696 | tf_op jit(solution)/shard_map/ppermute | solution.py:442
  45.4 18.4 %collective-permute-start.9 = (bf16[352,1024]{1,0:T(8,128)(2,1)S(1)}, bf16[352,1024]{1,0:T(8,128)(2,1)}, u32[]{:S(2)}, u32[]{:S(2)}) collective-permute-start(bf16[352,1024]{1,0:T(8,128)(2,1)S(1)} %collective-permute-done.3.refs_9_), channel_id=1, source_target_pairs={{0,4},{1,3},{4,8},{5,1},{8,12},{9,5},{12,14},{13,9},{14,10},{15,13... | collective-permute-start | bytes 2162696 | tf_op jit(solution)/shard_map/ppermute | solution.py:436
  50.7 20.1 %collective-permute-start.28 = (bf16[4,16,4608]{2,1,0:T(8,128)(2,1)S(1)}, bf16[4,16,4608]{2,1,0:T(8,128)(2,1)S(1)}, u32[]{:S(2)}, u32[]{:S(2)}) collective-permute-start(bf16[4,16,4608]{2,1,0:T(8,128)(2,1)S(1)} %get-tuple-element.34), channel_id=1, source_target_pairs={{0,2},{2,0},{4,6},{6,4},{8,10},{10,8},{12,14},{14,12},{1,3},{3,1},... | collective-permute-start | bytes 1769480 | tf_op jit(solution)/shard_map/ppermute | solution.py:445
  61.2 12.9 %collective-permute-start.13 = (bf16[320,1024]{1,0:T(8,128)(2,1)}, bf16[320,1024]{1,0:T(8,128)(2,1)}, u32[]{:S(2)}, u32[]{:S(2)}) collective-permute-start(bf16[320,1024]{1,0:T(8,128)(2,1)} %collective-permute-done.10.refs_10_), channel_id=1, source_target_pairs={{0,1},{1,0},{2,3},{3,2},{4,5},{5,4},{6,7},{7,6},{8,9},{9,8},{10,11... | collective-permute-start | bytes 1966088 | tf_op jit(solution)/shard_map/ppermute | solution.py:442
  62.1 15.9 %collective-permute-start.16 = (bf16[320,1024]{1,0:T(8,128)(2,1)}, bf16[320,1024]{1,0:T(8,128)(2,1)}, u32[]{:S(2)}, u32[]{:S(2)}) collective-permute-start(bf16[320,1024]{1,0:T(8,128)(2,1)} %collective-permute-done.10.refs_10_), channel_id=1, source_target_pairs={{0,4},{1,3},{4,8},{5,1},{8,12},{9,5},{12,14},{13,9},{14,10},{15,13... | collective-permute-start | bytes 1966088 | tf_op jit(solution)/shard_map/ppermute | solution.py:436
  63.8 23.6 %collective-permute-start.8 = (bf16[352,1024]{1,0:T(8,128)(2,1)}, bf16[352,1024]{1,0:T(8,128)(2,1)}, u32[]{:S(2)}, u32[]{:S(2)}) collective-permute-start(bf16[352,1024]{1,0:T(8,128)(2,1)} %collective-permute-done.5.refs_11_), channel_id=1, source_target_pairs={{0,1},{1,0},{2,3},{3,2},{4,5},{5,4},{6,7},{7,6},{8,9},{9,8},{10,11... | collective-permute-start | bytes 2162696 | tf_op jit(solution)/shard_map/ppermute | solution.py:442
  70.8 14.8 %collective-permute-start.15 = (bf16[352,1024]{1,0:T(8,128)(2,1)}, bf16[352,1024]{1,0:T(8,128)(2,1)}, u32[]{:S(2)}, u32[]{:S(2)}) collective-permute-start(bf16[352,1024]{1,0:T(8,128)(2,1)} %collective-permute-done.9.refs_9_), channel_id=1, source_target_pairs={{0,4},{1,3},{4,8},{5,1},{8,12},{9,5},{12,14},{13,9},{14,10},{15,13... | collective-permute-start | bytes 2162696 | tf_op jit(solution)/shard_map/ppermute | solution.py:436
  74.1 13.3 %collective-permute-start.29 = (bf16[2,16,4608]{2,1,0:T(8,128)(2,1)S(1)}, bf16[2,16,4608]{2,1,0:T(8,128)(2,1)}, u32[]{:S(2)}, u32[]{:S(2)}) collective-permute-start(bf16[2,16,4608]{2,1,0:T(8,128)(2,1)S(1)} %get-tuple-element.36), channel_id=1, source_target_pairs={{0,4},{2,6},{4,0},{6,2},{8,12},{10,14},{12,8},{14,10},{1,5},{3,7},... | collective-permute-start | bytes 884744 | tf_op jit(solution)/shard_map/ppermute | solution.py:445
  77.9 17.2 %collective-permute-start.11 = (bf16[352,1024]{1,0:T(8,128)(2,1)}, bf16[352,1024]{1,0:T(8,128)(2,1)}, u32[]{:S(2)}, u32[]{:S(2)}) collective-permute-start(bf16[352,1024]{1,0:T(8,128)(2,1)} %collective-permute-done.9.refs_9_), channel_id=1, source_target_pairs={{0,16},{16,0},{1,17},{17,1},{2,18},{18,2},{3,19},{19,3},{4,20},{20... | collective-permute-start | bytes 2162696 | tf_op jit(solution)/shard_map/ppermute | solution.py:439
  85.7 17.1 %collective-permute-start.12 = (bf16[352,1024]{1,0:T(8,128)(2,1)}, bf16[352,1024]{1,0:T(8,128)(2,1)}, u32[]{:S(2)}, u32[]{:S(2)}) collective-permute-start(bf16[352,1024]{1,0:T(8,128)(2,1)} %collective-permute-done.9.refs_9_), channel_id=1, source_target_pairs={{0,1},{1,0},{2,3},{3,2},{4,5},{5,4},{6,7},{7,6},{8,9},{9,8},{10,11... | collective-permute-start | bytes 2162696 | tf_op jit(solution)/shard_map/ppermute | solution.py:442
  87.4 15.4 %collective-permute-start.22 = (bf16[160,1024]{1,0:T(8,128)(2,1)}, bf16[160,1024]{1,0:T(8,128)(2,1)}, u32[]{:S(2)}, u32[]{:S(2)}) collective-permute-start(bf16[160,1024]{1,0:T(8,128)(2,1)} %constant_dynamic-slice_fusion), channel_id=1, source_target_pairs={{0,4},{1,3},{4,8},{5,1},{8,12},{9,5},{12,14},{13,9},{14,10},{15,13... | collective-permute-start | bytes 983048 | tf_op jit(solution)/shard_map/ppermute | solution.py:436
  87.4 17.0 %collective-permute-start.21 = (bf16[176,1024]{1,0:T(8,128)(2,1)}, bf16[176,1024]{1,0:T(8,128)(2,1)S(1)}, u32[]{:S(2)}, u32[]{:S(2)}) collective-permute-start(bf16[176,1024]{1,0:T(8,128)(2,1)} %constant_dynamic-slice_fusion.1), channel_id=1, source_target_pairs={{0,4},{1,3},{4,8},{5,1},{8,12},{9,5},{12,14},{13,9},{14,10},{15,13... | collective-permute-start | bytes 1081352 | tf_op jit(solution)/shard_map/ppermute | solution.py:436
  102.8 19.2 %collective-permute-start.17 = (bf16[352,1024]{1,0:T(8,128)(2,1)}, bf16[352,1024]{1,0:T(8,128)(2,1)S(1)}, u32[]{:S(2)}, u32[]{:S(2)}) collective-permute-start(bf16[352,1024]{1,0:T(8,128)(2,1)} %collective-permute-done.15.refs_9_), channel_id=1, source_target_pairs={{0,16},{16,0},{1,17},{17,1},{2,18},{18,2},{3,19},{19,3},{4,20},{20... | collective-permute-start | bytes 2162696 | tf_op jit(solution)/shard_map/ppermute | solution.py:439
  104.6 24.7 %collective-permute-start.23 = (bf16[176,1024]{1,0:T(8,128)(2,1)S(1)}, bf16[176,1024]{1,0:T(8,128)(2,1)S(1)}, u32[]{:S(2)}, u32[]{:S(2)}) collective-permute-start(bf16[176,1024]{1,0:T(8,128)(2,1)S(1)} %collective-permute-done.21.refs_10_), channel_id=1, source_target_pairs={{0,16},{16,0},{1,17},{17,1},{2,18},{18,2},{3,19},{19,3},{4,20},{20... | collective-permute-start | bytes 1081352 | tf_op jit(solution)/shard_map/ppermute | solution.py:439
  107.2 46.8 %collective-permute-start.18 = (bf16[352,1024]{1,0:T(8,128)(2,1)}, bf16[352,1024]{1,0:T(8,128)(2,1)S(1)}, u32[]{:S(2)}, u32[]{:S(2)}) collective-permute-start(bf16[352,1024]{1,0:T(8,128)(2,1)} %collective-permute-done.15.refs_9_), channel_id=1, source_target_pairs={{0,1},{1,0},{2,3},{3,2},{4,5},{5,4},{6,7},{7,6},{8,9},{9,8},{10,11... | collective-permute-start | bytes 2162696 | tf_op jit(solution)/shard_map/ppermute | solution.py:442
  107.3 57.1 %collective-permute-start.25 = (bf16[160,1024]{1,0:T(8,128)(2,1)}, bf16[160,1024]{1,0:T(8,128)(2,1)S(1)}, u32[]{:S(2)}, u32[]{:S(2)}) collective-permute-start(bf16[160,1024]{1,0:T(8,128)(2,1)} %collective-permute-done.22.refs_11_), channel_id=1, source_target_pairs={{0,1},{1,0},{2,3},{3,2},{4,5},{5,4},{6,7},{7,6},{8,9},{9,8},{10,11... | collective-permute-start | bytes 983048 | tf_op jit(solution)/shard_map/ppermute | solution.py:442
  122.0 42.3 %collective-permute-start.24 = (bf16[176,1024]{1,0:T(8,128)(2,1)S(1)}, bf16[176,1024]{1,0:T(8,128)(2,1)S(1)}, u32[]{:S(2)}, u32[]{:S(2)}) collective-permute-start(bf16[176,1024]{1,0:T(8,128)(2,1)S(1)} %collective-permute-done.21.refs_10_), channel_id=1, source_target_pairs={{0,1},{1,0},{2,3},{3,2},{4,5},{5,4},{6,7},{7,6},{8,9},{9,8},{10,11... | collective-permute-start | bytes 1081352 | tf_op jit(solution)/shard_map/ppermute | solution.py:442
  129.3 24.7 %collective-permute-start.20 = (bf16[352,1024]{1,0:T(8,128)(2,1)S(1)}, bf16[352,1024]{1,0:T(8,128)(2,1)S(1)}, u32[]{:S(2)}, u32[]{:S(2)}) collective-permute-start(bf16[352,1024]{1,0:T(8,128)(2,1)S(1)} %collective-permute-done.17.refs_11_), channel_id=1, source_target_pairs={{0,1},{1,0},{2,3},{3,2},{4,5},{5,4},{6,7},{7,6},{8,9},{9,8},{10,11... | collective-permute-start | bytes 2162696 | tf_op jit(solution)/shard_map/ppermute | solution.py:442
  129.3 35.1 %collective-permute-start.26 = (bf16[176,1024]{1,0:T(8,128)(2,1)S(1)}, bf16[176,1024]{1,0:T(8,128)(2,1)S(1)}, u32[]{:S(2)}, u32[]{:S(2)}) collective-permute-start(bf16[176,1024]{1,0:T(8,128)(2,1)S(1)} %collective-permute-done.23.refs_12_), channel_id=1, source_target_pairs={{0,1},{1,0},{2,3},{3,2},{4,5},{5,4},{6,7},{7,6},{8,9},{9,8},{10,11... | collective-permute-start | bytes 1081352 | tf_op jit(solution)/shard_map/ppermute | solution.py:442
  (34 other events, 359.7 us)

commit v2 on v0

v2 whole, which is shorter than its diff:
```python
import functools

import jax
import jax.numpy as jnp
import numpy as np
from jax import lax
from jax.experimental import pallas as pl
from jax.experimental.pallas import tpu as pltpu
from jax.sharding import PartitionSpec as P

adapter_scale = 2.0
ALL = ("group", "shard", "dp")
NT = (((1,), (1,)), ((), ()))
VMEM_LIMIT = 60 << 20
COST = 1e6
GATE = 1e5
ANY = pl.BlockSpec(memory_space=pl.ANY)
SMEM = pl.BlockSpec(memory_space=pltpu.SMEM)


def ring_of(shards):
    if shards == 8:
        return [0, 2, 4, 6, 7, 5, 3, 1]
    return list(range(shards))


def dot(x, y):
    return jnp.dot(x, y, preferred_element_type=jnp.float32)


def dot_nt(x, y):
    return lax.dot_general(x, y, NT, preferred_element_type=jnp.float32)


def groups_of(shape, axis, rank):
    return lax.div(lax.broadcasted_iota(jnp.int32, shape, axis), jnp.int32(rank))


def ranks(home, wanted, slots):
    count = jnp.int32(0)
    places = []
    for i in range(slots):
        hit = home(i) == wanted
        places.append(jnp.where(hit, count, -1))
        count = count + hit.astype(jnp.int32)
    return places, count


def slot_at(places, place):
    found = jnp.int32(0)
    for i, here in enumerate(places):
        found = jnp.where(here == place, jnp.int32(i), found)
    return found


def head_kernel(
    dims, info, home, length, adapter, owner, sibling, held, grad, grad_sib, down, up,
    send, packed, table, masked, back_work, mask_slots, back_slots, low_part,
    rows_v, grad_v, down_v, up_v, mask_v, mask_w, back_w, back_v, low_v, sums_v,
    row_sem, in_sem, down_sem, sum_sem, pack_sem, out_sem,
):
    slots, tokens, blk, shards, cols, rank, adapters, width = dims
    core = info[0]
    first = (1 - core) * (shards // 2)
    inputs = [
        pltpu.make_async_copy(grad, grad_v.at[0], in_sem.at[0]),
        pltpu.make_async_copy(grad_sib, grad_v.at[1], in_sem.at[1]),
        pltpu.make_async_copy(up, up_v, in_sem.at[2]),
    ]
    for copy in inputs:
        copy.start()
    stream = Stream(dims, first, held, down, rows_v, down_v, sums_v, row_sem, down_sem, sum_sem, pack_sem)
    stream.start()

    mine, mine_count = ranks(lambda i: home[i], core, slots)
    other, other_count = ranks(lambda i: home[i], 1 - core, slots)
    packs = [slot_at(other, k) for k in range(blk)]
    theirs, _ = ranks(lambda i: sibling[0, i], core, slots)
    there_count = blk - mine_count
    chosen = []
    for w in range(blk):
        local = jnp.where(core == 0, w < mine_count, w >= there_count)
        local_place = jnp.where(core == 0, w, w - there_count)
        there_place = jnp.clip(jnp.where(core == 0, w - mine_count, w), 0, blk - 1)
        local_slot = slot_at(mine, local_place)
        there_slot = slot_at(theirs, there_place)
        adapter_w = jnp.where(local, adapter[local_slot], sibling[2, there_slot])
        length_w = jnp.where(local, length[local_slot], sibling[1, there_slot])
        table[0, w] = local.astype(jnp.int32)
        table[1, w] = jnp.where(local, local_slot, there_place)
        table[2, w] = packs[w]
        chosen.append((adapter_w, length_w))
    for copy in inputs:
        copy.wait()
    token = lax.broadcasted_iota(jnp.int32, (tokens, width), 0)
    zero = jnp.zeros((), jnp.bfloat16)
    for i in range(slots):
        is_mine = home[i] == core
        place = jnp.where(is_mine, mine[i], other[i])
        count = jnp.where(is_mine, mine_count, other_count)
        work = jnp.clip(jnp.where(core == 0, place, blk - count + place), 0, blk - 1)
        source = jnp.where(is_mine, 0, 1)
        live = jnp.where(home[i] >= 0, length[i], 0)
        at = pl.ds(pl.multiple_of(work * tokens, tokens), tokens)
        mask_v[pl.ds(i * tokens, tokens), :] = jnp.where(token < live, grad_v[source, at, :], zero)
    flat = adapters * rank
    back = own_columns(dims, [adapter[i] for i in range(slots)], adapter_scale * dot_nt(mask_v[...], up_v[...]))
    back_v[...] = dot_nt(spread_matrix(dims, owner), back).astype(jnp.bfloat16)
    low_v[...] = jnp.zeros_like(low_v)
    mask_slots_out = pltpu.make_async_copy(mask_v, mask_slots, out_sem.at[0])
    back_slots_out = pltpu.make_async_copy(back_v, back_slots, out_sem.at[1])
    mask_slots_out.start()
    back_slots_out.start()
    stream.run(back_v, low_v, send, packed, packs)
    low_out = pltpu.make_async_copy(low_v, low_part, out_sem.at[2])
    low_out.start()
    for w, (_, length_w) in enumerate(chosen):
        own = pl.ds(w * tokens, tokens)
        mask_w[own, :] = jnp.where(token < length_w, grad_v[0, own, :], zero)
    masked_out = pltpu.make_async_copy(mask_w, masked, out_sem.at[3])
    masked_out.start()
    back_w[...] = own_columns(
        dims, [adapter_w for adapter_w, _ in chosen], adapter_scale * dot_nt(mask_w[...], up_v[...])
    )
    back_out = pltpu.make_async_copy(back_w, back_work, out_sem.at[4])
    back_out.start()
    stream.drain(send, packed, packs)
    for copy in (mask_slots_out, back_slots_out, low_out, masked_out, back_out):
        copy.wait()


def tail_kernel(
    dims, info, adapter, owner, table, held, down, mask_slots, back_slots, low_part, after,
    keep, keep_up, send_up, packed, low_slots, low_send,
    rows_v, down_v, mask_v, back_v, low_v, sums_v, low_b, up_sums_v,
    row_sem, in_sem, down_sem, sum_sem, pack_sem, up_sem, low_sem,
):
    slots, tokens, blk, shards, cols, rank, adapters, width = dims
    core = info[0]
    first = core * (shards // 2)
    inputs = [
        pltpu.make_async_copy(back_slots, back_v, in_sem.at[0]),
        pltpu.make_async_copy(low_part, low_v, in_sem.at[1]),
        pltpu.make_async_copy(mask_slots, mask_v, in_sem.at[2]),
    ]
    for copy in inputs:
        copy.start()
    stream = Stream(dims, first, held, down, rows_v, down_v, sums_v, row_sem, down_sem, sum_sem, pack_sem)
    stream.start()
    packs = [jnp.clip(table[2, k], 0, slots - 1) for k in range(blk)]
    for copy in inputs:
        copy.wait()
    stream.run(back_v, low_v, keep, packed, packs)
    low_b[...] = own_columns(dims, [adapter[i] for i in range(slots)], low_v[...])
    lows = [pltpu.make_async_copy(low_b, low_slots, low_sem.at[blk])]
    for k in range(blk):
        taken = pl.ds(pl.multiple_of(packs[k] * tokens, tokens), tokens)
        lows.append(
            pltpu.make_async_copy(
                low_b.at[taken, :], low_send.at[pl.ds(k * tokens, tokens), :], low_sem.at[k]
            )
        )
    for copy in lows:
        copy.start()
    low_t = dot_nt(spread_matrix(dims, owner), low_b[...]).astype(jnp.bfloat16)
    up_sums_v[...] = adapter_scale * dot(low_t, mask_v[...])
    half_width = width // 2

    def up_copy(part, target_ref):
        return pltpu.make_async_copy(
            up_sums_v.at[:, pl.ds(part * half_width, half_width)], target_ref, up_sem.at[part]
        )

    for part in range(2):

        @pl.when(core == part)
        def _():
            up_copy(part, keep_up).start()
            up_copy(1 - part, send_up).start()

    stream.drain(keep, packed, packs)
    for copy in lows:
        copy.wait()
    for part in range(2):
        up_copy(part, keep_up).wait()


def own_columns(dims, chosen, full):
    slots, tokens, blk, shards, cols, rank, adapters, width = dims
    column_adapter = groups_of((tokens, adapters * rank), 1, rank)
    parts = []
    for i, adapter_i in enumerate(chosen):
        kept = column_adapter == adapter_i
        parts.append(jnp.where(kept, full[i * tokens:(i + 1) * tokens, :], 0.0))
    return jnp.concatenate(parts, axis=0).astype(jnp.bfloat16)


def spread_matrix(dims, owner):
    slots, tokens, blk, shards, cols, rank, adapters, width = dims
    flat = adapters * rank
    row_group = groups_of((flat, flat), 0, rank)
    column_group = groups_of((flat, flat), 1, rank)
    row_rank = lax.broadcasted_iota(jnp.int32, (flat, flat), 0) - row_group * rank
    column_rank = lax.broadcasted_iota(jnp.int32, (flat, flat), 1) - column_group * rank
    target = jnp.full((flat, flat), -1, jnp.int32)
    for a in range(adapters):
        target = jnp.where(column_group == a, owner[a], target)
    spread = jnp.where((target == row_group) & (row_rank == column_rank), 1.0, 0.0)
    return spread.astype(jnp.bfloat16)


class Stream:
    def __init__(self, dims, first, held, down, rows_v, down_v, sums_v, row_sem, down_sem, sum_sem, pack_sem):
        slots, self.tokens, self.blk, shards, self.cols, rank, adapters, width = dims
        self.count = shards // 2
        self.first = first
        self.held, self.down, self.rows_v, self.down_v, self.sums_v = held, down, rows_v, down_v, sums_v
        self.row_sem, self.down_sem, self.sum_sem, self.pack_sem = row_sem, down_sem, sum_sem, pack_sem

    def at(self, j):
        return pl.ds(pl.multiple_of((self.first + j) * self.cols, self.cols), self.cols)

    def row_copy(self, j):
        return pltpu.make_async_copy(self.held.at[:, self.at(j)], self.rows_v.at[j], self.row_sem.at[j])

    def down_copy(self, j):
        return pltpu.make_async_copy(self.down.at[:, self.at(j)], self.down_v.at[j], self.down_sem.at[j])

    def sum_copy(self, j, target):
        return pltpu.make_async_copy(
            self.sums_v.at[j], target.at[:, pl.ds(j * self.cols, self.cols)], self.sum_sem.at[j]
        )

    def pack_copy(self, j, k, packed, packs):
        taken = pl.ds(pl.multiple_of(packs[k] * self.tokens, self.tokens), self.tokens)
        return pltpu.make_async_copy(
            self.rows_v.at[j, taken, :],
            packed.at[pl.ds(k * self.tokens, self.tokens), pl.ds(j * self.cols, self.cols)],
            self.pack_sem.at[j, k],
        )

    def start(self):
        for j in range(self.count):
            self.row_copy(j).start()
            self.down_copy(j).start()

    def run(self, back_v, low_v, target, packed, packs):
        for j in range(self.count):
            self.row_copy(j).wait()
            self.down_copy(j).wait()
            for k in range(self.blk):
                self.pack_copy(j, k, packed, packs).start()
            self.sums_v[j] = dot(back_v[...], self.rows_v[j])
            self.sum_copy(j, target).start()
            low_v[...] += dot_nt(self.rows_v[j], self.down_v[j])

    def drain(self, target, packed, packs):
        for j in range(self.count):
            self.sum_copy(j, target).wait()
            for k in range(self.blk):
                self.pack_copy(j, k, packed, packs).wait()


def halve_kernel(parts, bit_at, after, info, *refs):
    kept = refs[:parts]
    arrived = refs[parts:2 * parts]
    keep, away = refs[2 * parts + after:2 * parts + after + 2]
    scratch = refs[2 * parts + after + 2:]
    kept_v, arrived_v = scratch[:parts], scratch[parts:2 * parts]
    keep_v, away_v, in_sem, out_sem = scratch[2 * parts:]
    count = keep.shape[0]
    here = info[bit_at]

    def loads(i):
        copies = []
        for p in range(parts):
            copies.append(pltpu.make_async_copy(kept[p].at[i], kept_v[p].at[i], in_sem.at[0, p, i]))
            copies.append(pltpu.make_async_copy(arrived[p].at[i], arrived_v[p].at[i], in_sem.at[1, p, i]))
        return copies

    for i in range(count):
        for copy in loads(i):
            copy.start()
    outs = []
    for i in range(count):
        for copy in loads(i):
            copy.wait()
        base = 0
        for p in range(parts):
            size = kept[p].shape[-1]
            at = pl.ds(base, size)
            keep_v[i, :, at] = kept_v[p][i, here] + arrived_v[p][i, here].astype(jnp.float32)
            away_v[i, :, at] = (
                kept_v[p][i, 1 - here] + arrived_v[p][i, 1 - here].astype(jnp.float32)
            ).astype(jnp.bfloat16)
            base += size
        outs.append(pltpu.make_async_copy(away_v.at[i], away.at[i], out_sem.at[0, i]))
        outs.append(pltpu.make_async_copy(keep_v.at[i], keep.at[i], out_sem.at[1, i]))
        outs[-2].start()
        outs[-1].start()
    for out in outs:
        out.wait()


def weight_kernel(dims, jobs, first, last, through, after, *refs):
    slots, tokens, blk, shards, cols, rank, adapters, width = dims
    refs = list(refs)

    def take(n):
        taken, refs[:n] = refs[:n], []
        return taken

    info, table, held, got, got_other, masked, back, down = take(8)
    up, low_slots, low_got = take(3) if last else (None, None, None)
    acc_in = None if first else take(1)[0]
    if not first:
        take(1)
    n_pieces = sum(len(pieces) for _, pieces, _ in jobs)
    piece_refs = take(n_pieces)
    take(through + after)
    input_grad, result = take(2)
    handed = take(sum(hand for _, _, hand in jobs))
    take(through)
    mask_v, back_v, up_v, low_v, acc_v, final_v = take(6)
    per_job = take(4 * len(jobs))
    sem, row_sem, piece_sem, out_sem, low_sem = refs
    core = info[0]

    starts = [
        pltpu.make_async_copy(masked, mask_v, sem.at[0]),
        pltpu.make_async_copy(back, back_v, sem.at[1]),
    ]
    for copy in starts:
        copy.start()
    work = []
    taken = 0
    for n, (shard_at, pieces, hand) in enumerate(jobs):
        weight_v, rows_v, down_v, out_v = per_job[4 * n:4 * n + 4]
        at = pl.ds(pl.multiple_of(info[shard_at] * cols, cols), cols)
        here = lax.div(info[shard_at], shards // 2) == core
        at_half = pl.ds(pl.multiple_of(lax.rem(info[shard_at], shards // 2) * cols, cols), cols)
        loads = []
        for row_at, only, cut in pieces:
            piece = piece_refs[taken]
            row = 0 if row_at is None else pl.multiple_of(info[row_at], 16)
            size = piece.shape[0] if cut is None else cut[1]
            source = piece if cut is None else piece.at[pl.ds(*cut), :]
            to = weight_v.at[pl.ds(row, size), :]
            copy = pltpu.make_async_copy(source, to, piece_sem.at[taken])
            if only is None:
                copy.start()
                loads.append((copy, None))
            else:

                @pl.when(core == only)
                def _():
                    copy.start()

                loads.append((copy, only))
            taken += 1
        down_in = pltpu.make_async_copy(down.at[:, at], down_v, row_sem.at[n, blk])
        down_in.start()
        loads.append((down_in, None))
        row_loads = []
        for w in range(blk):
            to = rows_v.at[pl.ds(w * tokens, tokens), :]

            @pl.when(table[0, w] == 1)
            def _():
                row = pl.multiple_of(jnp.clip(table[1, w], 0, slots - 1) * tokens, tokens)
                pltpu.make_async_copy(held.at[pl.ds(row, tokens), at], to, row_sem.at[n, w]).start()

            remote = table[0, w] != 1
            row_got = pl.multiple_of(jnp.clip(table[1, w], 0, blk - 1) * tokens, tokens)

            @pl.when(remote & here)
            def _():
                pltpu.make_async_copy(
                    got.at[pl.ds(row_got, tokens), at_half], to, row_sem.at[n, w]
                ).start()

            @pl.when(remote & jnp.logical_not(here))
            def _():
                pltpu.make_async_copy(
                    got_other.at[pl.ds(row_got, tokens), at_half], to, row_sem.at[n, w]
                ).start()

            row_loads.append(
                pltpu.make_async_copy(held.at[pl.ds(0, tokens), at], to, row_sem.at[n, w])
            )
        if n == 0 and not first:
            acc_load = pltpu.make_async_copy(acc_in, acc_v, sem.at[2])
            acc_load.start()
        work.append((loads, row_loads, at, weight_v, rows_v, down_v, out_v, hand))
    if last:
        up_in = pltpu.make_async_copy(up, up_v, sem.at[3])
        up_in.start()
        for w in range(blk):
            to = low_v.at[pl.ds(w * tokens, tokens), :]

            @pl.when(table[0, w] == 1)
            def _():
                row = pl.multiple_of(jnp.clip(table[1, w], 0, slots - 1) * tokens, tokens)
                pltpu.make_async_copy(low_slots.at[pl.ds(row, tokens), :], to, low_sem.at[w]).start()

            @pl.when(table[0, w] != 1)
            def _():
                row = pl.multiple_of(jnp.clip(table[1, w], 0, blk - 1) * tokens, tokens)
                pltpu.make_async_copy(low_got.at[pl.ds(row, tokens), :], to, low_sem.at[w]).start()

    for copy in starts:
        copy.wait()
    tile = min(256, width)
    back_tile = min(256, cols)
    outs = []
    handed_at = 0
    for n, (loads, row_loads, at, weight_v, rows_v, down_v, out_v, hand) in enumerate(work):
        for copy, only in loads:
            if only is None:
                copy.wait()
            else:

                @pl.when(core == only)
                def _():
                    copy.wait()

        if hand:
            out = pltpu.make_async_copy(weight_v, handed[handed_at], out_sem.at[1, n])
            handed_at += 1
            out.start()
            outs.append(out)
        for i in range(cols // back_tile):
            cut = pl.ds(i * back_tile, back_tile)
            out_v[:, cut] = (
                dot_nt(mask_v[...], weight_v[cut, :]) + dot(back_v[...], down_v[:, cut])
            ).astype(out_v.dtype)
        out = pltpu.make_async_copy(out_v, input_grad.at[:, at], out_sem.at[0, n])
        out.start()
        outs.append(out)
        for copy in row_loads:
            copy.wait()
        if n == 0 and not first:
            acc_load.wait()
        for i in range(width // tile):
            cut = pl.ds(i * tile, tile)
            product = dot(rows_v[...], weight_v[:, cut])
            if first and n == 0:
                acc_v[:, cut] = product
            else:
                acc_v[:, cut] += product
    if last:
        up_in.wait()
        for w in range(blk):
            pltpu.make_async_copy(
                low_slots.at[pl.ds(0, tokens), :], low_v.at[pl.ds(w * tokens, tokens), :], low_sem.at[w]
            ).wait()
        final_v[...] = (acc_v[...] + adapter_scale * dot(low_v[...], up_v[...])).astype(jnp.bfloat16)
        finish = pltpu.make_async_copy(final_v, result, sem.at[4])
    else:
        finish = pltpu.make_async_copy(acc_v, result, sem.at[4])
    finish.start()
    for out in outs:
        out.wait()
    finish.wait()


def gate_kernel(*refs):
    pass


def gate(values, tokens):
    out = pl.pallas_call(
        gate_kernel,
        out_shape=tuple(jax.ShapeDtypeStruct(value.shape, value.dtype) for value in values),
        in_specs=[ANY] * (len(values) + len(tokens)),
        out_specs=(ANY,) * len(values),
        input_output_aliases={i: i for i in range(len(values))},
        cost_estimate=cost(GATE),
        name="gate",
    )(*values, *tokens)
    return list(out)


def cost(us):
    return pl.CostEstimate(flops=int(us * COST), bytes_accessed=0, transcendentals=0)


def body(
    held_rows,
    block_home,
    block_len,
    block_adapter,
    adapter_down,
    adapter_up,
    value_weight,
    adapter_owner,
    value_grad,
):
    groups, shards, cores = (lax.axis_size(name) for name in ALL)
    slots = block_home.shape[0]
    blk = slots // 2
    tokens = held_rows.shape[0] // slots
    model = held_rows.shape[1]
    cols, width = value_weight.shape
    adapters, rank = adapter_down.shape[:2]
    flat = adapters * rank
    work_rows = blk * tokens
    held_tokens = slots * tokens
    dims = (slots, tokens, blk, shards, cols, rank, adapters, width)
    f32, bf16 = jnp.float32, jnp.bfloat16
    sds = jax.ShapeDtypeStruct
    dma = pltpu.SemaphoreType.DMA
    vmem = pltpu.VMEM
    params = pltpu.CompilerParams(vmem_limit_bytes=VMEM_LIMIT)

    piece = -(-cols // 48) * 16
    steps = shards // 2
    ring = ring_of(shards)
    place = {shard: i for i, shard in enumerate(ring)}
    bits = shards.bit_length() - 1
    middle_at = (cols - piece) // 2 // 16 * 16
    middle_cut = (piece - middle_at, cols - 2 * piece)
    rows = []
    for parity in range(2):
        for core in range(2):
            for shard in range(shards):
                way = -1 if core == 0 else 1
                mine = [ring[(place[shard] + way * k) % shards] for k in range(1, steps + 1)]
                theirs = [ring[(place[shard] - way * k) % shards] for k in range(1, steps + 1)]
                edge_at, other_at = (0, cols - piece) if parity == 0 else (cols - piece, 0)
                rows.append(
                    [core, shard, edge_at, piece, other_at]
                    + [(shard >> bit) & 1 for bit in range(bits)]
                    + mine
                    + theirs
                )
    SHARD, EDGE, MIDDLE, OTHER, BITS = 1, 2, 3, 4, 5
    MINE = BITS + bits
    THEIRS = MINE + steps
    group_at, shard_at, core_at = (lax.axis_index(name) for name in ALL)
    parity_at = lax.rem(group_at, 2)
    plan = jnp.asarray(np.array(rows, np.int32))
    info = lax.dynamic_slice(
        plan, ((parity_at * 2 + core_at) * shards + shard_at, 0), (1, plan.shape[1])
    ).reshape(-1)

    def index(g, s, c):
        return (g * shards + s) * cores + c

    ring_pairs = []
    for g in range(groups):
        for i in range(shards):
            ring_pairs.append((index(g, ring[i], 0), index(g, ring[(i + 1) % shards], 0)))
            ring_pairs.append((index(g, ring[i], 1), index(g, ring[(i - 1) % shards], 1)))
    first_core = [
        (index(g, s, 0), index(g ^ 1, s, 0)) for g in range(groups) for s in range(shards)
    ]

    def around(value):
        return lax.ppermute(value, ALL, ring_pairs)

    def partner(value):
        return lax.ppermute(value, "group", [(g, g ^ 1) for g in range(groups)])

    def swap(value):
        return lax.ppermute(value, "dp", [(0, 1), (1, 0)])

    def flip(value, bit):
        return lax.ppermute(value, "shard", [(s, s ^ bit) for s in range(shards)])

    down = adapter_down.reshape(flat, model)
    up = adapter_up.reshape(flat, width)
    meta = jnp.stack([block_home, block_len, block_adapter])
    sibling = swap(meta)
    grad_sib = swap(value_grad)
    edge_start = jnp.where(parity_at == 0, 0, cols - piece)
    edge_rows = around(lax.dynamic_slice(value_weight, (edge_start, 0), (piece, width)))
    middle_rows = around(value_weight[middle_at:middle_at + piece])

    half_model, half_width = model // 2, width // 2
    half = half_model + half_width
    half_chunks = shards // 2
    stream_scratch = [
        vmem((half_chunks, held_tokens, cols), bf16),
        vmem((half_chunks, flat, cols), bf16),
    ]
    stream_sems = [dma((half_chunks,)), dma((3,)), dma((half_chunks,)), dma((half_chunks,)), dma((half_chunks, blk))]
    send, packed, table, masked, back, mask_slots, back_slots, low_part = pl.pallas_call(
        functools.partial(head_kernel, dims),
        out_shape=(
            sds((flat, half_model), f32),
            sds((work_rows, half_model), bf16),
            sds((3, blk), jnp.int32),
            sds((work_rows, width), bf16),
            sds((work_rows, flat), bf16),
            sds((held_tokens, width), bf16),
            sds((flat, held_tokens), bf16),
            sds((held_tokens, flat), f32),
        ),
        in_specs=[SMEM] * 6 + [ANY] * 5,
        out_specs=(ANY, ANY, SMEM) + (ANY,) * 5,
        scratch_shapes=[
            stream_scratch[0],
            vmem((2, work_rows, width), bf16),
            stream_scratch[1],
            vmem((flat, width), bf16),
            vmem((held_tokens, width), bf16),
            vmem((work_rows, width), bf16),
            vmem((work_rows, flat), bf16),
            vmem((flat, held_tokens), bf16),
            vmem((held_tokens, flat), f32),
            vmem((half_chunks, flat, cols), f32),
        ] + stream_sems + [dma((5,))],
        compiler_params=params,
        cost_estimate=cost(7),
        name="head",
    )(
        info, block_home, block_len, block_adapter, adapter_owner, sibling,
        held_rows, value_grad, grad_sib, down, up,
    )
    sent = swap(send)
    got = swap(packed)

    edges, middles, others = [], [], []

    def next_edge(token):
        value = around(edges[-1]) if edges else edge_rows
        (value,) = gate([value], [token])
        edges.append(value)
        others.append(partner(value))

    def next_middle(token):
        value = around(middles[-1]) if middles else middle_rows
        (value,) = gate([value], [token])
        middles.append(value)

    next_edge(low_part)

    keep, keep_up, send_up, packed_other, low_slots, low_send = pl.pallas_call(
        functools.partial(tail_kernel, dims),
        out_shape=(
            sds((flat, half_model), f32),
            sds((flat, half_width), f32),
            sds((flat, half_width), f32),
            sds((work_rows, half_model), bf16),
            sds((held_tokens, flat), bf16),
            sds((work_rows, flat), bf16),
        ),
        in_specs=[SMEM] * 4 + [ANY] * 6,
        out_specs=(ANY,) * 6,
        scratch_shapes=stream_scratch + [
            vmem((held_tokens, width), bf16),
            vmem((flat, held_tokens), bf16),
            vmem((held_tokens, flat), f32),
            vmem((half_chunks, flat, cols), f32),
            vmem((held_tokens, flat), bf16),
            vmem((flat, width), f32),
        ] + stream_sems + [dma((2,)), dma((blk + 1,))],
        compiler_params=params,
        cost_estimate=cost(7),
        name="tail",
    )(
        info, block_adapter, adapter_owner, table,
        held_rows, down, mask_slots, back_slots, low_part, edges[0],
    )
    next_middle(keep_up)
    sent_up = swap(send_up)
    low_got = swap(low_send)
    got_other = swap(packed_other)

    def halve(kept, arrived, bit, after=()):
        parts = len(kept)
        count = shards >> (bit + 1)
        owned = flat // shards
        kept = [part.reshape(count, 2, owned, -1) for part in kept]
        arrived = [part.reshape(count, 2, owned, -1) for part in arrived]
        return pl.pallas_call(
            functools.partial(halve_kernel, parts, BITS + bit, len(after)),
            out_shape=(sds((count, owned, half), f32), sds((count, owned, half), bf16)),
            in_specs=[SMEM] + [ANY] * (2 * parts + len(after)),
            out_specs=(ANY, ANY),
            scratch_shapes=[vmem(part.shape, part.dtype) for part in kept + arrived]
            + [vmem((count, owned, half), f32), vmem((count, owned, half), bf16)]
            + [dma((2, parts, count)), dma((2, count))],
            compiler_params=params,
            cost_estimate=cost(2),
            name="halve",
        )(info, *kept, *arrived, *after)

    def multiply(state, jobs, pieces, last=False, through=(), after=(), us=6):
        input_grad, acc = state
        first = acc is None
        operands = [info, table, held_rows, got, got_other, masked, back, down]
        if last:
            operands += [up, low_slots, low_got]
        aliases = {}
        if not first:
            operands.append(acc)
            aliases[len(operands)] = 0
            operands.append(input_grad)
        operands += pieces
        hands = sum(hand for _, _, hand in jobs)
        for i, passed in enumerate(through):
            aliases[len(operands)] = 2 + hands + i
            operands.append(passed)
        operands += after
        result = sds((work_rows, width), bf16 if last else f32)
        out_shape = (
            (sds((work_rows, model), bf16), result)
            + (sds((cols, width), bf16),) * hands
            + tuple(sds(passed.shape, passed.dtype) for passed in through)
        )
        out = pl.pallas_call(
            functools.partial(weight_kernel, dims, jobs, first, last, len(through), len(after)),
            out_shape=out_shape,
            in_specs=[SMEM] * 2 + [ANY] * (len(operands) - 2),
            out_specs=(ANY,) * len(out_shape),
            scratch_shapes=[
                vmem((work_rows, width), bf16),
                vmem((work_rows, flat), bf16),
                vmem((flat, width), bf16),
                vmem((work_rows, flat), bf16),
                vmem((work_rows, width), f32),
                vmem((work_rows, width), bf16),
            ]
            + [
                vmem((cols, width), bf16),
                vmem((work_rows, cols), bf16),
                vmem((flat, cols), bf16),
                vmem((work_rows, cols), bf16),
            ] * len(jobs)
            + [dma((5,)), dma((len(jobs), blk + 1)), dma((len(pieces),)), dma((2, len(jobs))), dma((blk,))],
            input_output_aliases=aliases,
            compiler_params=params,
            cost_estimate=cost(us),
            name="weights",
        )(*operands)
        return out[:2], out[2:2 + hands], out[2 + hands:]

    sums, away = halve([keep, keep_up], [sent, sent_up], 0, middles)
    moved = flip(away, 1)
    bit = 1
    if steps > 2:
        next_edge(sums)

    whole = [(EDGE, None, None), (MIDDLE, None, middle_cut), (OTHER, None, None)]
    full = [(None, None, None)]
    state, _, _ = multiply(
        (None, None), [(SHARD, full, 0)], [value_weight], after=edges[1:] or [sums], us=4
    )
    after = []
    if steps > 2:
        next_middle(state[1])
        after = [middles[-1]]
    last = None
    for k in range(1, steps):
        jobs = [(MINE + k - 1, whole, 1)]
        pieces = [edges[k - 1], middles[k - 1], others[k - 1]]
        if k > 1:
            jobs.append((THEIRS + k - 2, full, 0))
            pieces.append(handed)
        state, out, _ = multiply(state, jobs, pieces, after=after, us=4 if k == 1 else 7)
        after = []
        handed = swap(out[0])
        if len(edges) < steps - 1:
            next_edge(state[1])
            after.append(edges[-1])
            if len(middles) < len(edges) - 1:
                next_middle(state[1])
                after.append(middles[-1])
        elif len(middles) < steps - 1:
            next_middle(state[1])
            after.append(middles[-1])
        if len(middles) == steps - 1 and last is None:
            last = around(jnp.where(core_at == 0, edges[-1], middles[-1]))
        if k > 1 and bit < bits:
            sums, away = halve([sums], [moved], bit, after)
            moved = flip(away, 1 << bit)
            after.append(sums)
            bit += 1
    (last,) = gate([last], [state[1], away])
    last_sib = swap(last)
    last_other = lax.ppermute(last, ALL, first_core)
    state, _, _ = multiply(state, [(THEIRS + steps - 2, full, 0)], [handed], after=[last], us=4)
    (last_other,) = gate([last_other], [state[1]])
    other_sib = swap(last_other)
    jobs = [(
        MINE + steps - 1,
        [(EDGE, 0, None), (MIDDLE, 1, middle_cut), (MIDDLE, 0, middle_cut), (EDGE, 1, None)]
        + [(OTHER, 0, None), (OTHER, 1, None)],
        0,
    )]
    pieces = [last, last, last_sib, last_sib, last_other, other_sib]
    state, _, _ = multiply(state, jobs, pieces, last=True, us=4)
    input_grad, value_projection_output = state
    sums = sums.reshape(-1, half)
    moved = moved.reshape(-1, half).astype(f32)
    own_down = sums[:, :half_model] + moved[:, :half_model]
    own_up = sums[:, half_model:] + moved[:, half_model:]

    per_shard = adapters // shards
    return (
        value_projection_output,
        input_grad,
        own_down.reshape(per_shard, rank, -1),
        own_up.reshape(per_shard, rank, -1),
    )


def solution(mesh):
    placed = (
        P(ALL, None),
        P(ALL),
        P(ALL),
        P(ALL),
        P("group", None, None),
        P("group", None, None),
        P("shard", None),
        P("group"),
        P(ALL, None),
    )
    return jax.shard_map(
        body,
        mesh=mesh,
        in_specs=placed,
        out_specs=(
            P(ALL, None),
            P(ALL, None),
            P(("group", "shard"), None, "dp"),
            P(("group", "shard"), None, "dp"),
        ),
        check_vma=False,
    )
```

time: 348 us -> 134 us (0.39)
  waiting for transfers between devices: 164 us -> 20.6 us
  Pallas kernels: 0 us -> 73.5 us
  local copies, waits for them, and re-layouts: 80.4 us -> 14.8 us
  matrix products: 47 us -> 0 us
  other arithmetic: 20.9 us -> 3.48 us
  between operations: 15.7 us -> 1.11 us
  starting transfers between devices: 15.3 us -> 20.1 us
  blocking collectives: 3.66 us -> 0 us
    all_gather x1 -> x0, waiting for transfers between devices: 86.5 us -> none  [body(): full_weight = lax.all_gather(value_weight, 'shard', axis=0, tiled=True)]
    pallas_call x0 -> x19, Pallas kernels: none -> 73.5 us  [the longest x6 43.9 us: multiply(): pl.pallas_call(functools.partial(weight_kernel, dims, jobs, first, last,...]
    reduce_scatter x2 -> x0, waiting for transfers between devices: 67.9 us -> none  [the longest x1 67.9 us: body(): lax.psum_scatter(grad_down.reshape(shards * core_count, per_shard, rank_s...]
    gather x17 -> x0, local copies, waits for them, and re-layouts: 62.6 us -> none  [the longest x5 32.3 us: body(): outgoing_rows.append(jnp.take(held_blocks, slot_index, axis=0))]
    dot_general x8 -> x0, matrix products: 47 us -> none  [the longest x1 15 us: body(): jnp.dot(flat_rows, full_weight, preferred_element_type=jnp.float32)]
    ppermute x0 -> x26, waiting for transfers between devices: none -> 20.6 us  [the longest x3 12.1 us: flip(): return lax.ppermute(value, 'shard', [(s, s ^ bit) for s in range(shards)])]
    ppermute x0 -> x26, starting transfers between devices: none -> 20.1 us  [the longest x7 9.65 us: around(): return lax.ppermute(value, ALL, ring_pairs)]
    all_to_all x3 -> x0, starting transfers between devices: 14.9 us -> none  [the longest x1 8.55 us: body(): lax.all_to_all(jnp.stack(outgoing_rows), 'dp', split_axis=0, concat_axis=...]
  transfers between devices with their start and end apart: 6 -> 26, of which waited for: 3 -> 7; matrix products, arithmetic and copies ran while one was open for 42% -> 5% of each run, Pallas kernels for 0% -> 50%
where the time goes in v2:
time: 134 us
  Pallas kernels  73.5 us (55%)
  waiting for transfers between devices  20.6 us (15%)
  starting transfers between devices  20.1 us (15%)
  local copies, waits for them, and re-layouts  14.8 us (11%)
  other arithmetic  3.48 us (3%)
    pallas_call x6, Pallas kernels, multiply(): pl.pallas_call(functools.partial(weight_kernel, dims, jobs, first, last,...  43.9 us
    ppermute x3, waiting for transfers between devices, flip(): return lax.ppermute(value, 'shard', [(s, s ^ bit) for s in range(shards)])  12.1 us
    unnamed x36, local copies, waits for them, and re-layouts  11.3 us
    pallas_call x1, Pallas kernels, body(): pl.pallas_call(functools.partial(head_kernel, dims), out_shape=(sds((flat...  10.3 us
    pallas_call x3, Pallas kernels, halve(): pl.pallas_call(functools.partial(halve_kernel, parts, BITS + bit, len(aft...  9.69 us
    ppermute x7, starting transfers between devices, around(): return lax.ppermute(value, ALL, ring_pairs)  9.65 us
    pallas_call x1, Pallas kernels, body(): pl.pallas_call(functools.partial(tail_kernel, dims), out_shape=(sds((flat...  9.52 us
    ppermute x7, waiting for transfers between devices, around(): return lax.ppermute(value, ALL, ring_pairs)  4.28 us
  transfers between devices with their start and end apart: 26, of which 7 were waited for; matrix products, arithmetic and copies ran while one was open for 5% of the time, Pallas kernels for 50%

profile of v2, /device:TPU:0, one launch (start us, length us, event | category | flops | bytes accessed | tf_op | source)
XLA Modules:
  0.0 133.6 jit_solution(872189416428550783)
XLA Ops:
  1.2 2.3 %fusion.2 = (bf16[352,1024]{1,0:T(8,128)(2,1)S(1)}, bf16[352,1024]{1,0:T(8,128)(2,1)}) fusion(bf16[1024,1024]{1,0:T(8,128)(2,1)} %refs_8_.1, s32[]{:T(128)S(6)} %select_n.17), kind=kLoop, calls=%fused_computation.9 | loop fusion | bytes 2883588 | tf_op jit(solution)/shard_map/slice | solution.py:578
  3.5 2.6 %collective-permute-start.3 = (bf16[352,1024]{1,0:T(8,128)(2,1)}, bf16[352,1024]{1,0:T(8,128)(2,1)S(1)}, u32[]{:S(2)}, u32[]{:S(2)}) collective-permute-start(bf16[352,1024]{1,0:T(8,128)(2,1)} %get-tuple-element.75), channel_id=1, source_target_pairs={{0,4},{1,3},{4,8},{5,1},{8,12},{9,5},{12,14},{13,9},{14,10},{15,13... | collective-permute-start | bytes 2162696 | tf_op jit(solution)/shard_map/ppermute | solution.py:560
  6.3 1.5 %collective-permute-start.9 = (bf16[352,1024]{1,0:T(8,128)(2,1)S(1)}, bf16[352,1024]{1,0:T(8,128)(2,1)S(1)}, u32[]{:S(2)}, u32[]{:S(2)}) collective-permute-start(bf16[352,1024]{1,0:T(8,128)(2,1)S(1)} %get-tuple-element.74), channel_id=1, source_target_pairs={{0,4},{1,3},{4,8},{5,1},{8,12},{9,5},{12,14},{13,9},{14,10},{15,13... | collective-permute-start | bytes 2162696 | tf_op jit(solution)/shard_map/ppermute | solution.py:560
  10.0 10.3 %head.1 = (f32[128,4096]{1,0:T(8,128)}, bf16[384,4096]{1,0:T(8,128)(2,1)}, s32[3,3]{1,0:T(4,128)}, bf16[384,1024]{1,0:T(8,128)(2,1)}, bf16[384,128]{1,0:T(8,128)...) custom-call(s32[16]{0:T(128)} %dynamic-slice_bitcast_fusion.info.refs_0_, s32[6]{0:T(128)} %home.1, ...), custom_call_target="tpu_custom_call" | custom-call | flops 7000000 | tf_op jit(solution)/shard_map/head/pallas_call | solution.py:588
  21.2 1.6 %collective-permute-start.6 = (bf16[352,1024]{1,0:T(8,128)(2,1)}, bf16[352,1024]{1,0:T(8,128)(2,1)}, u32[]{:S(2)}, u32[]{:S(2)}) collective-permute-start(bf16[352,1024]{1,0:T(8,128)(2,1)} %gate.8.after.refs_10_), channel_id=1, source_target_pairs={{0,4},{1,3},{4,8},{5,1},{8,12},{9,5},{12,14},{13,9},{14,10},{15,13... | collective-permute-start | bytes 2162696 | tf_op jit(solution)/shard_map/ppermute | solution.py:560
  22.8 1.5 %collective-permute-start.10 = (bf16[352,1024]{1,0:T(8,128)(2,1)}, bf16[352,1024]{1,0:T(8,128)(2,1)}, u32[]{:S(2)}, u32[]{:S(2)}) collective-permute-start(bf16[352,1024]{1,0:T(8,128)(2,1)} %gate.8.after.refs_10_), channel_id=1, source_target_pairs={{0,16},{16,0},{1,17},{17,1},{2,18},{18,2},{3,19},{19,3},{4,20},{20... | collective-permute-start | bytes 2162696 | tf_op jit(solution)/shard_map/ppermute | solution.py:563
  24.8 9.5 %tail.1 = (f32[128,4096]{1,0:T(8,128)}, f32[128,512]{1,0:T(8,128)}, f32[128,512]{1,0:T(8,128)}, bf16[384,4096]{1,0:T(8,128)(2,1)}, bf16[768,128]{1,0:T(8,128)(2,1)}, /*index=5*/bf16[384,128]{1,0:T(8,128)(2,1)}) custom-call(s32[16]{0:T(128)} %dynamic-slice_bitcast_fusion.info.refs_0_, s32[6]{0:T(128)} %adapter.3, s32[8]{0:T(128)} %owner.3, ...), custom_call_target="tpu_custom_call" | custom-call | flops 7000000 | tf_op jit(solution)/shard_map/tail/pallas_call | solution.py:639
  36.3 1.5 %collective-permute-start.11 = (bf16[352,1024]{1,0:T(8,128)(2,1)}, bf16[352,1024]{1,0:T(8,128)(2,1)}, u32[]{:S(2)}, u32[]{:S(2)}) collective-permute-start(bf16[352,1024]{1,0:T(8,128)(2,1)} %gate.9.refs_4_.refs_11_), channel_id=1, source_target_pairs={{0,4},{1,3},{4,8},{5,1},{8,12},{9,5},{12,14},{13,9},{14,10},{15,13... | collective-permute-start | bytes 2162696 | tf_op jit(solution)/shard_map/ppermute | solution.py:560
  37.8 4.1 %halve.3 = (f32[4,16,4608]{2,1,0:T(8,128)}, bf16[4,16,4608]{2,1,0:T(8,128)(2,1)}) custom-call(s32[16]{0:T(128)} %dynamic-slice_bitcast_fusion.info.refs_0_, f32[4,2,16,4096]{3,2,1,0:T(8,128)} %bitcast.32, f32[4,2,16,512]{3,2,1,0:T(8,128)} %bitcast.39, f32[4,2,16,4096]{3,2,1,0:T(8,128)} %bitcast.8.refs_2_, f32[4,2,16,512]{3,2,1,0:T(8,128)} %bitcast.40, ...), custom_call_target="tpu_custom_call" | custom-call | flops 2000000 | tf_op jit(solution)/shard_map/halve/pallas_call | solution.py:677
  43.2 1.4 %collective-permute-start.18 = (bf16[4,16,4608]{2,1,0:T(8,128)(2,1)}, bf16[4,16,4608]{2,1,0:T(8,128)(2,1)}, u32[]{:S(2)}, u32[]{:S(2)}) collective-permute-start(bf16[4,16,4608]{2,1,0:T(8,128)(2,1)} %get-tuple-element.62), channel_id=1, source_target_pairs={{0,2},{2,0},{4,6},{6,4},{8,10},{10,8},{12,14},{14,12},{1,3},{3,1},... | collective-permute-start | bytes 1769480 | tf_op jit(solution)/shard_map/ppermute | solution.py:569
  44.9 6.3 %weights.6 = (bf16[384,8192]{1,0:T(8,128)(2,1)}, f32[384,1024]{1,0:T(8,128)}) custom-call(s32[16]{0:T(128)} %dynamic-slice_bitcast_fusion.info.refs_0_, s32[3,3]{1,0:T(4,128)} %get-tuple-element.39.table.refs_1_, bf16[768,8192]{1,0:T(8,128)(2,1)} %refs_2_.11, bf16[384,4096]{1,0:T(8,128)(2,1)} %collective-permute-done.2.refs_3_, bf16[384,4096]{1,0:T(8,128)(2,1)} %copy-done, ...), custom_call_target="tpu_custom_call" | custom-call | flops 4000000 | tf_op jit(solution)/shard_map/weights/pallas_call | solution.py:713
  51.3 1.8 %collective-permute-start.15 = (bf16[352,1024]{1,0:T(8,128)(2,1)}, bf16[352,1024]{1,0:T(8,128)(2,1)S(1)}, u32[]{:S(2)}, u32[]{:S(2)}) collective-permute-start(bf16[352,1024]{1,0:T(8,128)(2,1)} %gate.11.refs_13_.refs_11_), channel_id=1, source_target_pairs={{0,4},{1,3},{4,8},{5,1},{8,12},{9,5},{12,14},{13,9},{14,10},{15,13... | collective-permute-start | bytes 2162696 | tf_op jit(solution)/shard_map/ppermute | solution.py:560
  53.0 6.3 %weights.7 = (bf16[384,8192]{1,0:T(8,128)(2,1)}, f32[384,1024]{1,0:T(8,128)}, bf16[1024,1024]{1,0:T(8,128)(2,1)}) custom-call(s32[16]{0:T(128)} %dynamic-slice_bitcast_fusion.info.refs_0_, s32[3,3]{1,0:T(4,128)} %get-tuple-element.39.table.refs_1_, bf16[768,8192]{1,0:T(8,128)(2,1)} %refs_2_.11, ...), custom_call_target="tpu_custom_call", output_to_operand_aliasing={{0}: (9, {})} | custom-call | flops 4000000 | tf_op jit(solution)/shard_map/weights/pallas_call | solution.py:713
  59.4 2.5 %collective-permute-done.14.refs_0_ = bf16[352,1024]{1,0:T(8,128)(2,1)} collective-permute-done((bf16[352,1024]{1,0:T(8,128)(2,1)}, bf16[352,1024]{1,0:T(8,128)(2,1)}, u32[]{:S(2)}, u32[]{:S(2)}) %collective-permute-start.14) | collective-permute-done | bytes 720928 | tf_op jit(solution)/shard_map/ppermute | solution.py:560
  65.1 8.8 %weights.8 = (bf16[384,8192]{1,0:T(8,128)(2,1)}, f32[384,1024]{1,0:T(8,128)}, bf16[1024,1024]{1,0:T(8,128)(2,1)}) custom-call(s32[16]{0:T(128)} %dynamic-slice_bitcast_fusion.info.refs_0_, s32[3,3]{1,0:T(4,128)} %get-tuple-element.39.table.refs_1_, bf16[768,8192]{1,0:T(8,128)(2,1)} %refs_2_.11, ...), custom_call_target="tpu_custom_call", output_to_operand_aliasing={{0}: (9, {})} | custom-call | flops 7000000 | tf_op jit(solution)/shard_map/weights/pallas_call | solution.py:713
  74.1 1.7 %collective-permute-done.15.refs_0_ = bf16[352,1024]{1,0:T(8,128)(2,1)S(1)} collective-permute-done((bf16[352,1024]{1,0:T(8,128)(2,1)}, bf16[352,1024]{1,0:T(8,128)(2,1)S(1)}, u32[]{:S(2)}, u32[]{:S(2)}) %collective-permute-start.15) | collective-permute-done | bytes 720928 | tf_op jit(solution)/shard_map/ppermute | solution.py:560
  78.0 2.9 %halve.4 = (f32[2,16,4608]{2,1,0:T(8,128)}, bf16[2,16,4608]{2,1,0:T(8,128)(2,1)}) custom-call(s32[16]{0:T(128)} %dynamic-slice_bitcast_fusion.info.refs_0_, f32[2,2,16,4608]{3,2,1,0:T(8,128)} %bitcast.33, bf16[2,2,16,4608]{3,2,1,0:T(8,128)(2,1)} %bitcast.11.refs_1_, bf16[352,1024]{1,0:T(8,128)(2,1)} %gate.13.refs_2_.refs_11_.refs_14_), custom_call_target="tpu_custom_call" | custom-call | flops 2000000 | tf_op jit(solution)/shard_map/halve/pallas_call | solution.py:677
  81.1 12.1 %collective-permute-done.21 = bf16[2,16,4608]{2,1,0:T(8,128)(2,1)S(1)} collective-permute-done((bf16[2,16,4608]{2,1,0:T(8,128)(2,1)}, bf16[2,16,4608]{2,1,0:T(8,128)(2,1)S(1)}, u32[]{:S(2)}, u32[]{:S(2)}) %collective-permute-start.21) | collective-permute-done | bytes 294944 | tf_op jit(solution)/shard_map/ppermute | solution.py:569
  93.9 2.6 %halve.5 = (f32[1,16,4608]{2,1,0:T(8,128)}, bf16[1,16,4608]{2,1,0:T(8,128)(2,1)}) custom-call(s32[16]{0:T(128)} %dynamic-slice_bitcast_fusion.info.refs_0_, f32[1,2,16,4608]{3,2,1,0:T(8,128)} %bitcast.31, bf16[1,2,16,4608]{3,2,1,0:T(8,128)(2,1)} %bitcast.38), custom_call_target="tpu_custom_call" | custom-call | flops 2000000 | tf_op jit(solution)/shard_map/halve/pallas_call | solution.py:677
  99.1 8.8 %weights.9 = (bf16[384,8192]{1,0:T(8,128)(2,1)}, f32[384,1024]{1,0:T(8,128)}, bf16[1024,1024]{1,0:T(8,128)(2,1)}) custom-call(s32[16]{0:T(128)} %dynamic-slice_bitcast_fusion.info.refs_0_, s32[3,3]{1,0:T(4,128)} %get-tuple-element.39.table.refs_1_, bf16[768,8192]{1,0:T(8,128)(2,1)} %refs_2_.11, ...), custom_call_target="tpu_custom_call", output_to_operand_aliasing={{0}: (9, {})} | custom-call | flops 7000000 | tf_op jit(solution)/shard_map/weights/pallas_call | solution.py:713
  109.7 2.4 %collective-permute-start.23 = (bf16[352,1024]{1,0:T(8,128)(2,1)}, bf16[352,1024]{1,0:T(8,128)(2,1)}, u32[]{:S(2)}, u32[]{:S(2)}) collective-permute-start(bf16[352,1024]{1,0:T(8,128)(2,1)} %gate.14.refs_11_.refs_13_.refs_14_), channel_id=1, source_target_pairs={{0,16},{2,18},{4,20},{6,22},{8,24},{10,26},{12,28},{14,30},{16,0},... | collective-permute-start | bytes 2162696 | tf_op jit(solution)/shard_map/ppermute | solution.py:783
  114.5 6.8 %weights.10 = (bf16[384,8192]{1,0:T(8,128)(2,1)}, f32[384,1024]{1,0:T(8,128)}) custom-call(s32[16]{0:T(128)} %dynamic-slice_bitcast_fusion.info.refs_0_, s32[3,3]{1,0:T(4,128)} %get-tuple-element.39.table.refs_1_, bf16[768,8192]{1,0:T(8,128)(2,1)} %refs_2_.11, bf16[384,4096]{1,0:T(8,128)(2,1)} %collective-permute-done.2.refs_3_, ...), custom_call_target="tpu_custom_call", output_to_operand_aliasing={{0}: (9, {})} | custom-call | flops 4000000 | tf_op jit(solution)/shard_map/weights/pallas_call | solution.py:713
  121.4 1.8 %collective-permute-done.23.refs_0_ = bf16[352,1024]{1,0:T(8,128)(2,1)} collective-permute-done((bf16[352,1024]{1,0:T(8,128)(2,1)}, bf16[352,1024]{1,0:T(8,128)(2,1)}, u32[]{:S(2)}, u32[]{:S(2)}) %collective-permute-start.23) | collective-permute-done | bytes 720928 | tf_op jit(solution)/shard_map/ppermute | solution.py:783
  126.6 6.8 %weights.11 = (bf16[384,8192]{1,0:T(8,128)(2,1)}, bf16[384,1024]{1,0:T(8,128)(2,1)}) custom-call(s32[16]{0:T(128)} %dynamic-slice_bitcast_fusion.info.refs_0_, s32[3,3]{1,0:T(4,128)} %get-tuple-element.39.table.refs_1_, bf16[768,8192]{1,0:T(8,128)(2,1)} %refs_2_.11, ...), custom_call_target="tpu_custom_call", output_to_operand_aliasing={{0}: (12, {})} | custom-call | flops 4000000 | tf_op jit(solution)/shard_map/weights/pallas_call | solution.py:713
  (90 shorter events, 24.3 us)
Async XLA Ops:
  0.7 8.4 %collective-permute-start.1 = (bf16[384,1024]{1,0:T(8,128)(2,1)}, bf16[384,1024]{1,0:T(8,128)(2,1)S(1)}, u32[]{:S(2)}, u32[]{:S(2)}) collective-permute-start(bf16[384,1024]{1,0:T(8,128)(2,1)} %grad.1), channel_id=1, source_target_pairs={{0,1},{1,0},{2,3},{3,2},{4,5},{5,4},{6,7},{7,6},{8,9},{9,8},{10,11... | collective-permute-start | bytes 2359304 | tf_op jit(solution)/shard_map/ppermute | solution.py:566
  3.5 16.9 %collective-permute-start.3 = (bf16[352,1024]{1,0:T(8,128)(2,1)}, bf16[352,1024]{1,0:T(8,128)(2,1)S(1)}, u32[]{:S(2)}, u32[]{:S(2)}) collective-permute-start(bf16[352,1024]{1,0:T(8,128)(2,1)} %get-tuple-element.75), channel_id=1, source_target_pairs={{0,4},{1,3},{4,8},{5,1},{8,12},{9,5},{12,14},{13,9},{14,10},{15,13... | collective-permute-start | bytes 2162696 | tf_op jit(solution)/shard_map/ppermute | solution.py:560
  6.1 3.0 %collective-permute-start = (s32[3,6]{1,0:T(4,128)S(1)}, s32[3,6]{1,0:T(4,128)S(1)}, u32[]{:S(2)}, u32[]{:S(2)}) collective-permute-start(s32[3,6]{1,0:T(4,128)S(1)} %pad_add_fusion), channel_id=1, source_target_pairs={{0,1},{1,0},{2,3},{3,2},{4,5},{5,4},{6,7},{7,6},{8,9},{9,8},{10,11... | collective-permute-start | bytes 224 | tf_op jit(solution)/shard_map/ppermute | solution.py:566
  6.3 28.0 %collective-permute-start.9 = (bf16[352,1024]{1,0:T(8,128)(2,1)S(1)}, bf16[352,1024]{1,0:T(8,128)(2,1)S(1)}, u32[]{:S(2)}, u32[]{:S(2)}) collective-permute-start(bf16[352,1024]{1,0:T(8,128)(2,1)S(1)} %get-tuple-element.74), channel_id=1, source_target_pairs={{0,4},{1,3},{4,8},{5,1},{8,12},{9,5},{12,14},{13,9},{14,10},{15,13... | collective-permute-start | bytes 2162696 | tf_op jit(solution)/shard_map/ppermute | solution.py:560
  21.2 20.7 %collective-permute-start.6 = (bf16[352,1024]{1,0:T(8,128)(2,1)}, bf16[352,1024]{1,0:T(8,128)(2,1)}, u32[]{:S(2)}, u32[]{:S(2)}) collective-permute-start(bf16[352,1024]{1,0:T(8,128)(2,1)} %gate.8.after.refs_10_), channel_id=1, source_target_pairs={{0,4},{1,3},{4,8},{5,1},{8,12},{9,5},{12,14},{13,9},{14,10},{15,13... | collective-permute-start | bytes 2162696 | tf_op jit(solution)/shard_map/ppermute | solution.py:560
  22.8 30.2 %collective-permute-start.10 = (bf16[352,1024]{1,0:T(8,128)(2,1)}, bf16[352,1024]{1,0:T(8,128)(2,1)}, u32[]{:S(2)}, u32[]{:S(2)}) collective-permute-start(bf16[352,1024]{1,0:T(8,128)(2,1)} %gate.8.after.refs_10_), channel_id=1, source_target_pairs={{0,16},{16,0},{1,17},{17,1},{2,18},{18,2},{3,19},{19,3},{4,20},{20... | collective-permute-start | bytes 2162696 | tf_op jit(solution)/shard_map/ppermute | solution.py:563
  24.3 18.3 %collective-permute-start.2 = (bf16[384,4096]{1,0:T(8,128)(2,1)}, bf16[384,4096]{1,0:T(8,128)(2,1)}, u32[]{:S(2)}, u32[]{:S(2)}) collective-permute-start(bf16[384,4096]{1,0:T(8,128)(2,1)} %get-tuple-element.40), channel_id=1, source_target_pairs={{0,1},{1,0},{2,3},{3,2},{4,5},{5,4},{6,7},{7,6},{8,9},{9,8},{10,11... | collective-permute-start | bytes 9437192 | tf_op jit(solution)/shard_map/ppermute | solution.py:566
  24.3 12.0 %collective-permute-start.7 = (f32[128,4096]{1,0:T(8,128)}, f32[128,4096]{1,0:T(8,128)}, u32[]{:S(2)}, u32[]{:S(2)}) collective-permute-start(f32[128,4096]{1,0:T(8,128)} %get-tuple-element.51), channel_id=1, source_target_pairs={{0,1},{1,0},{2,3},{3,2},{4,5},{5,4},{6,7},{7,6},{8,9},{9,8},{10,11... | collective-permute-start | bytes 6291464 | tf_op jit(solution)/shard_map/ppermute | solution.py:566
  36.1 7.1 %collective-permute-start.4 = (bf16[384,4096]{1,0:T(8,128)(2,1)}, bf16[384,4096]{1,0:T(8,128)(2,1)S(1)}, u32[]{:S(2)}, u32[]{:S(2)}) collective-permute-start(bf16[384,4096]{1,0:T(8,128)(2,1)} %get-tuple-element.44), channel_id=1, source_target_pairs={{0,1},{1,0},{2,3},{3,2},{4,5},{5,4},{6,7},{7,6},{8,9},{9,8},{10,11... | collective-permute-start | bytes 9437192 | tf_op jit(solution)/shard_map/ppermute | solution.py:566
  36.3 15.0 %collective-permute-start.11 = (bf16[352,1024]{1,0:T(8,128)(2,1)}, bf16[352,1024]{1,0:T(8,128)(2,1)}, u32[]{:S(2)}, u32[]{:S(2)}) collective-permute-start(bf16[352,1024]{1,0:T(8,128)(2,1)} %gate.9.refs_4_.refs_11_), channel_id=1, source_target_pairs={{0,4},{1,3},{4,8},{5,1},{8,12},{9,5},{12,14},{13,9},{14,10},{15,13... | collective-permute-start | bytes 2162696 | tf_op jit(solution)/shard_map/ppermute | solution.py:560
  42.0 20.5 %collective-permute-start.12 = (bf16[352,1024]{1,0:T(8,128)(2,1)}, bf16[352,1024]{1,0:T(8,128)(2,1)}, u32[]{:S(2)}, u32[]{:S(2)}) collective-permute-start(bf16[352,1024]{1,0:T(8,128)(2,1)} %gate.10.refs_9_.refs_10_), channel_id=1, source_target_pairs={{0,16},{16,0},{1,17},{17,1},{2,18},{18,2},{3,19},{19,3},{4,20},{20... | collective-permute-start | bytes 2162696 | tf_op jit(solution)/shard_map/ppermute | solution.py:563
  42.6 19.4 %collective-permute-start.14 = (bf16[352,1024]{1,0:T(8,128)(2,1)}, bf16[352,1024]{1,0:T(8,128)(2,1)}, u32[]{:S(2)}, u32[]{:S(2)}) collective-permute-start(bf16[352,1024]{1,0:T(8,128)(2,1)} %gate.10.refs_9_.refs_10_), channel_id=1, source_target_pairs={{0,4},{1,3},{4,8},{5,1},{8,12},{9,5},{12,14},{13,9},{14,10},{15,13... | collective-permute-start | bytes 2162696 | tf_op jit(solution)/shard_map/ppermute | solution.py:560
  43.2 34.8 %collective-permute-start.18 = (bf16[4,16,4608]{2,1,0:T(8,128)(2,1)}, bf16[4,16,4608]{2,1,0:T(8,128)(2,1)}, u32[]{:S(2)}, u32[]{:S(2)}) collective-permute-start(bf16[4,16,4608]{2,1,0:T(8,128)(2,1)} %get-tuple-element.62), channel_id=1, source_target_pairs={{0,2},{2,0},{4,6},{6,4},{8,10},{10,8},{12,14},{14,12},{1,3},{3,1},... | collective-permute-start | bytes 1769480 | tf_op jit(solution)/shard_map/ppermute | solution.py:569
  51.3 24.6 %collective-permute-start.15 = (bf16[352,1024]{1,0:T(8,128)(2,1)}, bf16[352,1024]{1,0:T(8,128)(2,1)S(1)}, u32[]{:S(2)}, u32[]{:S(2)}) collective-permute-start(bf16[352,1024]{1,0:T(8,128)(2,1)} %gate.11.refs_13_.refs_11_), channel_id=1, source_target_pairs={{0,4},{1,3},{4,8},{5,1},{8,12},{9,5},{12,14},{13,9},{14,10},{15,13... | collective-permute-start | bytes 2162696 | tf_op jit(solution)/shard_map/ppermute | solution.py:560
  59.3 4.4 %collective-permute-start.13 = (bf16[1024,1024]{1,0:T(8,128)(2,1)}, bf16[1024,1024]{1,0:T(8,128)(2,1)S(1)}, u32[]{:S(2)}, u32[]{:S(2)}) collective-permute-start(bf16[1024,1024]{1,0:T(8,128)(2,1)} %get-tuple-element.58), channel_id=1, source_target_pairs={{0,1},{1,0},{2,3},{3,2},{4,5},{5,4},{6,7},{7,6},{8,9},{9,8},{10,11... | collective-permute-start | bytes 6291464 | tf_op jit(solution)/shard_map/ppermute | solution.py:566
  61.9 35.9 %collective-permute-start.16 = (bf16[352,1024]{1,0:T(8,128)(2,1)}, bf16[352,1024]{1,0:T(8,128)(2,1)}, u32[]{:S(2)}, u32[]{:S(2)}) collective-permute-start(bf16[352,1024]{1,0:T(8,128)(2,1)} %gate.12.refs_14_.refs_10_), channel_id=1, source_target_pairs={{0,16},{16,0},{1,17},{17,1},{2,18},{18,2},{3,19},{19,3},{4,20},{20... | collective-permute-start | bytes 2162696 | tf_op jit(solution)/shard_map/ppermute | solution.py:563
  73.9 23.9 %collective-permute-start.17 = (bf16[1024,1024]{1,0:T(8,128)(2,1)}, bf16[1024,1024]{1,0:T(8,128)(2,1)S(1)}, u32[]{:S(2)}, u32[]{:S(2)}) collective-permute-start(bf16[1024,1024]{1,0:T(8,128)(2,1)} %get-tuple-element.61), channel_id=1, source_target_pairs={{0,1},{1,0},{2,3},{3,2},{4,5},{5,4},{6,7},{7,6},{8,9},{9,8},{10,11... | collective-permute-start | bytes 6291464 | tf_op jit(solution)/shard_map/ppermute | solution.py:566
  77.9 30.9 %collective-permute-start.20 = (bf16[352,1024]{1,0:T(8,128)(2,1)S(1)}, bf16[352,1024]{1,0:T(8,128)(2,1)S(1)}, u32[]{:S(2)}, u32[]{:S(2)}) collective-permute-start(bf16[352,1024]{1,0:T(8,128)(2,1)S(1)} %broadcast_select_fusion), channel_id=1, source_target_pairs={{0,4},{1,3},{4,8},{5,1},{8,12},{9,5},{12,14},{13,9},{14,10},{15,13... | collective-permute-start | bytes 2162696 | tf_op jit(solution)/shard_map/ppermute | solution.py:560
  80.9 12.3 %collective-permute-start.21 = (bf16[2,16,4608]{2,1,0:T(8,128)(2,1)}, bf16[2,16,4608]{2,1,0:T(8,128)(2,1)S(1)}, u32[]{:S(2)}, u32[]{:S(2)}) collective-permute-start(bf16[2,16,4608]{2,1,0:T(8,128)(2,1)} %get-tuple-element.67), channel_id=1, source_target_pairs={{0,4},{2,6},{4,0},{6,2},{8,12},{10,14},{12,8},{14,10},{1,5},{3,7},... | collective-permute-start | bytes 884744 | tf_op jit(solution)/shard_map/ppermute | solution.py:569
  81.0 44.5 %collective-permute-start.5 = (bf16[384,128]{1,0:T(8,128)(2,1)}, bf16[384,128]{1,0:T(8,128)(2,1)}, u32[]{:S(2)}, u32[]{:S(2)}) collective-permute-start(bf16[384,128]{1,0:T(8,128)(2,1)} %get-tuple-element.48), channel_id=1, source_target_pairs={{0,1},{1,0},{2,3},{3,2},{4,5},{5,4},{6,7},{7,6},{8,9},{9,8},{10,11... | collective-permute-start | bytes 294920 | tf_op jit(solution)/shard_map/ppermute | solution.py:566
  96.6 15.6 %collective-permute-start.25 = (bf16[1,16,4608]{2,1,0:T(8,128)(2,1)}, bf16[1,16,4608]{2,1,0:T(8,128)(2,1)}, u32[]{:S(2)}, u32[]{:S(2)}) collective-permute-start(bf16[1,16,4608]{2,1,0:T(8,128)(2,1)} %get-tuple-element.68.refs_2_), channel_id=1, source_target_pairs={{0,8},{2,10},{4,12},{6,14},{8,0},{10,2},{12,4},{14,6},{1,9},{3,11}... | collective-permute-start | bytes 442376 | tf_op jit(solution)/shard_map/ppermute | solution.py:569
  107.9 5.2 %collective-permute-start.19 = (bf16[1024,1024]{1,0:T(8,128)(2,1)}, bf16[1024,1024]{1,0:T(8,128)(2,1)S(1)}, u32[]{:S(2)}, u32[]{:S(2)}) collective-permute-start(bf16[1024,1024]{1,0:T(8,128)(2,1)} %get-tuple-element.66), channel_id=1, source_target_pairs={{0,1},{1,0},{2,3},{3,2},{4,5},{5,4},{6,7},{7,6},{8,9},{9,8},{10,11... | collective-permute-start | bytes 6291464 | tf_op jit(solution)/shard_map/ppermute | solution.py:566
  109.7 13.5 %collective-permute-start.23 = (bf16[352,1024]{1,0:T(8,128)(2,1)}, bf16[352,1024]{1,0:T(8,128)(2,1)}, u32[]{:S(2)}, u32[]{:S(2)}) collective-permute-start(bf16[352,1024]{1,0:T(8,128)(2,1)} %gate.14.refs_11_.refs_13_.refs_14_), channel_id=1, source_target_pairs={{0,16},{2,18},{4,20},{6,22},{8,24},{10,26},{12,28},{14,30},{16,0},... | collective-permute-start | bytes 2162696 | tf_op jit(solution)/shard_map/ppermute | solution.py:783
  113.1 12.4 %collective-permute-start.22 = (bf16[352,1024]{1,0:T(8,128)(2,1)}, bf16[352,1024]{1,0:T(8,128)(2,1)S(1)}, u32[]{:S(2)}, u32[]{:S(2)}) collective-permute-start(bf16[352,1024]{1,0:T(8,128)(2,1)} %gate.14.refs_11_.refs_13_.refs_14_), channel_id=1, source_target_pairs={{0,1},{1,0},{2,3},{3,2},{4,5},{5,4},{6,7},{7,6},{8,9},{9,8},{10,11... | collective-permute-start | bytes 2162696 | tf_op jit(solution)/shard_map/ppermute | solution.py:566
  (20 other events, 36.4 us)

commit v3 on v2

--- a/solution.py
+++ b/solution.py
@@ -11,7 +11,7 @@
 adapter_scale = 2.0
 ALL = ("group", "shard", "dp")
 NT = (((1,), (1,)), ((), ()))
-VMEM_LIMIT = 60 << 20
+VMEM_LIMIT = 63 << 20
 COST = 1e6
 GATE = 1e5
 ANY = pl.BlockSpec(memory_space=pl.ANY)
@@ -302,6 +302,27 @@
         out.wait()
 
 
+def final_kernel(sums, moved, after, own_down, own_up, sums_v, moved_v, sem):
+    loads = [
+        pltpu.make_async_copy(sums, sums_v, sem.at[0]),
+        pltpu.make_async_copy(moved, moved_v, sem.at[1]),
+    ]
+    for copy in loads:
+        copy.start()
+    for copy in loads:
+        copy.wait()
+    sums_v[...] += moved_v[...].astype(jnp.float32)
+    cut = own_down.shape[1]
+    outs = [
+        pltpu.make_async_copy(sums_v.at[:, pl.ds(0, cut)], own_down, sem.at[2]),
+        pltpu.make_async_copy(sums_v.at[:, pl.ds(cut, own_up.shape[1])], own_up, sem.at[3]),
+    ]
+    for copy in outs:
+        copy.start()
+    for copy in outs:
+        copy.wait()
+
+
 def weight_kernel(dims, jobs, first, last, through, after, *refs):
     slots, tokens, blk, shards, cols, rank, adapters, width = dims
     refs = list(refs)
@@ -323,7 +344,7 @@
     take(through)
     mask_v, back_v, up_v, low_v, acc_v, final_v = take(6)
     per_job = take(4 * len(jobs))
-    sem, row_sem, piece_sem, out_sem, low_sem = refs
+    sem, row_sem, piece_sem, out_sem, low_sem, tile_sem = refs
     core = info[0]
 
     starts = [
@@ -347,20 +368,25 @@
             source = piece if cut is None else piece.at[pl.ds(*cut), :]
             to = weight_v.at[pl.ds(row, size), :]
             copy = pltpu.make_async_copy(source, to, piece_sem.at[taken])
+            loads.append((copy, only))
+            taken += 1
+        down_in = pltpu.make_async_copy(down.at[:, at], down_v, row_sem.at[n, blk])
+        loads.append((down_in, None))
+        work.append((loads, (at, here, at_half), weight_v, rows_v, down_v, out_v, hand))
+
+    def start_weights(n):
+        for copy, only in work[n][0]:
             if only is None:
                 copy.start()
-                loads.append((copy, None))
             else:
 
                 @pl.when(core == only)
                 def _():
                     copy.start()
 
-                loads.append((copy, only))
-            taken += 1
-        down_in = pltpu.make_async_copy(down.at[:, at], down_v, row_sem.at[n, blk])
-        down_in.start()
-        loads.append((down_in, None))
+    def start_rows(n):
+        at, here, at_half = work[n][1]
+        rows_v = work[n][3]
         row_loads = []
         for w in range(blk):
             to = rows_v.at[pl.ds(w * tokens, tokens), :]
@@ -388,10 +414,9 @@
             row_loads.append(
                 pltpu.make_async_copy(held.at[pl.ds(0, tokens), at], to, row_sem.at[n, w])
             )
-        if n == 0 and not first:
-            acc_load = pltpu.make_async_copy(acc_in, acc_v, sem.at[2])
-            acc_load.start()
-        work.append((loads, row_loads, at, weight_v, rows_v, down_v, out_v, hand))
+        return row_loads
+
+    start_weights(0)
     if last:
         up_in = pltpu.make_async_copy(up, up_v, sem.at[3])
         up_in.start()
@@ -414,7 +439,8 @@
     back_tile = min(256, cols)
     outs = []
     handed_at = 0
-    for n, (loads, row_loads, at, weight_v, rows_v, down_v, out_v, hand) in enumerate(work):
+    for n, (loads, (at, _, _), weight_v, rows_v, down_v, out_v, hand) in enumerate(work):
+        final_job = n + 1 == len(work)
         for copy, only in loads:
             if only is None:
                 copy.wait()
@@ -424,6 +450,12 @@
                 def _():
                     copy.wait()
 
+        row_loads = start_rows(n)
+        if n == 0 and not first:
+            acc_load = pltpu.make_async_copy(acc_in, acc_v, sem.at[2])
+            acc_load.start()
+        if not final_job:
+            start_weights(n + 1)
         if hand:
             out = pltpu.make_async_copy(weight_v, handed[handed_at], out_sem.at[1, n])
             handed_at += 1
@@ -448,6 +480,10 @@
                 acc_v[:, cut] = product
             else:
                 acc_v[:, cut] += product
+            if final_job and not last:
+                out = pltpu.make_async_copy(acc_v.at[:, cut], result.at[:, cut], tile_sem.at[i])
+                out.start()
+                outs.append(out)
     if last:
         up_in.wait()
         for w in range(blk):
@@ -455,13 +491,11 @@
                 low_slots.at[pl.ds(0, tokens), :], low_v.at[pl.ds(w * tokens, tokens), :], low_sem.at[w]
             ).wait()
         final_v[...] = (acc_v[...] + adapter_scale * dot(low_v[...], up_v[...])).astype(jnp.bfloat16)
-        finish = pltpu.make_async_copy(final_v, result, sem.at[4])
-    else:
-        finish = pltpu.make_async_copy(acc_v, result, sem.at[4])
-    finish.start()
+        out = pltpu.make_async_copy(final_v, result, sem.at[4])
+        out.start()
+        outs.append(out)
     for out in outs:
         out.wait()
-    finish.wait()
 
 
 def gate_kernel(*refs):
@@ -475,6 +509,7 @@
         in_specs=[ANY] * (len(values) + len(tokens)),
         out_specs=(ANY,) * len(values),
         input_output_aliases={i: i for i in range(len(values))},
+        compiler_params=pltpu.CompilerParams(vmem_limit_bytes=VMEM_LIMIT),
         cost_estimate=cost(GATE),
         name="gate",
     )(*values, *tokens)
@@ -621,20 +656,17 @@
     sent = swap(send)
     got = swap(packed)
 
-    edges, middles, others = [], [], []
-
     def next_edge(token):
-        value = around(edges[-1]) if edges else edge_rows
-        (value,) = gate([value], [token])
+        (value,) = gate([around(edges[-1])], [token])
         edges.append(value)
         others.append(partner(value))
 
-    def next_middle(token):
-        value = around(middles[-1]) if middles else middle_rows
-        (value,) = gate([value], [token])
+    def next_middle(*tokens):
+        (value,) = gate([around(middles[-1])], tokens)
         middles.append(value)
 
-    next_edge(low_part)
+    edges, middles = (list(pair) for pair in zip(gate([edge_rows, middle_rows], [low_part])))
+    others = [partner(edges[0])]
 
     keep, keep_up, send_up, packed_other, low_slots, low_send = pl.pallas_call(
         functools.partial(tail_kernel, dims),
@@ -663,7 +695,8 @@
         info, block_adapter, adapter_owner, table,
         held_rows, down, mask_slots, back_slots, low_part, edges[0],
     )
-    next_middle(keep_up)
+    if steps > 2:
+        next_edge(keep_up)
     sent_up = swap(send_up)
     low_got = swap(low_send)
     got_other = swap(packed_other)
@@ -729,7 +762,8 @@
                 vmem((flat, cols), bf16),
                 vmem((work_rows, cols), bf16),
             ] * len(jobs)
-            + [dma((5,)), dma((len(jobs), blk + 1)), dma((len(pieces),)), dma((2, len(jobs))), dma((blk,))],
+            + [dma((5,)), dma((len(jobs), blk + 1)), dma((len(pieces),)), dma((2, len(jobs))), dma((blk,))]
+            + [dma((max(1, width // 256),))],
             input_output_aliases=aliases,
             compiler_params=params,
             cost_estimate=cost(us),
@@ -737,52 +771,53 @@
         )(*operands)
         return out[:2], out[2:2 + hands], out[2 + hands:]
 
-    sums, away = halve([keep, keep_up], [sent, sent_up], 0, middles)
+    sums, away = halve([keep, keep_up], [sent, sent_up], 0, edges[1:])
     moved = flip(away, 1)
     bit = 1
     if steps > 2:
-        next_edge(sums)
+        next_middle(sums)
 
     whole = [(EDGE, None, None), (MIDDLE, None, middle_cut), (OTHER, None, None)]
     full = [(None, None, None)]
-    state, _, _ = multiply(
-        (None, None), [(SHARD, full, 0)], [value_weight], after=edges[1:] or [sums], us=4
-    )
-    after = []
-    if steps > 2:
-        next_middle(state[1])
-        after = [middles[-1]]
-    last = None
+    state, after, last = (None, None), middles[1:] or [sums], None
     for k in range(1, steps):
-        jobs = [(MINE + k - 1, whole, 1)]
-        pieces = [edges[k - 1], middles[k - 1], others[k - 1]]
-        if k > 1:
+        jobs, pieces = [], []
+        if k == 1:
+            jobs.append((SHARD, full, 0))
+            pieces.append(value_weight)
+        else:
             jobs.append((THEIRS + k - 2, full, 0))
             pieces.append(handed)
-        state, out, _ = multiply(state, jobs, pieces, after=after, us=4 if k == 1 else 7)
+        mine = [edges[k - 1], middles[k - 1], others[k - 1]]
+        handing = k + 1 < steps
+        jobs.append((MINE + k - 1, whole, int(handing)))
+        pieces += mine
+        if not handing:
+            jobs.append((THEIRS + k - 1, whole, 0))
+            pieces += [swap(part) for part in mine]
+            if last is not None:
+                (last,) = gate([last], after)
+                after = [last]
+                last_sib = swap(last)
+                last_other = lax.ppermute(last, ALL, first_core)
+        state, out, _ = multiply(state, jobs, pieces, after=after, us=7)
         after = []
-        handed = swap(out[0])
-        if len(edges) < steps - 1:
-            next_edge(state[1])
-            after.append(edges[-1])
-            if len(middles) < len(edges) - 1:
-                next_middle(state[1])
+        if handing:
+            handed = swap(out[0])
+            if len(middles) < len(edges):
+                next_middle(state[1], moved)
                 after.append(middles[-1])
-        elif len(middles) < steps - 1:
-            next_middle(state[1])
-            after.append(middles[-1])
-        if len(middles) == steps - 1 and last is None:
-            last = around(jnp.where(core_at == 0, edges[-1], middles[-1]))
-        if k > 1 and bit < bits:
-            sums, away = halve([sums], [moved], bit, after)
+            if len(edges) < steps - 1:
+                next_edge(state[1])
+                after.append(edges[-1])
+            if len(middles) == steps - 1:
+                last = around(jnp.where(core_at == 0, edges[-1], middles[-1]))
+        if (k > 1 or not handing) and bit < bits:
+            sums, away = halve([sums], [moved], bit, after or [state[1]])
             moved = flip(away, 1 << bit)
             after.append(sums)
             bit += 1
-    (last,) = gate([last], [state[1], away])
-    last_sib = swap(last)
-    last_other = lax.ppermute(last, ALL, first_core)
-    state, _, _ = multiply(state, [(THEIRS + steps - 2, full, 0)], [handed], after=[last], us=4)
-    (last_other,) = gate([last_other], [state[1]])
+    (last_other,) = gate([last_other], [state[1], sums])
     other_sib = swap(last_other)
     jobs = [(
         MINE + steps - 1,
@@ -793,10 +828,24 @@
     pieces = [last, last, last_sib, last_sib, last_other, other_sib]
     state, _, _ = multiply(state, jobs, pieces, last=True, us=4)
     input_grad, value_projection_output = state
-    sums = sums.reshape(-1, half)
-    moved = moved.reshape(-1, half).astype(f32)
-    own_down = sums[:, :half_model] + moved[:, :half_model]
-    own_up = sums[:, half_model:] + moved[:, half_model:]
+    while bit < bits:
+        sums, away = halve([sums], [moved], bit)
+        moved = flip(away, 1 << bit)
+        bit += 1
+    own_down, own_up = pl.pallas_call(
+        final_kernel,
+        out_shape=(sds((flat // shards, half_model), f32), sds((flat // shards, half_width), f32)),
+        in_specs=[ANY] * 3,
+        out_specs=(ANY,) * 2,
+        scratch_shapes=[
+            vmem((flat // shards, half), f32),
+            vmem((flat // shards, half), bf16),
+            dma((4,)),
+        ],
+        compiler_params=params,
+        cost_estimate=cost(2),
+        name="final",
+    )(sums.reshape(-1, half), moved.reshape(-1, half), value_projection_output)
 
     per_shard = adapters // shards
     return (

time: 134 us -> 124 us (0.925)
  local copies, waits for them, and re-layouts: 14.8 us -> 6.75 us
  Pallas kernels: 73.5 us -> 67.3 us
  starting transfers between devices: 20.1 us -> 23.8 us
  waiting for transfers between devices: 20.6 us -> 22.7 us
    ppermute x7, waiting for transfers between devices: 4.28 us -> 16.7 us  [around(): return lax.ppermute(value, ALL, ring_pairs)]
    ppermute x3, waiting for transfers between devices: 12.1 us -> 3.08 us  [flip(): return lax.ppermute(value, 'shard', [(s, s ^ bit) for s in range(shards)])]
    unnamed x36 -> x24, local copies, waits for them, and re-layouts: 11.3 us -> 3 us
    pallas_call x6 -> x4, Pallas kernels: 43.9 us -> 36 us  [multiply(): pl.pallas_call(functools.partial(weight_kernel, dims, jobs, first, last,...]
    ppermute x1, waiting for transfers between devices: 1.79 us -> 0.01 us  [body(): last_other = lax.ppermute(last, ALL, first_core)]
    pallas_call x0 -> x1, Pallas kernels: none -> 1.76 us  [body(): pl.pallas_call(final_kernel, out_shape=(sds((flat // shards, half_model),...]
    reshape x2 -> x0, other arithmetic: 1.35 us -> none  [the longest x1 0.73 us: body(): own_down.reshape(per_shard, rank, -1)]
    ppermute x12 -> x14, waiting for transfers between devices: 2.36 us -> 2.91 us  [swap(): return lax.ppermute(value, 'dp', [(0, 1), (1, 0)])]
  transfers between devices with their start and end apart: 26 -> 28, of which waited for: 7 -> 6; matrix products, arithmetic and copies ran while one was open for 5% -> 5% of each run, Pallas kernels for 50% -> 53%
where the time goes in v3:
time: 124 us
  Pallas kernels  67.3 us (54%)
  starting transfers between devices  23.8 us (19%)
  waiting for transfers between devices  22.7 us (18%)
  local copies, waits for them, and re-layouts  6.75 us (5%)
  other arithmetic  2.2 us (2%)
    pallas_call x4, Pallas kernels, multiply(): pl.pallas_call(functools.partial(weight_kernel, dims, jobs, first, last,...  36 us
    ppermute x7, waiting for transfers between devices, around(): return lax.ppermute(value, ALL, ring_pairs)  16.7 us
    ppermute x7, starting transfers between devices, around(): return lax.ppermute(value, ALL, ring_pairs)  11 us
    pallas_call x1, Pallas kernels, body(): pl.pallas_call(functools.partial(head_kernel, dims), out_shape=(sds((flat...  10.4 us
    pallas_call x3, Pallas kernels, halve(): pl.pallas_call(functools.partial(halve_kernel, parts, BITS + bit, len(aft...  9.67 us
    pallas_call x1, Pallas kernels, body(): pl.pallas_call(functools.partial(tail_kernel, dims), out_shape=(sds((flat...  9.53 us
    ppermute x1, starting transfers between devices, body(): last_other = lax.ppermute(last, ALL, first_core)  3.61 us
    ppermute x3, starting transfers between devices, partner(): return lax.ppermute(value, 'group', [(g, g ^ 1) for g in range(groups)])  3.52 us
  transfers between devices with their start and end apart: 28, of which 6 were waited for; matrix products, arithmetic and copies ran while one was open for 5% of the time, Pallas kernels for 53%

profile of v3, /device:TPU:0, one launch (start us, length us, event | category | flops | bytes accessed | tf_op | source)
XLA Modules:
  0.0 123.8 jit_solution(1979718219471465079)
XLA Ops:
  1.2 2.5 %fusion = (bf16[352,1024]{1,0:T(8,128)(2,1)}, bf16[352,1024]{1,0:T(8,128)(2,1)}) fusion(bf16[1024,1024]{1,0:T(8,128)(2,1)} %refs_8_.1, s32[]{:T(128)S(6)} %select_n.17), kind=kLoop, calls=%fused_computation.4 | loop fusion | bytes 2883588 | tf_op jit(solution)/shard_map/slice | solution.py:613
  3.7 2.6 %collective-permute-start.3 = (bf16[352,1024]{1,0:T(8,128)(2,1)}, bf16[352,1024]{1,0:T(8,128)(2,1)S(1)}, u32[]{:S(2)}, u32[]{:S(2)}) collective-permute-start(bf16[352,1024]{1,0:T(8,128)(2,1)} %get-tuple-element.73), channel_id=1, source_target_pairs={{0,4},{1,3},{4,8},{5,1},{8,12},{9,5},{12,14},{13,9},{14,10},{15,13... | collective-permute-start | bytes 2162696 | tf_op jit(solution)/shard_map/ppermute | solution.py:595
  6.3 1.6 %collective-permute-start.4 = (bf16[352,1024]{1,0:T(8,128)(2,1)}, bf16[352,1024]{1,0:T(8,128)(2,1)}, u32[]{:S(2)}, u32[]{:S(2)}) collective-permute-start(bf16[352,1024]{1,0:T(8,128)(2,1)} %get-tuple-element.72), channel_id=1, source_target_pairs={{0,4},{1,3},{4,8},{5,1},{8,12},{9,5},{12,14},{13,9},{14,10},{15,13... | collective-permute-start | bytes 2162696 | tf_op jit(solution)/shard_map/ppermute | solution.py:595
  9.8 10.4 %head.1 = (f32[128,4096]{1,0:T(8,128)}, bf16[384,4096]{1,0:T(8,128)(2,1)}, s32[3,3]{1,0:T(4,128)}, bf16[384,1024]{1,0:T(8,128)(2,1)}, bf16[384,128]{1,0:T(8,128)...) custom-call(s32[16]{0:T(128)} %dynamic-slice_bitcast_fusion.info.refs_0_, s32[6]{0:T(128)} %home.1, ...), custom_call_target="tpu_custom_call" | custom-call | flops 7000000 | tf_op jit(solution)/shard_map/head/pallas_call | solution.py:623
  20.2 3.4 %collective-permute-done.4.refs_1_ = bf16[352,1024]{1,0:T(8,128)(2,1)} collective-permute-done((bf16[352,1024]{1,0:T(8,128)(2,1)}, bf16[352,1024]{1,0:T(8,128)(2,1)}, u32[]{:S(2)}, u32[]{:S(2)}) %collective-permute-start.4) | collective-permute-done | bytes 720928 | tf_op jit(solution)/shard_map/ppermute | solution.py:595
  23.6 2.1 %collective-permute-start.11 = (bf16[352,1024]{1,0:T(8,128)(2,1)}, bf16[352,1024]{1,0:T(8,128)(2,1)}, u32[]{:S(2)}, u32[]{:S(2)}) collective-permute-start(bf16[352,1024]{1,0:T(8,128)(2,1)} %get-tuple-element.43.after.refs_9_), channel_id=1, source_target_pairs={{0,4},{1,3},{4,8},{5,1},{8,12},{9,5},{12,14},{13,9},{14,10},{15,13... | collective-permute-start | bytes 2162696 | tf_op jit(solution)/shard_map/ppermute | solution.py:595
  27.1 1.6 %collective-permute-start.8 = (bf16[352,1024]{1,0:T(8,128)(2,1)}, bf16[352,1024]{1,0:T(8,128)(2,1)S(1)}, u32[]{:S(2)}, u32[]{:S(2)}) collective-permute-start(bf16[352,1024]{1,0:T(8,128)(2,1)} %get-tuple-element.49.refs_10_), channel_id=1, source_target_pairs={{0,4},{1,3},{4,8},{5,1},{8,12},{9,5},{12,14},{13,9},{14,10},{15,13... | collective-permute-start | bytes 2162696 | tf_op jit(solution)/shard_map/ppermute | solution.py:595
  28.7 9.5 %tail.1 = (f32[128,4096]{1,0:T(8,128)}, f32[128,512]{1,0:T(8,128)}, f32[128,512]{1,0:T(8,128)}, bf16[384,4096]{1,0:T(8,128)(2,1)}, bf16[768,128]{1,0:T(8,128)(2,1)}, /*index=5*/bf16[384,128]{1,0:T(8,128)(2,1)}) custom-call(s32[16]{0:T(128)} %dynamic-slice_bitcast_fusion.info.refs_0_, s32[6]{0:T(128)} %adapter.3, s32[8]{0:T(128)} %owner.3, ...), custom_call_target="tpu_custom_call" | custom-call | flops 7000000 | tf_op jit(solution)/shard_map/tail/pallas_call | solution.py:671
  41.1 4.1 %halve.3 = (f32[4,16,4608]{2,1,0:T(8,128)}, bf16[4,16,4608]{2,1,0:T(8,128)(2,1)}) custom-call(s32[16]{0:T(128)} %dynamic-slice_bitcast_fusion.info.refs_0_, f32[4,2,16,4096]{3,2,1,0:T(8,128)} %bitcast.25, f32[4,2,16,512]{3,2,1,0:T(8,128)} %bitcast.31, f32[4,2,16,4096]{3,2,1,0:T(8,128)} %bitcast.8.refs_2_, f32[4,2,16,512]{3,2,1,0:T(8,128)} %bitcast.32, ...), custom_call_target="tpu_custom_call" | custom-call | flops 2000000 | tf_op jit(solution)/shard_map/halve/pallas_call | solution.py:710
  45.3 1.6 %collective-permute-start.14 = (bf16[352,1024]{1,0:T(8,128)(2,1)}, bf16[352,1024]{1,0:T(8,128)(2,1)}, u32[]{:S(2)}, u32[]{:S(2)}) collective-permute-start(bf16[352,1024]{1,0:T(8,128)(2,1)} %gate.8.refs_4_.refs_11_), channel_id=1, source_target_pairs={{0,4},{1,3},{4,8},{5,1},{8,12},{9,5},{12,14},{13,9},{14,10},{15,13... | collective-permute-start | bytes 2162696 | tf_op jit(solution)/shard_map/ppermute | solution.py:595
  46.9 1.5 %collective-permute-start.16 = (bf16[352,1024]{1,0:T(8,128)(2,1)}, bf16[352,1024]{1,0:T(8,128)(2,1)S(1)}, u32[]{:S(2)}, u32[]{:S(2)}) collective-permute-start(bf16[352,1024]{1,0:T(8,128)(2,1)} %gate.9.refs_12_), channel_id=1, source_target_pairs={{0,4},{1,3},{4,8},{5,1},{8,12},{9,5},{12,14},{13,9},{14,10},{15,13... | collective-permute-start | bytes 2162696 | tf_op jit(solution)/shard_map/ppermute | solution.py:595
  48.9 8.5 %weights.4 = (bf16[384,8192]{1,0:T(8,128)(2,1)}, f32[384,1024]{1,0:T(8,128)}, bf16[1024,1024]{1,0:T(8,128)(2,1)}) custom-call(s32[16]{0:T(128)} %dynamic-slice_bitcast_fusion.info.refs_0_, s32[3,3]{1,0:T(4,128)} %get-tuple-element.38.table.refs_1_, bf16[768,8192]{1,0:T(8,128)(2,1)} %refs_2_.7, bf16[384,4096]{1,0:T(8,128)(2,1)} %collective-permute-done.2.refs_3_, ...), custom_call_target="tpu_custom_call" | custom-call | flops 7000000 | tf_op jit(solution)/shard_map/weights/pallas_call | solution.py:746
  57.6 5.7 %collective-permute-done.14.refs_0_ = bf16[352,1024]{1,0:T(8,128)(2,1)} collective-permute-done((bf16[352,1024]{1,0:T(8,128)(2,1)}, bf16[352,1024]{1,0:T(8,128)(2,1)}, u32[]{:S(2)}, u32[]{:S(2)}) %collective-permute-start.14) | collective-permute-done | bytes 720928 | tf_op jit(solution)/shard_map/ppermute | solution.py:595
  64.8 9.5 %weights.5 = (bf16[384,8192]{1,0:T(8,128)(2,1)}, f32[384,1024]{1,0:T(8,128)}, bf16[1024,1024]{1,0:T(8,128)(2,1)}) custom-call(s32[16]{0:T(128)} %dynamic-slice_bitcast_fusion.info.refs_0_, s32[3,3]{1,0:T(4,128)} %get-tuple-element.38.table.refs_1_, bf16[768,8192]{1,0:T(8,128)(2,1)} %refs_2_.7, ...), custom_call_target="tpu_custom_call", output_to_operand_aliasing={{0}: (9, {})} | custom-call | flops 7000000 | tf_op jit(solution)/shard_map/weights/pallas_call | solution.py:746
  74.2 3.1 %collective-permute-done.17.refs_2_ = bf16[4,16,4608]{2,1,0:T(8,128)(2,1)} collective-permute-done((bf16[4,16,4608]{2,1,0:T(8,128)(2,1)}, bf16[4,16,4608]{2,1,0:T(8,128)(2,1)}, u32[]{:S(2)}, u32[]{:S(2)}) %collective-permute-start.17) | collective-permute-done | bytes 589856 | tf_op jit(solution)/shard_map/ppermute | solution.py:604
  78.2 2.2 %broadcast_select_fusion = bf16[352,1024]{1,0:T(8,128)(2,1)} fusion(bf16[352,1024]{1,0:T(8,128)(2,1)} %gate.10.refs_14_.refs_11_, bf16[352,1024]{1,0:T(8,128)(2,1)} %gate.11.refs_2_.refs_1_.refs_12_, pred[]{:T(512)S(6)} %eq.7), kind=kLoop, calls=%fused_computation | loop fusion | flops 360448 | bytes 2162689 | tf_op jit(solution)/shard_map/jit(_where)/select_n | solution.py:814
  81.4 2.9 %halve.4 = (f32[2,16,4608]{2,1,0:T(8,128)}, bf16[2,16,4608]{2,1,0:T(8,128)(2,1)}) custom-call(s32[16]{0:T(128)} %dynamic-slice_bitcast_fusion.info.refs_0_, f32[2,2,16,4608]{3,2,1,0:T(8,128)} %bitcast.26, bf16[2,2,16,4608]{3,2,1,0:T(8,128)(2,1)} %bitcast.11.refs_1_, bf16[352,1024]{1,0:T(8,128)(2,1)} %gate.11.refs_2_.refs_1_.refs_12_), custom_call_target="tpu_custom_call" | custom-call | flops 2000000 | tf_op jit(solution)/shard_map/halve/pallas_call | solution.py:710
  84.3 7.6 %collective-permute-done.22.refs_0_ = bf16[352,1024]{1,0:T(8,128)(2,1)} collective-permute-done((bf16[352,1024]{1,0:T(8,128)(2,1)}, bf16[352,1024]{1,0:T(8,128)(2,1)}, u32[]{:S(2)}, u32[]{:S(2)}) %collective-permute-start.22) | collective-permute-done | bytes 720928 | tf_op jit(solution)/shard_map/ppermute | solution.py:595
  92.0 3.6 %collective-permute-start.24 = (bf16[352,1024]{1,0:T(8,128)(2,1)}, bf16[352,1024]{1,0:T(8,128)(2,1)}, u32[]{:S(2)}, u32[]{:S(2)}) collective-permute-start(bf16[352,1024]{1,0:T(8,128)(2,1)} %gate.12.refs_17_.refs_13_.refs_14_), channel_id=1, source_target_pairs={{0,16},{2,18},{4,20},{6,22},{8,24},{10,26},{12,28},{14,30},{16,0},... | collective-permute-start | bytes 2162696 | tf_op jit(solution)/shard_map/ppermute | solution.py:802
  95.8 11.3 %weights.6 = (bf16[384,8192]{1,0:T(8,128)(2,1)}, f32[384,1024]{1,0:T(8,128)}) custom-call(s32[16]{0:T(128)} %dynamic-slice_bitcast_fusion.info.refs_0_, s32[3,3]{1,0:T(4,128)} %get-tuple-element.38.table.refs_1_, bf16[768,8192]{1,0:T(8,128)(2,1)} %refs_2_.7, bf16[384,4096]{1,0:T(8,128)(2,1)} %collective-permute-done.2.refs_3_, ...), custom_call_target="tpu_custom_call", output_to_operand_aliasing={{0}: (9, {})} | custom-call | flops 7000000 | tf_op jit(solution)/shard_map/weights/pallas_call | solution.py:746
  107.1 2.6 %halve.5 = (f32[1,16,4608]{2,1,0:T(8,128)}, bf16[1,16,4608]{2,1,0:T(8,128)(2,1)}) custom-call(s32[16]{0:T(128)} %dynamic-slice_bitcast_fusion.info.refs_0_, f32[1,2,16,4608]{3,2,1,0:T(8,128)} %bitcast.29, bf16[1,2,16,4608]{3,2,1,0:T(8,128)(2,1)} %bitcast.13.refs_1_, f32[384,1024]{1,0:T(8,128)} %get-tuple-element.63.refs_2_.refs_1_.refs_11_), custom_call_target="tpu_custom_call" | custom-call | flops 2000000 | tf_op jit(solution)/shard_map/halve/pallas_call | solution.py:710
  110.3 1.9 %collective-permute-start.27 = (bf16[1,16,4608]{2,1,0:T(8,128)(2,1)}, bf16[1,16,4608]{2,1,0:T(8,128)(2,1)S(1)}, u32[]{:S(2)}, u32[]{:S(2)}) collective-permute-start(bf16[1,16,4608]{2,1,0:T(8,128)(2,1)} %get-tuple-element.69), channel_id=1, source_target_pairs={{0,8},{2,10},{4,12},{6,14},{8,0},{10,2},{12,4},{14,6},{1,9},{3,11}... | collective-permute-start | bytes 442376 | tf_op jit(solution)/shard_map/ppermute | solution.py:604
  114.5 6.7 %weights.7 = (bf16[384,8192]{1,0:T(8,128)(2,1)}, bf16[384,1024]{1,0:T(8,128)(2,1)}) custom-call(s32[16]{0:T(128)} %dynamic-slice_bitcast_fusion.info.refs_0_, s32[3,3]{1,0:T(4,128)} %get-tuple-element.38.table.refs_1_, bf16[768,8192]{1,0:T(8,128)(2,1)} %refs_2_.7, ...), custom_call_target="tpu_custom_call", output_to_operand_aliasing={{0}: (12, {})} | custom-call | flops 4000000 | tf_op jit(solution)/shard_map/weights/pallas_call | solution.py:746
  121.9 1.8 %final.1 = (f32[16,4096]{1,0:T(8,128)}, f32[16,512]{1,0:T(8,128)}) custom-call(f32[16,4608]{1,0:T(8,128)} %bitcast.30, bf16[16,4608]{1,0:T(8,128)(2,1)} %bitcast.33, bf16[384,1024]{1,0:T(8,128)(2,1)} %get-tuple-element.34.after), custom_call_target="tpu_custom_call" | custom-call | flops 2000000 | tf_op jit(solution)/shard_map/final/pallas_call | solution.py:835
  (77 shorter events, 14.5 us)
Async XLA Ops:
  0.7 8.6 %collective-permute-start.1 = (bf16[384,1024]{1,0:T(8,128)(2,1)}, bf16[384,1024]{1,0:T(8,128)(2,1)}, u32[]{:S(2)}, u32[]{:S(2)}) collective-permute-start(bf16[384,1024]{1,0:T(8,128)(2,1)} %grad.1), channel_id=1, source_target_pairs={{0,1},{1,0},{2,3},{3,2},{4,5},{5,4},{6,7},{7,6},{8,9},{9,8},{10,11... | collective-permute-start | bytes 2359304 | tf_op jit(solution)/shard_map/ppermute | solution.py:601
  3.7 16.5 %collective-permute-start.3 = (bf16[352,1024]{1,0:T(8,128)(2,1)}, bf16[352,1024]{1,0:T(8,128)(2,1)S(1)}, u32[]{:S(2)}, u32[]{:S(2)}) collective-permute-start(bf16[352,1024]{1,0:T(8,128)(2,1)} %get-tuple-element.73), channel_id=1, source_target_pairs={{0,4},{1,3},{4,8},{5,1},{8,12},{9,5},{12,14},{13,9},{14,10},{15,13... | collective-permute-start | bytes 2162696 | tf_op jit(solution)/shard_map/ppermute | solution.py:595
  6.3 17.2 %collective-permute-start.4 = (bf16[352,1024]{1,0:T(8,128)(2,1)}, bf16[352,1024]{1,0:T(8,128)(2,1)}, u32[]{:S(2)}, u32[]{:S(2)}) collective-permute-start(bf16[352,1024]{1,0:T(8,128)(2,1)} %get-tuple-element.72), channel_id=1, source_target_pairs={{0,4},{1,3},{4,8},{5,1},{8,12},{9,5},{12,14},{13,9},{14,10},{15,13... | collective-permute-start | bytes 2162696 | tf_op jit(solution)/shard_map/ppermute | solution.py:595
  23.6 14.7 %collective-permute-start.11 = (bf16[352,1024]{1,0:T(8,128)(2,1)}, bf16[352,1024]{1,0:T(8,128)(2,1)}, u32[]{:S(2)}, u32[]{:S(2)}) collective-permute-start(bf16[352,1024]{1,0:T(8,128)(2,1)} %get-tuple-element.43.after.refs_9_), channel_id=1, source_target_pairs={{0,4},{1,3},{4,8},{5,1},{8,12},{9,5},{12,14},{13,9},{14,10},{15,13... | collective-permute-start | bytes 2162696 | tf_op jit(solution)/shard_map/ppermute | solution.py:595
  25.6 21.3 %collective-permute-start.7 = (bf16[352,1024]{1,0:T(8,128)(2,1)}, bf16[352,1024]{1,0:T(8,128)(2,1)}, u32[]{:S(2)}, u32[]{:S(2)}) collective-permute-start(bf16[352,1024]{1,0:T(8,128)(2,1)} %get-tuple-element.43.after.refs_9_), channel_id=1, source_target_pairs={{0,16},{16,0},{1,17},{17,1},{2,18},{18,2},{3,19},{19,3},{4,20},{20... | collective-permute-start | bytes 2162696 | tf_op jit(solution)/shard_map/ppermute | solution.py:598
  27.1 21.3 %collective-permute-start.2 = (bf16[384,4096]{1,0:T(8,128)(2,1)}, bf16[384,4096]{1,0:T(8,128)(2,1)}, u32[]{:S(2)}, u32[]{:S(2)}) collective-permute-start(bf16[384,4096]{1,0:T(8,128)(2,1)} %get-tuple-element.39), channel_id=1, source_target_pairs={{0,1},{1,0},{2,3},{3,2},{4,5},{5,4},{6,7},{7,6},{8,9},{9,8},{10,11... | collective-permute-start | bytes 9437192 | tf_op jit(solution)/shard_map/ppermute | solution.py:601
  27.1 18.1 %collective-permute-start.8 = (bf16[352,1024]{1,0:T(8,128)(2,1)}, bf16[352,1024]{1,0:T(8,128)(2,1)S(1)}, u32[]{:S(2)}, u32[]{:S(2)}) collective-permute-start(bf16[352,1024]{1,0:T(8,128)(2,1)} %get-tuple-element.49.refs_10_), channel_id=1, source_target_pairs={{0,4},{1,3},{4,8},{5,1},{8,12},{9,5},{12,14},{13,9},{14,10},{15,13... | collective-permute-start | bytes 2162696 | tf_op jit(solution)/shard_map/ppermute | solution.py:595
  28.7 11.9 %collective-permute-start.9 = (f32[128,4096]{1,0:T(8,128)}, f32[128,4096]{1,0:T(8,128)}, u32[]{:S(2)}, u32[]{:S(2)}) collective-permute-start(f32[128,4096]{1,0:T(8,128)} %get-tuple-element.52), channel_id=1, source_target_pairs={{0,1},{1,0},{2,3},{3,2},{4,5},{5,4},{6,7},{7,6},{8,9},{9,8},{10,11... | collective-permute-start | bytes 6291464 | tf_op jit(solution)/shard_map/ppermute | solution.py:601
  40.2 8.7 %collective-permute-start.5 = (bf16[384,4096]{1,0:T(8,128)(2,1)}, bf16[384,4096]{1,0:T(8,128)(2,1)}, u32[]{:S(2)}, u32[]{:S(2)}) collective-permute-start(bf16[384,4096]{1,0:T(8,128)(2,1)} %get-tuple-element.44), channel_id=1, source_target_pairs={{0,1},{1,0},{2,3},{3,2},{4,5},{5,4},{6,7},{7,6},{8,9},{9,8},{10,11... | collective-permute-start | bytes 9437192 | tf_op jit(solution)/shard_map/ppermute | solution.py:601
  40.6 24.2 %collective-permute-start.13 = (bf16[352,1024]{1,0:T(8,128)(2,1)}, bf16[352,1024]{1,0:T(8,128)(2,1)}, u32[]{:S(2)}, u32[]{:S(2)}) collective-permute-start(bf16[352,1024]{1,0:T(8,128)(2,1)} %gate.8.refs_4_.refs_11_), channel_id=1, source_target_pairs={{0,16},{16,0},{1,17},{17,1},{2,18},{18,2},{3,19},{19,3},{4,20},{20... | collective-permute-start | bytes 2162696 | tf_op jit(solution)/shard_map/ppermute | solution.py:598
  45.3 18.0 %collective-permute-start.14 = (bf16[352,1024]{1,0:T(8,128)(2,1)}, bf16[352,1024]{1,0:T(8,128)(2,1)}, u32[]{:S(2)}, u32[]{:S(2)}) collective-permute-start(bf16[352,1024]{1,0:T(8,128)(2,1)} %gate.8.refs_4_.refs_11_), channel_id=1, source_target_pairs={{0,4},{1,3},{4,8},{5,1},{8,12},{9,5},{12,14},{13,9},{14,10},{15,13... | collective-permute-start | bytes 2162696 | tf_op jit(solution)/shard_map/ppermute | solution.py:595
  46.9 30.4 %collective-permute-start.16 = (bf16[352,1024]{1,0:T(8,128)(2,1)}, bf16[352,1024]{1,0:T(8,128)(2,1)S(1)}, u32[]{:S(2)}, u32[]{:S(2)}) collective-permute-start(bf16[352,1024]{1,0:T(8,128)(2,1)} %gate.9.refs_12_), channel_id=1, source_target_pairs={{0,4},{1,3},{4,8},{5,1},{8,12},{9,5},{12,14},{13,9},{14,10},{15,13... | collective-permute-start | bytes 2162696 | tf_op jit(solution)/shard_map/ppermute | solution.py:595
  48.4 28.9 %collective-permute-start.17 = (bf16[4,16,4608]{2,1,0:T(8,128)(2,1)}, bf16[4,16,4608]{2,1,0:T(8,128)(2,1)}, u32[]{:S(2)}, u32[]{:S(2)}) collective-permute-start(bf16[4,16,4608]{2,1,0:T(8,128)(2,1)} %get-tuple-element.61), channel_id=1, source_target_pairs={{0,2},{2,0},{4,6},{6,4},{8,10},{10,8},{12,14},{14,12},{1,3},{3,1},... | collective-permute-start | bytes 1769480 | tf_op jit(solution)/shard_map/ppermute | solution.py:604
  57.5 7.3 %collective-permute-start.12 = (bf16[1024,1024]{1,0:T(8,128)(2,1)}, bf16[1024,1024]{1,0:T(8,128)(2,1)}, u32[]{:S(2)}, u32[]{:S(2)}) collective-permute-start(bf16[1024,1024]{1,0:T(8,128)(2,1)} %get-tuple-element.57), channel_id=1, source_target_pairs={{0,1},{1,0},{2,3},{3,2},{4,5},{5,4},{6,7},{7,6},{8,9},{9,8},{10,11... | collective-permute-start | bytes 6291464 | tf_op jit(solution)/shard_map/ppermute | solution.py:601
  63.3 17.1 %collective-permute-start.18 = (bf16[352,1024]{1,0:T(8,128)(2,1)}, bf16[352,1024]{1,0:T(8,128)(2,1)}, u32[]{:S(2)}, u32[]{:S(2)}) collective-permute-start(bf16[352,1024]{1,0:T(8,128)(2,1)} %gate.10.refs_14_.refs_11_), channel_id=1, source_target_pairs={{0,16},{16,0},{1,17},{17,1},{2,18},{18,2},{3,19},{19,3},{4,20},{20... | collective-permute-start | bytes 2162696 | tf_op jit(solution)/shard_map/ppermute | solution.py:598
  80.4 11.6 %collective-permute-start.22 = (bf16[352,1024]{1,0:T(8,128)(2,1)}, bf16[352,1024]{1,0:T(8,128)(2,1)}, u32[]{:S(2)}, u32[]{:S(2)}) collective-permute-start(bf16[352,1024]{1,0:T(8,128)(2,1)} %broadcast_select_fusion), channel_id=1, source_target_pairs={{0,4},{1,3},{4,8},{5,1},{8,12},{9,5},{12,14},{13,9},{14,10},{15,13... | collective-permute-start | bytes 2162696 | tf_op jit(solution)/shard_map/ppermute | solution.py:595
  80.4 15.2 %collective-permute-start.19 = (bf16[352,1024]{1,0:T(8,128)(2,1)}, bf16[352,1024]{1,0:T(8,128)(2,1)}, u32[]{:S(2)}, u32[]{:S(2)}) collective-permute-start(bf16[352,1024]{1,0:T(8,128)(2,1)} %gate.10.refs_14_.refs_11_), channel_id=1, source_target_pairs={{0,1},{1,0},{2,3},{3,2},{4,5},{5,4},{6,7},{7,6},{8,9},{9,8},{10,11... | collective-permute-start | bytes 2162696 | tf_op jit(solution)/shard_map/ppermute | solution.py:601
  80.4 15.3 %collective-permute-start.21 = (bf16[352,1024]{1,0:T(8,128)(2,1)}, bf16[352,1024]{1,0:T(8,128)(2,1)}, u32[]{:S(2)}, u32[]{:S(2)}) collective-permute-start(bf16[352,1024]{1,0:T(8,128)(2,1)} %collective-permute-done.18.refs_13_), channel_id=1, source_target_pairs={{0,1},{1,0},{2,3},{3,2},{4,5},{5,4},{6,7},{7,6},{8,9},{9,8},{10,11... | collective-permute-start | bytes 2162696 | tf_op jit(solution)/shard_map/ppermute | solution.py:601
  80.9 14.9 %collective-permute-start.20 = (bf16[352,1024]{1,0:T(8,128)(2,1)S(1)}, bf16[352,1024]{1,0:T(8,128)(2,1)}, u32[]{:S(2)}, u32[]{:S(2)}) collective-permute-start(bf16[352,1024]{1,0:T(8,128)(2,1)S(1)} %copy-done.1), channel_id=1, source_target_pairs={{0,1},{1,0},{2,3},{3,2},{4,5},{5,4},{6,7},{7,6},{8,9},{9,8},{10,11... | collective-permute-start | bytes 2162696 | tf_op jit(solution)/shard_map/ppermute | solution.py:601
  80.9 14.8 %collective-permute-start.15 = (bf16[1024,1024]{1,0:T(8,128)(2,1)}, bf16[1024,1024]{1,0:T(8,128)(2,1)}, u32[]{:S(2)}, u32[]{:S(2)}) collective-permute-start(bf16[1024,1024]{1,0:T(8,128)(2,1)} %get-tuple-element.60), channel_id=1, source_target_pairs={{0,1},{1,0},{2,3},{3,2},{4,5},{5,4},{6,7},{7,6},{8,9},{9,8},{10,11... | collective-permute-start | bytes 6291464 | tf_op jit(solution)/shard_map/ppermute | solution.py:601
  92.0 17.7 %collective-permute-start.24 = (bf16[352,1024]{1,0:T(8,128)(2,1)}, bf16[352,1024]{1,0:T(8,128)(2,1)}, u32[]{:S(2)}, u32[]{:S(2)}) collective-permute-start(bf16[352,1024]{1,0:T(8,128)(2,1)} %gate.12.refs_17_.refs_13_.refs_14_), channel_id=1, source_target_pairs={{0,16},{2,18},{4,20},{6,22},{8,24},{10,26},{12,28},{14,30},{16,0},... | collective-permute-start | bytes 2162696 | tf_op jit(solution)/shard_map/ppermute | solution.py:802
  95.6 11.5 %collective-permute-start.25 = (bf16[2,16,4608]{2,1,0:T(8,128)(2,1)}, bf16[2,16,4608]{2,1,0:T(8,128)(2,1)}, u32[]{:S(2)}, u32[]{:S(2)}) collective-permute-start(bf16[2,16,4608]{2,1,0:T(8,128)(2,1)} %get-tuple-element.65), channel_id=1, source_target_pairs={{0,4},{2,6},{4,0},{6,2},{8,12},{10,14},{12,8},{14,10},{1,5},{3,7},... | collective-permute-start | bytes 884744 | tf_op jit(solution)/shard_map/ppermute | solution.py:604
  95.7 17.9 %collective-permute-start.23 = (bf16[352,1024]{1,0:T(8,128)(2,1)}, bf16[352,1024]{1,0:T(8,128)(2,1)}, u32[]{:S(2)}, u32[]{:S(2)}) collective-permute-start(bf16[352,1024]{1,0:T(8,128)(2,1)} %gate.12.refs_17_.refs_13_.refs_14_), channel_id=1, source_target_pairs={{0,1},{1,0},{2,3},{3,2},{4,5},{5,4},{6,7},{7,6},{8,9},{9,8},{10,11... | collective-permute-start | bytes 2162696 | tf_op jit(solution)/shard_map/ppermute | solution.py:601
  110.3 11.0 %collective-permute-start.27 = (bf16[1,16,4608]{2,1,0:T(8,128)(2,1)}, bf16[1,16,4608]{2,1,0:T(8,128)(2,1)S(1)}, u32[]{:S(2)}, u32[]{:S(2)}) collective-permute-start(bf16[1,16,4608]{2,1,0:T(8,128)(2,1)} %get-tuple-element.69), channel_id=1, source_target_pairs={{0,8},{2,10},{4,12},{6,14},{8,0},{10,2},{12,4},{14,6},{1,9},{3,11}... | collective-permute-start | bytes 442376 | tf_op jit(solution)/shard_map/ppermute | solution.py:604
  (16 other events, 42.7 us)

commit v4 on v3

--- a/solution.py
+++ b/solution.py
@@ -502,7 +502,7 @@
     pass
 
 
-def gate(values, tokens):
+def gate(values, tokens, weight=1.0):
     out = pl.pallas_call(
         gate_kernel,
         out_shape=tuple(jax.ShapeDtypeStruct(value.shape, value.dtype) for value in values),
@@ -510,7 +510,7 @@
         out_specs=(ANY,) * len(values),
         input_output_aliases={i: i for i in range(len(values))},
         compiler_params=pltpu.CompilerParams(vmem_limit_bytes=VMEM_LIMIT),
-        cost_estimate=cost(GATE),
+        cost_estimate=cost(GATE * weight),
         name="gate",
     )(*values, *tokens)
     return list(out)
@@ -656,8 +656,8 @@
     sent = swap(send)
     got = swap(packed)
 
-    def next_edge(token):
-        (value,) = gate([around(edges[-1])], [token])
+    def next_edge(*tokens):
+        (value,) = gate([around(edges[-1])], tokens)
         edges.append(value)
         others.append(partner(value))
 
@@ -665,8 +665,9 @@
         (value,) = gate([around(middles[-1])], tokens)
         middles.append(value)
 
-    edges, middles = (list(pair) for pair in zip(gate([edge_rows, middle_rows], [low_part])))
+    edges = gate([edge_rows], [low_part])
     others = [partner(edges[0])]
+    middles = gate([middle_rows], [edges[0]], 0.0)
 
     keep, keep_up, send_up, packed_other, low_slots, low_send = pl.pallas_call(
         functools.partial(tail_kernel, dims),
@@ -693,7 +694,7 @@
         name="tail",
     )(
         info, block_adapter, adapter_owner, table,
-        held_rows, down, mask_slots, back_slots, low_part, edges[0],
+        held_rows, down, mask_slots, back_slots, low_part, middles[0],
     )
     if steps > 2:
         next_edge(keep_up)
@@ -779,7 +780,7 @@
 
     whole = [(EDGE, None, None), (MIDDLE, None, middle_cut), (OTHER, None, None)]
     full = [(None, None, None)]
-    state, after, last = (None, None), middles[1:] or [sums], None
+    state, after, last = (None, None), (middles[1:] or [sums]) + [low_got], None
     for k in range(1, steps):
         jobs, pieces = [], []
         if k == 1:
@@ -795,11 +796,10 @@
         if not handing:
             jobs.append((THEIRS + k - 1, whole, 0))
             pieces += [swap(part) for part in mine]
-            if last is not None:
-                (last,) = gate([last], after)
-                after = [last]
-                last_sib = swap(last)
-                last_other = lax.ppermute(last, ALL, first_core)
+            (last,) = gate([last], after)
+            after = [last]
+            last_sib = swap(last)
+            last_other = lax.ppermute(last, ALL, first_core)
         state, out, _ = multiply(state, jobs, pieces, after=after, us=7)
         after = []
         if handing:

time: 124 us -> 122 us (0.984)
  waiting for transfers between devices: 22.7 us -> 15.7 us
  starting transfers between devices: 23.8 us -> 26.5 us
  local copies, waits for them, and re-layouts: 6.75 us -> 8.02 us
    ppermute x7, waiting for transfers between devices: 16.7 us -> 10.5 us  [around(): return lax.ppermute(value, ALL, ring_pairs)]
    dynamic_slice x0 -> x1, local copies, waits for them, and re-layouts: none -> 2.58 us  [body(): lax.dynamic_slice(value_weight, (edge_start, 0), (piece, width))]
    slice x1 -> x0, local copies, waits for them, and re-layouts: 2.52 us -> none  [body(): middle_rows = around(value_weight[middle_at:middle_at + piece])]
    ppermute x3, starting transfers between devices: 3.52 us -> 5.41 us  [partner(): return lax.ppermute(value, 'group', [(g, g ^ 1) for g in range(groups)])]
    ppermute x3, waiting for transfers between devices: 0.01 us -> 1.63 us  [partner(): return lax.ppermute(value, 'group', [(g, g ^ 1) for g in range(groups)])]
    ppermute x14, waiting for transfers between devices: 2.91 us -> 1.5 us  [swap(): return lax.ppermute(value, 'dp', [(0, 1), (1, 0)])]
  transfers between devices with their start and end apart: 28 -> 28, of which waited for: 6 -> 7; matrix products, arithmetic and copies ran while one was open for 5% -> 5% of each run, Pallas kernels for 53% -> 54%
where the time goes in v4:
time: 122 us; the launch traced here: 121 us
  Pallas kernels  67.5 us (55%)
  starting transfers between devices  26.5 us (22%)
  waiting for transfers between devices  15.7 us (13%)
  local copies, waits for them, and re-layouts  8.02 us (7%)
  other arithmetic  2.21 us (2%)
    pallas_call x4, Pallas kernels, multiply(): pl.pallas_call(functools.partial(weight_kernel, dims, jobs, first, last,...  36.2 us
    ppermute x7, starting transfers between devices, around(): return lax.ppermute(value, ALL, ring_pairs)  11.2 us
    ppermute x7, waiting for transfers between devices, around(): return lax.ppermute(value, ALL, ring_pairs)  10.5 us
    pallas_call x1, Pallas kernels, body(): pl.pallas_call(functools.partial(head_kernel, dims), out_shape=(sds((flat...  10.4 us
    pallas_call x3, Pallas kernels, halve(): pl.pallas_call(functools.partial(halve_kernel, parts, BITS + bit, len(aft...  9.67 us
    pallas_call x1, Pallas kernels, body(): pl.pallas_call(functools.partial(tail_kernel, dims), out_shape=(sds((flat...  9.53 us
    ppermute x3, starting transfers between devices, partner(): return lax.ppermute(value, 'group', [(g, g ^ 1) for g in range(groups)])  5.41 us
    unnamed x24, local copies, waits for them, and re-layouts  4.17 us
  transfers between devices with their start and end apart: 28, of which 7 were waited for; matrix products, arithmetic and copies ran while one was open for 5% of the time, Pallas kernels for 54%

profile of v4, /device:TPU:0, one launch (start us, length us, event | category | flops | bytes accessed | tf_op | source)
XLA Modules:
  0.0 121.0 jit_solution(6489199042060132073)
XLA Ops:
  1.2 2.6 %constant_dynamic-slice_fusion = (bf16[352,1024]{1,0:T(8,128)(2,1)}, bf16[352,1024]{1,0:T(8,128)(2,1)}) fusion(bf16[1024,1024]{1,0:T(8,128)(2,1)} %refs_8_.1, s32[]{:T(128)S(6)} %select_n.17), kind=kLoop, calls=%fused_computation.3 | loop fusion | bytes 2883588 | tf_op jit(solution)/shard_map/dynamic_slice | solution.py:612
  3.8 2.6 %collective-permute-start.4 = (bf16[352,1024]{1,0:T(8,128)(2,1)}, bf16[352,1024]{1,0:T(8,128)(2,1)}, u32[]{:S(2)}, u32[]{:S(2)}) collective-permute-start(bf16[352,1024]{1,0:T(8,128)(2,1)} %get-tuple-element.68), channel_id=1, source_target_pairs={{0,4},{1,3},{4,8},{5,1},{8,12},{9,5},{12,14},{13,9},{14,10},{15,13... | collective-permute-start | bytes 2162696 | tf_op jit(solution)/shard_map/ppermute | solution.py:595
  9.9 10.4 %head.1 = (f32[128,4096]{1,0:T(8,128)}, bf16[384,4096]{1,0:T(8,128)(2,1)}, s32[3,3]{1,0:T(4,128)}, bf16[384,1024]{1,0:T(8,128)(2,1)}, bf16[384,128]{1,0:T(8,128)...) custom-call(s32[16]{0:T(128)} %dynamic-slice_bitcast_fusion.info.refs_0_, s32[6]{0:T(128)} %home.1, ...), custom_call_target="tpu_custom_call" | custom-call | flops 7000000 | tf_op jit(solution)/shard_map/head/pallas_call | solution.py:623
  20.3 1.6 %collective-permute-start.11 = (bf16[352,1024]{1,0:T(8,128)(2,1)}, bf16[352,1024]{1,0:T(8,128)(2,1)}, u32[]{:S(2)}, u32[]{:S(2)}) collective-permute-start(bf16[352,1024]{1,0:T(8,128)(2,1)} %gate.8.refs_1_.refs_9_), channel_id=1, source_target_pairs={{0,4},{1,3},{4,8},{5,1},{8,12},{9,5},{12,14},{13,9},{14,10},{15,13... | collective-permute-start | bytes 2162696 | tf_op jit(solution)/shard_map/ppermute | solution.py:595
  24.4 2.1 %collective-permute-start.8 = (bf16[352,1024]{1,0:T(8,128)(2,1)}, bf16[352,1024]{1,0:T(8,128)(2,1)S(1)}, u32[]{:S(2)}, u32[]{:S(2)}) collective-permute-start(bf16[352,1024]{1,0:T(8,128)(2,1)} %gate.9.after.refs_10_), channel_id=1, source_target_pairs={{0,4},{1,3},{4,8},{5,1},{8,12},{9,5},{12,14},{13,9},{14,10},{15,13... | collective-permute-start | bytes 2162696 | tf_op jit(solution)/shard_map/ppermute | solution.py:595
  26.5 9.5 %tail.1 = (f32[128,4096]{1,0:T(8,128)}, f32[128,512]{1,0:T(8,128)}, f32[128,512]{1,0:T(8,128)}, bf16[384,4096]{1,0:T(8,128)(2,1)}, bf16[768,128]{1,0:T(8,128)(2,1)}, /*index=5*/bf16[384,128]{1,0:T(8,128)(2,1)}) custom-call(s32[16]{0:T(128)} %dynamic-slice_bitcast_fusion.info.refs_0_, s32[6]{0:T(128)} %adapter.3, s32[8]{0:T(128)} %owner.3, ...), custom_call_target="tpu_custom_call" | custom-call | flops 7000000 | tf_op jit(solution)/shard_map/tail/pallas_call | solution.py:672
  39.0 4.1 %halve.3 = (f32[4,16,4608]{2,1,0:T(8,128)}, bf16[4,16,4608]{2,1,0:T(8,128)(2,1)}) custom-call(s32[16]{0:T(128)} %dynamic-slice_bitcast_fusion.info.refs_0_, f32[4,2,16,4096]{3,2,1,0:T(8,128)} %bitcast.25, f32[4,2,16,512]{3,2,1,0:T(8,128)} %bitcast.31, f32[4,2,16,4096]{3,2,1,0:T(8,128)} %bitcast.8.refs_2_, f32[4,2,16,512]{3,2,1,0:T(8,128)} %bitcast.32, ...), custom_call_target="tpu_custom_call" | custom-call | flops 2000000 | tf_op jit(solution)/shard_map/halve/pallas_call | solution.py:711
  43.2 1.6 %collective-permute-start.14 = (bf16[352,1024]{1,0:T(8,128)(2,1)}, bf16[352,1024]{1,0:T(8,128)(2,1)}, u32[]{:S(2)}, u32[]{:S(2)}) collective-permute-start(bf16[352,1024]{1,0:T(8,128)(2,1)} %gate.10.refs_4_.refs_11_), channel_id=1, source_target_pairs={{0,4},{1,3},{4,8},{5,1},{8,12},{9,5},{12,14},{13,9},{14,10},{15,13... | collective-permute-start | bytes 2162696 | tf_op jit(solution)/shard_map/ppermute | solution.py:595
  44.8 1.6 %collective-permute-start.13 = (bf16[352,1024]{1,0:T(8,128)(2,1)}, bf16[352,1024]{1,0:T(8,128)(2,1)}, u32[]{:S(2)}, u32[]{:S(2)}) collective-permute-start(bf16[352,1024]{1,0:T(8,128)(2,1)} %gate.10.refs_4_.refs_11_), channel_id=1, source_target_pairs={{0,16},{16,0},{1,17},{17,1},{2,18},{18,2},{3,19},{19,3},{4,20},{20... | collective-permute-start | bytes 2162696 | tf_op jit(solution)/shard_map/ppermute | solution.py:598
  46.4 1.6 %collective-permute-start.16 = (bf16[352,1024]{1,0:T(8,128)(2,1)}, bf16[352,1024]{1,0:T(8,128)(2,1)S(1)}, u32[]{:S(2)}, u32[]{:S(2)}) collective-permute-start(bf16[352,1024]{1,0:T(8,128)(2,1)} %gate.11.refs_12_), channel_id=1, source_target_pairs={{0,4},{1,3},{4,8},{5,1},{8,12},{9,5},{12,14},{13,9},{14,10},{15,13... | collective-permute-start | bytes 2162696 | tf_op jit(solution)/shard_map/ppermute | solution.py:595
  48.4 8.8 %weights.4 = (bf16[384,8192]{1,0:T(8,128)(2,1)}, f32[384,1024]{1,0:T(8,128)}, bf16[1024,1024]{1,0:T(8,128)(2,1)}) custom-call(s32[16]{0:T(128)} %dynamic-slice_bitcast_fusion.info.refs_0_, s32[3,3]{1,0:T(4,128)} %get-tuple-element.36.table.refs_1_, bf16[768,8192]{1,0:T(8,128)(2,1)} %refs_2_.7, bf16[384,4096]{1,0:T(8,128)(2,1)} %collective-permute-done.2.refs_3_, ...), custom_call_target="tpu_custom_call" | custom-call | flops 7000000 | tf_op jit(solution)/shard_map/weights/pallas_call | solution.py:747
  57.3 3.0 %collective-permute-done.14.refs_0_ = bf16[352,1024]{1,0:T(8,128)(2,1)} collective-permute-done((bf16[352,1024]{1,0:T(8,128)(2,1)}, bf16[352,1024]{1,0:T(8,128)(2,1)}, u32[]{:S(2)}, u32[]{:S(2)}) %collective-permute-start.14) | collective-permute-done | bytes 720928 | tf_op jit(solution)/shard_map/ppermute | solution.py:595
  60.3 2.4 %collective-permute-start.18 = (bf16[352,1024]{1,0:T(8,128)(2,1)}, bf16[352,1024]{1,0:T(8,128)(2,1)}, u32[]{:S(2)}, u32[]{:S(2)}) collective-permute-start(bf16[352,1024]{1,0:T(8,128)(2,1)} %gate.12.refs_14_.refs_11_), channel_id=1, source_target_pairs={{0,16},{16,0},{1,17},{17,1},{2,18},{18,2},{3,19},{19,3},{4,20},{20... | collective-permute-start | bytes 2162696 | tf_op jit(solution)/shard_map/ppermute | solution.py:598
  62.6 1.6 %collective-permute-done.13.refs_13_ = bf16[352,1024]{1,0:T(8,128)(2,1)} collective-permute-done((bf16[352,1024]{1,0:T(8,128)(2,1)}, bf16[352,1024]{1,0:T(8,128)(2,1)}, u32[]{:S(2)}, u32[]{:S(2)}) %collective-permute-start.13) | collective-permute-done | bytes 720928 | tf_op jit(solution)/shard_map/ppermute | solution.py:598
  64.3 9.5 %weights.5 = (bf16[384,8192]{1,0:T(8,128)(2,1)}, f32[384,1024]{1,0:T(8,128)}, bf16[1024,1024]{1,0:T(8,128)(2,1)}) custom-call(s32[16]{0:T(128)} %dynamic-slice_bitcast_fusion.info.refs_0_, s32[3,3]{1,0:T(4,128)} %get-tuple-element.36.table.refs_1_, bf16[768,8192]{1,0:T(8,128)(2,1)} %refs_2_.7, ...), custom_call_target="tpu_custom_call", output_to_operand_aliasing={{0}: (9, {})} | custom-call | flops 7000000 | tf_op jit(solution)/shard_map/weights/pallas_call | solution.py:747
  76.1 2.2 %broadcast_select_fusion = bf16[352,1024]{1,0:T(8,128)(2,1)} fusion(bf16[352,1024]{1,0:T(8,128)(2,1)} %gate.12.refs_14_.refs_11_, bf16[352,1024]{1,0:T(8,128)(2,1)} %gate.13.refs_2_.refs_1_.refs_12_, pred[]{:T(512)S(6)} %eq.7), kind=kLoop, calls=%fused_computation | loop fusion | flops 360448 | bytes 2162689 | tf_op jit(solution)/shard_map/jit(_where)/select_n | solution.py:814
  79.4 2.9 %halve.4 = (f32[2,16,4608]{2,1,0:T(8,128)}, bf16[2,16,4608]{2,1,0:T(8,128)(2,1)}) custom-call(s32[16]{0:T(128)} %dynamic-slice_bitcast_fusion.info.refs_0_, f32[2,2,16,4608]{3,2,1,0:T(8,128)} %bitcast.26, bf16[2,2,16,4608]{3,2,1,0:T(8,128)(2,1)} %bitcast.11.refs_1_, bf16[352,1024]{1,0:T(8,128)(2,1)} %gate.13.refs_2_.refs_1_.refs_12_), custom_call_target="tpu_custom_call" | custom-call | flops 2000000 | tf_op jit(solution)/shard_map/halve/pallas_call | solution.py:711
  82.4 7.5 %collective-permute-done.22.refs_0_ = bf16[352,1024]{1,0:T(8,128)(2,1)} collective-permute-done((bf16[352,1024]{1,0:T(8,128)(2,1)}, bf16[352,1024]{1,0:T(8,128)(2,1)}, u32[]{:S(2)}, u32[]{:S(2)}) %collective-permute-start.22) | collective-permute-done | bytes 720928 | tf_op jit(solution)/shard_map/ppermute | solution.py:595
  89.9 3.6 %collective-permute-start.24 = (bf16[352,1024]{1,0:T(8,128)(2,1)}, bf16[352,1024]{1,0:T(8,128)(2,1)}, u32[]{:S(2)}, u32[]{:S(2)}) collective-permute-start(bf16[352,1024]{1,0:T(8,128)(2,1)} %gate.14.refs_17_.refs_13_.refs_14_), channel_id=1, source_target_pairs={{0,16},{2,18},{4,20},{6,22},{8,24},{10,26},{12,28},{14,30},{16,0},... | collective-permute-start | bytes 2162696 | tf_op jit(solution)/shard_map/ppermute | solution.py:802
  93.7 11.4 %weights.6 = (bf16[384,8192]{1,0:T(8,128)(2,1)}, f32[384,1024]{1,0:T(8,128)}) custom-call(s32[16]{0:T(128)} %dynamic-slice_bitcast_fusion.info.refs_0_, s32[3,3]{1,0:T(4,128)} %get-tuple-element.36.table.refs_1_, bf16[768,8192]{1,0:T(8,128)(2,1)} %refs_2_.7, bf16[384,4096]{1,0:T(8,128)(2,1)} %collective-permute-done.2.refs_3_, ...), custom_call_target="tpu_custom_call", output_to_operand_aliasing={{0}: (9, {})} | custom-call | flops 7000000 | tf_op jit(solution)/shard_map/weights/pallas_call | solution.py:747
  105.1 2.6 %halve.5 = (f32[1,16,4608]{2,1,0:T(8,128)}, bf16[1,16,4608]{2,1,0:T(8,128)(2,1)}) custom-call(s32[16]{0:T(128)} %dynamic-slice_bitcast_fusion.info.refs_0_, f32[1,2,16,4608]{3,2,1,0:T(8,128)} %bitcast.29, bf16[1,2,16,4608]{3,2,1,0:T(8,128)(2,1)} %bitcast.13.refs_1_, f32[384,1024]{1,0:T(8,128)} %get-tuple-element.59.refs_2_.refs_1_.refs_11_), custom_call_target="tpu_custom_call" | custom-call | flops 2000000 | tf_op jit(solution)/shard_map/halve/pallas_call | solution.py:711
  108.3 1.9 %collective-permute-start.27 = (bf16[1,16,4608]{2,1,0:T(8,128)(2,1)}, bf16[1,16,4608]{2,1,0:T(8,128)(2,1)S(1)}, u32[]{:S(2)}, u32[]{:S(2)}) collective-permute-start(bf16[1,16,4608]{2,1,0:T(8,128)(2,1)} %get-tuple-element.65), channel_id=1, source_target_pairs={{0,8},{2,10},{4,12},{6,14},{8,0},{10,2},{12,4},{14,6},{1,9},{3,11}... | collective-permute-start | bytes 442376 | tf_op jit(solution)/shard_map/ppermute | solution.py:604
  111.2 6.6 %weights.7 = (bf16[384,8192]{1,0:T(8,128)(2,1)}, bf16[384,1024]{1,0:T(8,128)(2,1)}) custom-call(s32[16]{0:T(128)} %dynamic-slice_bitcast_fusion.info.refs_0_, s32[3,3]{1,0:T(4,128)} %get-tuple-element.36.table.refs_1_, bf16[768,8192]{1,0:T(8,128)(2,1)} %refs_2_.7, ...), custom_call_target="tpu_custom_call", output_to_operand_aliasing={{0}: (12, {})} | custom-call | flops 4000000 | tf_op jit(solution)/shard_map/weights/pallas_call | solution.py:747
  119.1 1.8 %final.1 = (f32[16,4096]{1,0:T(8,128)}, f32[16,512]{1,0:T(8,128)}) custom-call(f32[16,4608]{1,0:T(8,128)} %bitcast.30, bf16[16,4608]{1,0:T(8,128)(2,1)} %bitcast.33, bf16[384,1024]{1,0:T(8,128)(2,1)} %get-tuple-element.32.after), custom_call_target="tpu_custom_call" | custom-call | flops 2000000 | tf_op jit(solution)/shard_map/final/pallas_call | solution.py:835
  (78 shorter events, 16.6 us)
Async XLA Ops:
  0.7 8.7 %collective-permute-start.1 = (bf16[384,1024]{1,0:T(8,128)(2,1)}, bf16[384,1024]{1,0:T(8,128)(2,1)}, u32[]{:S(2)}, u32[]{:S(2)}) collective-permute-start(bf16[384,1024]{1,0:T(8,128)(2,1)} %grad.1), channel_id=1, source_target_pairs={{0,1},{1,0},{2,3},{3,2},{4,5},{5,4},{6,7},{7,6},{8,9},{9,8},{10,11... | collective-permute-start | bytes 2359304 | tf_op jit(solution)/shard_map/ppermute | solution.py:601
  3.8 16.6 %collective-permute-start.4 = (bf16[352,1024]{1,0:T(8,128)(2,1)}, bf16[352,1024]{1,0:T(8,128)(2,1)}, u32[]{:S(2)}, u32[]{:S(2)}) collective-permute-start(bf16[352,1024]{1,0:T(8,128)(2,1)} %get-tuple-element.68), channel_id=1, source_target_pairs={{0,4},{1,3},{4,8},{5,1},{8,12},{9,5},{12,14},{13,9},{14,10},{15,13... | collective-permute-start | bytes 2162696 | tf_op jit(solution)/shard_map/ppermute | solution.py:595
  6.6 16.9 %collective-permute-start.3 = (bf16[352,1024]{1,0:T(8,128)(2,1)}, bf16[352,1024]{1,0:T(8,128)(2,1)S(1)}, u32[]{:S(2)}, u32[]{:S(2)}) collective-permute-start(bf16[352,1024]{1,0:T(8,128)(2,1)} %get-tuple-element.69), channel_id=1, source_target_pairs={{0,4},{1,3},{4,8},{5,1},{8,12},{9,5},{12,14},{13,9},{14,10},{15,13... | collective-permute-start | bytes 2162696 | tf_op jit(solution)/shard_map/ppermute | solution.py:595
  20.3 15.7 %collective-permute-start.11 = (bf16[352,1024]{1,0:T(8,128)(2,1)}, bf16[352,1024]{1,0:T(8,128)(2,1)}, u32[]{:S(2)}, u32[]{:S(2)}) collective-permute-start(bf16[352,1024]{1,0:T(8,128)(2,1)} %gate.8.refs_1_.refs_9_), channel_id=1, source_target_pairs={{0,4},{1,3},{4,8},{5,1},{8,12},{9,5},{12,14},{13,9},{14,10},{15,13... | collective-permute-start | bytes 2162696 | tf_op jit(solution)/shard_map/ppermute | solution.py:595
  22.0 24.4 %collective-permute-start.7 = (bf16[352,1024]{1,0:T(8,128)(2,1)}, bf16[352,1024]{1,0:T(8,128)(2,1)}, u32[]{:S(2)}, u32[]{:S(2)}) collective-permute-start(bf16[352,1024]{1,0:T(8,128)(2,1)} %gate.8.refs_1_.refs_9_), channel_id=1, source_target_pairs={{0,16},{16,0},{1,17},{17,1},{2,18},{18,2},{3,19},{19,3},{4,20},{20... | collective-permute-start | bytes 2162696 | tf_op jit(solution)/shard_map/ppermute | solution.py:598
  23.5 24.5 %collective-permute-start.2 = (bf16[384,4096]{1,0:T(8,128)(2,1)}, bf16[384,4096]{1,0:T(8,128)(2,1)}, u32[]{:S(2)}, u32[]{:S(2)}) collective-permute-start(bf16[384,4096]{1,0:T(8,128)(2,1)} %get-tuple-element.37), channel_id=1, source_target_pairs={{0,1},{1,0},{2,3},{3,2},{4,5},{5,4},{6,7},{7,6},{8,9},{9,8},{10,11... | collective-permute-start | bytes 9437192 | tf_op jit(solution)/shard_map/ppermute | solution.py:601
  24.4 18.8 %collective-permute-start.8 = (bf16[352,1024]{1,0:T(8,128)(2,1)}, bf16[352,1024]{1,0:T(8,128)(2,1)S(1)}, u32[]{:S(2)}, u32[]{:S(2)}) collective-permute-start(bf16[352,1024]{1,0:T(8,128)(2,1)} %gate.9.after.refs_10_), channel_id=1, source_target_pairs={{0,4},{1,3},{4,8},{5,1},{8,12},{9,5},{12,14},{13,9},{14,10},{15,13... | collective-permute-start | bytes 2162696 | tf_op jit(solution)/shard_map/ppermute | solution.py:595
  26.4 11.9 %collective-permute-start.9 = (f32[128,4096]{1,0:T(8,128)}, f32[128,4096]{1,0:T(8,128)}, u32[]{:S(2)}, u32[]{:S(2)}) collective-permute-start(f32[128,4096]{1,0:T(8,128)} %get-tuple-element.48), channel_id=1, source_target_pairs={{0,1},{1,0},{2,3},{3,2},{4,5},{5,4},{6,7},{7,6},{8,9},{9,8},{10,11... | collective-permute-start | bytes 6291464 | tf_op jit(solution)/shard_map/ppermute | solution.py:601
  38.0 10.5 %collective-permute-start.5 = (bf16[384,4096]{1,0:T(8,128)(2,1)}, bf16[384,4096]{1,0:T(8,128)(2,1)}, u32[]{:S(2)}, u32[]{:S(2)}) collective-permute-start(bf16[384,4096]{1,0:T(8,128)(2,1)} %get-tuple-element.41), channel_id=1, source_target_pairs={{0,1},{1,0},{2,3},{3,2},{4,5},{5,4},{6,7},{7,6},{8,9},{9,8},{10,11... | collective-permute-start | bytes 9437192 | tf_op jit(solution)/shard_map/ppermute | solution.py:601
  43.2 17.1 %collective-permute-start.14 = (bf16[352,1024]{1,0:T(8,128)(2,1)}, bf16[352,1024]{1,0:T(8,128)(2,1)}, u32[]{:S(2)}, u32[]{:S(2)}) collective-permute-start(bf16[352,1024]{1,0:T(8,128)(2,1)} %gate.10.refs_4_.refs_11_), channel_id=1, source_target_pairs={{0,4},{1,3},{4,8},{5,1},{8,12},{9,5},{12,14},{13,9},{14,10},{15,13... | collective-permute-start | bytes 2162696 | tf_op jit(solution)/shard_map/ppermute | solution.py:595
  44.8 19.5 %collective-permute-start.13 = (bf16[352,1024]{1,0:T(8,128)(2,1)}, bf16[352,1024]{1,0:T(8,128)(2,1)}, u32[]{:S(2)}, u32[]{:S(2)}) collective-permute-start(bf16[352,1024]{1,0:T(8,128)(2,1)} %gate.10.refs_4_.refs_11_), channel_id=1, source_target_pairs={{0,16},{16,0},{1,17},{17,1},{2,18},{18,2},{3,19},{19,3},{4,20},{20... | collective-permute-start | bytes 2162696 | tf_op jit(solution)/shard_map/ppermute | solution.py:598
  46.4 28.8 %collective-permute-start.16 = (bf16[352,1024]{1,0:T(8,128)(2,1)}, bf16[352,1024]{1,0:T(8,128)(2,1)S(1)}, u32[]{:S(2)}, u32[]{:S(2)}) collective-permute-start(bf16[352,1024]{1,0:T(8,128)(2,1)} %gate.11.refs_12_), channel_id=1, source_target_pairs={{0,4},{1,3},{4,8},{5,1},{8,12},{9,5},{12,14},{13,9},{14,10},{15,13... | collective-permute-start | bytes 2162696 | tf_op jit(solution)/shard_map/ppermute | solution.py:595
  48.0 27.2 %collective-permute-start.17 = (bf16[4,16,4608]{2,1,0:T(8,128)(2,1)}, bf16[4,16,4608]{2,1,0:T(8,128)(2,1)}, u32[]{:S(2)}, u32[]{:S(2)}) collective-permute-start(bf16[4,16,4608]{2,1,0:T(8,128)(2,1)} %get-tuple-element.57), channel_id=1, source_target_pairs={{0,2},{2,0},{4,6},{6,4},{8,10},{10,8},{12,14},{14,12},{1,3},{3,1},... | collective-permute-start | bytes 1769480 | tf_op jit(solution)/shard_map/ppermute | solution.py:604
  57.2 7.1 %collective-permute-start.12 = (bf16[1024,1024]{1,0:T(8,128)(2,1)}, bf16[1024,1024]{1,0:T(8,128)(2,1)}, u32[]{:S(2)}, u32[]{:S(2)}) collective-permute-start(bf16[1024,1024]{1,0:T(8,128)(2,1)} %get-tuple-element.53), channel_id=1, source_target_pairs={{0,1},{1,0},{2,3},{3,2},{4,5},{5,4},{6,7},{7,6},{8,9},{9,8},{10,11... | collective-permute-start | bytes 6291464 | tf_op jit(solution)/shard_map/ppermute | solution.py:601
  60.3 18.1 %collective-permute-start.18 = (bf16[352,1024]{1,0:T(8,128)(2,1)}, bf16[352,1024]{1,0:T(8,128)(2,1)}, u32[]{:S(2)}, u32[]{:S(2)}) collective-permute-start(bf16[352,1024]{1,0:T(8,128)(2,1)} %gate.12.refs_14_.refs_11_), channel_id=1, source_target_pairs={{0,16},{16,0},{1,17},{17,1},{2,18},{18,2},{3,19},{19,3},{4,20},{20... | collective-permute-start | bytes 2162696 | tf_op jit(solution)/shard_map/ppermute | solution.py:598
  78.3 11.6 %collective-permute-start.22 = (bf16[352,1024]{1,0:T(8,128)(2,1)}, bf16[352,1024]{1,0:T(8,128)(2,1)}, u32[]{:S(2)}, u32[]{:S(2)}) collective-permute-start(bf16[352,1024]{1,0:T(8,128)(2,1)} %broadcast_select_fusion), channel_id=1, source_target_pairs={{0,4},{1,3},{4,8},{5,1},{8,12},{9,5},{12,14},{13,9},{14,10},{15,13... | collective-permute-start | bytes 2162696 | tf_op jit(solution)/shard_map/ppermute | solution.py:595
  78.4 15.1 %collective-permute-start.19 = (bf16[352,1024]{1,0:T(8,128)(2,1)}, bf16[352,1024]{1,0:T(8,128)(2,1)}, u32[]{:S(2)}, u32[]{:S(2)}) collective-permute-start(bf16[352,1024]{1,0:T(8,128)(2,1)} %gate.12.refs_14_.refs_11_), channel_id=1, source_target_pairs={{0,1},{1,0},{2,3},{3,2},{4,5},{5,4},{6,7},{7,6},{8,9},{9,8},{10,11... | collective-permute-start | bytes 2162696 | tf_op jit(solution)/shard_map/ppermute | solution.py:601
  78.4 15.3 %collective-permute-start.21 = (bf16[352,1024]{1,0:T(8,128)(2,1)}, bf16[352,1024]{1,0:T(8,128)(2,1)}, u32[]{:S(2)}, u32[]{:S(2)}) collective-permute-start(bf16[352,1024]{1,0:T(8,128)(2,1)} %collective-permute-done.18.refs_13_), channel_id=1, source_target_pairs={{0,1},{1,0},{2,3},{3,2},{4,5},{5,4},{6,7},{7,6},{8,9},{9,8},{10,11... | collective-permute-start | bytes 2162696 | tf_op jit(solution)/shard_map/ppermute | solution.py:601
  78.9 14.8 %collective-permute-start.20 = (bf16[352,1024]{1,0:T(8,128)(2,1)S(1)}, bf16[352,1024]{1,0:T(8,128)(2,1)}, u32[]{:S(2)}, u32[]{:S(2)}) collective-permute-start(bf16[352,1024]{1,0:T(8,128)(2,1)S(1)} %copy-done.2), channel_id=1, source_target_pairs={{0,1},{1,0},{2,3},{3,2},{4,5},{5,4},{6,7},{7,6},{8,9},{9,8},{10,11... | collective-permute-start | bytes 2162696 | tf_op jit(solution)/shard_map/ppermute | solution.py:601
  79.0 14.7 %collective-permute-start.15 = (bf16[1024,1024]{1,0:T(8,128)(2,1)}, bf16[1024,1024]{1,0:T(8,128)(2,1)}, u32[]{:S(2)}, u32[]{:S(2)}) collective-permute-start(bf16[1024,1024]{1,0:T(8,128)(2,1)} %get-tuple-element.56), channel_id=1, source_target_pairs={{0,1},{1,0},{2,3},{3,2},{4,5},{5,4},{6,7},{7,6},{8,9},{9,8},{10,11... | collective-permute-start | bytes 6291464 | tf_op jit(solution)/shard_map/ppermute | solution.py:601
  89.9 17.9 %collective-permute-start.24 = (bf16[352,1024]{1,0:T(8,128)(2,1)}, bf16[352,1024]{1,0:T(8,128)(2,1)}, u32[]{:S(2)}, u32[]{:S(2)}) collective-permute-start(bf16[352,1024]{1,0:T(8,128)(2,1)} %gate.14.refs_17_.refs_13_.refs_14_), channel_id=1, source_target_pairs={{0,16},{2,18},{4,20},{6,22},{8,24},{10,26},{12,28},{14,30},{16,0},... | collective-permute-start | bytes 2162696 | tf_op jit(solution)/shard_map/ppermute | solution.py:802
  93.5 11.6 %collective-permute-start.25 = (bf16[2,16,4608]{2,1,0:T(8,128)(2,1)}, bf16[2,16,4608]{2,1,0:T(8,128)(2,1)}, u32[]{:S(2)}, u32[]{:S(2)}) collective-permute-start(bf16[2,16,4608]{2,1,0:T(8,128)(2,1)} %get-tuple-element.61), channel_id=1, source_target_pairs={{0,4},{2,6},{4,0},{6,2},{8,12},{10,14},{12,8},{14,10},{1,5},{3,7},... | collective-permute-start | bytes 884744 | tf_op jit(solution)/shard_map/ppermute | solution.py:604
  93.7 16.5 %collective-permute-start.23 = (bf16[352,1024]{1,0:T(8,128)(2,1)}, bf16[352,1024]{1,0:T(8,128)(2,1)}, u32[]{:S(2)}, u32[]{:S(2)}) collective-permute-start(bf16[352,1024]{1,0:T(8,128)(2,1)} %gate.14.refs_17_.refs_13_.refs_14_), channel_id=1, source_target_pairs={{0,1},{1,0},{2,3},{3,2},{4,5},{5,4},{6,7},{7,6},{8,9},{9,8},{10,11... | collective-permute-start | bytes 2162696 | tf_op jit(solution)/shard_map/ppermute | solution.py:601
  108.3 10.1 %collective-permute-start.27 = (bf16[1,16,4608]{2,1,0:T(8,128)(2,1)}, bf16[1,16,4608]{2,1,0:T(8,128)(2,1)S(1)}, u32[]{:S(2)}, u32[]{:S(2)}) collective-permute-start(bf16[1,16,4608]{2,1,0:T(8,128)(2,1)} %get-tuple-element.65), channel_id=1, source_target_pairs={{0,8},{2,10},{4,12},{6,14},{8,0},{10,2},{12,4},{14,6},{1,9},{3,11}... | collective-permute-start | bytes 442376 | tf_op jit(solution)/shard_map/ppermute | solution.py:604
  (16 other events, 43.5 us)

commit v5 on v4

--- a/solution.py
+++ b/solution.py
@@ -12,8 +12,8 @@
 ALL = ("group", "shard", "dp")
 NT = (((1,), (1,)), ((), ()))
 VMEM_LIMIT = 63 << 20
-COST = 1e6
-GATE = 1e5
+COST = 2e8
+GATE = 5e2
 ANY = pl.BlockSpec(memory_space=pl.ANY)
 SMEM = pl.BlockSpec(memory_space=pltpu.SMEM)
 
@@ -780,7 +780,7 @@
 
     whole = [(EDGE, None, None), (MIDDLE, None, middle_cut), (OTHER, None, None)]
     full = [(None, None, None)]
-    state, after, last = (None, None), (middles[1:] or [sums]) + [low_got], None
+    state, after, last = (None, None), (middles[1:] or [sums]), None
     for k in range(1, steps):
         jobs, pieces = [], []
         if k == 1:

time: 122 us -> 121 us (level)
  waiting for transfers between devices: 15.7 us -> 19.5 us
  starting transfers between devices: 26.5 us -> 23.1 us
    ppermute x3, waiting for transfers between devices: 2.04 us -> 4.92 us  [flip(): return lax.ppermute(value, 'shard', [(s, s ^ bit) for s in range(shards)])]
    ppermute x7, waiting for transfers between devices: 10.5 us -> 13.1 us  [around(): return lax.ppermute(value, ALL, ring_pairs)]
    ppermute x3, starting transfers between devices: 5.41 us -> 3.52 us  [partner(): return lax.ppermute(value, 'group', [(g, g ^ 1) for g in range(groups)])]
    ppermute x3, waiting for transfers between devices: 1.63 us -> 0.01 us  [partner(): return lax.ppermute(value, 'group', [(g, g ^ 1) for g in range(groups)])]
  transfers between devices with their start and end apart: 28 -> 28, of which waited for: 7 -> 5; matrix products, arithmetic and copies ran while one was open for 5% -> 5% of each run, Pallas kernels for 54% -> 54%
where the time goes in v5:
time: 121 us
  Pallas kernels  67.6 us (56%)
  starting transfers between devices  23.1 us (19%)
  waiting for transfers between devices  19.5 us (16%)
  local copies, waits for them, and re-layouts  7.33 us (6%)
  other arithmetic  2.21 us (2%)
    pallas_call x4, Pallas kernels, multiply(): pl.pallas_call(functools.partial(weight_kernel, dims, jobs, first, last,...  36.2 us
    ppermute x7, waiting for transfers between devices, around(): return lax.ppermute(value, ALL, ring_pairs)  13.1 us
    ppermute x7, starting transfers between devices, around(): return lax.ppermute(value, ALL, ring_pairs)  11 us
    pallas_call x1, Pallas kernels, body(): pl.pallas_call(functools.partial(head_kernel, dims), out_shape=(sds((flat...  10.4 us
    pallas_call x3, Pallas kernels, halve(): pl.pallas_call(functools.partial(halve_kernel, parts, BITS + bit, len(aft...  9.68 us
    pallas_call x1, Pallas kernels, body(): pl.pallas_call(functools.partial(tail_kernel, dims), out_shape=(sds((flat...  9.54 us
    ppermute x3, waiting for transfers between devices, flip(): return lax.ppermute(value, 'shard', [(s, s ^ bit) for s in range(shards)])  4.92 us
    ppermute x3, starting transfers between devices, partner(): return lax.ppermute(value, 'group', [(g, g ^ 1) for g in range(groups)])  3.52 us
  transfers between devices with their start and end apart: 28, of which 5 were waited for; matrix products, arithmetic and copies ran while one was open for 5% of the time, Pallas kernels for 54%

profile of v5, /device:TPU:0, one launch (start us, length us, event | category | flops | bytes accessed | tf_op | source)
XLA Modules:
  0.0 120.8 jit_solution(3043795843797930876)
XLA Ops:
  1.2 2.6 %constant_dynamic-slice_fusion = (bf16[352,1024]{1,0:T(8,128)(2,1)}, bf16[352,1024]{1,0:T(8,128)(2,1)}) fusion(bf16[1024,1024]{1,0:T(8,128)(2,1)} %refs_8_.1, s32[]{:T(128)S(6)} %select_n.17), kind=kLoop, calls=%fused_computation.3 | loop fusion | bytes 2883588 | tf_op jit(solution)/shard_map/dynamic_slice | solution.py:612
  3.8 2.6 %collective-permute-start.4 = (bf16[352,1024]{1,0:T(8,128)(2,1)}, bf16[352,1024]{1,0:T(8,128)(2,1)}, u32[]{:S(2)}, u32[]{:S(2)}) collective-permute-start(bf16[352,1024]{1,0:T(8,128)(2,1)} %get-tuple-element.68), channel_id=1, source_target_pairs={{0,4},{1,3},{4,8},{5,1},{8,12},{9,5},{12,14},{13,9},{14,10},{15,13... | collective-permute-start | bytes 2162696 | tf_op jit(solution)/shard_map/ppermute | solution.py:595
  6.6 1.5 %collective-permute-start.3 = (bf16[352,1024]{1,0:T(8,128)(2,1)}, bf16[352,1024]{1,0:T(8,128)(2,1)S(1)}, u32[]{:S(2)}, u32[]{:S(2)}) collective-permute-start(bf16[352,1024]{1,0:T(8,128)(2,1)} %get-tuple-element.69), channel_id=1, source_target_pairs={{0,4},{1,3},{4,8},{5,1},{8,12},{9,5},{12,14},{13,9},{14,10},{15,13... | collective-permute-start | bytes 2162696 | tf_op jit(solution)/shard_map/ppermute | solution.py:595
  9.9 10.4 %head.1 = (f32[128,4096]{1,0:T(8,128)}, bf16[384,4096]{1,0:T(8,128)(2,1)}, s32[3,3]{1,0:T(4,128)}, bf16[384,1024]{1,0:T(8,128)(2,1)}, bf16[384,128]{1,0:T(8,128)...) custom-call(s32[16]{0:T(128)} %dynamic-slice_bitcast_fusion.info.refs_0_, s32[6]{0:T(128)} %home.1, ...), custom_call_target="tpu_custom_call" | custom-call | flops 1400000000 | tf_op jit(solution)/shard_map/head/pallas_call | solution.py:623
  20.3 1.6 %collective-permute-start.11 = (bf16[352,1024]{1,0:T(8,128)(2,1)}, bf16[352,1024]{1,0:T(8,128)(2,1)}, u32[]{:S(2)}, u32[]{:S(2)}) collective-permute-start(bf16[352,1024]{1,0:T(8,128)(2,1)} %gate.8.refs_1_.refs_9_), channel_id=1, source_target_pairs={{0,4},{1,3},{4,8},{5,1},{8,12},{9,5},{12,14},{13,9},{14,10},{15,13... | collective-permute-start | bytes 2162696 | tf_op jit(solution)/shard_map/ppermute | solution.py:595
  22.0 1.5 %collective-permute-start.7 = (bf16[352,1024]{1,0:T(8,128)(2,1)}, bf16[352,1024]{1,0:T(8,128)(2,1)}, u32[]{:S(2)}, u32[]{:S(2)}) collective-permute-start(bf16[352,1024]{1,0:T(8,128)(2,1)} %gate.8.refs_1_.refs_9_), channel_id=1, source_target_pairs={{0,16},{16,0},{1,17},{17,1},{2,18},{18,2},{3,19},{19,3},{4,20},{20... | collective-permute-start | bytes 2162696 | tf_op jit(solution)/shard_map/ppermute | solution.py:598
  24.4 2.1 %collective-permute-start.8 = (bf16[352,1024]{1,0:T(8,128)(2,1)}, bf16[352,1024]{1,0:T(8,128)(2,1)S(1)}, u32[]{:S(2)}, u32[]{:S(2)}) collective-permute-start(bf16[352,1024]{1,0:T(8,128)(2,1)} %gate.9.after.refs_10_), channel_id=1, source_target_pairs={{0,4},{1,3},{4,8},{5,1},{8,12},{9,5},{12,14},{13,9},{14,10},{15,13... | collective-permute-start | bytes 2162696 | tf_op jit(solution)/shard_map/ppermute | solution.py:595
  26.5 9.5 %tail.1 = (f32[128,4096]{1,0:T(8,128)}, f32[128,512]{1,0:T(8,128)}, f32[128,512]{1,0:T(8,128)}, bf16[384,4096]{1,0:T(8,128)(2,1)}, bf16[768,128]{1,0:T(8,128)(2,1)}, /*index=5*/bf16[384,128]{1,0:T(8,128)(2,1)}) custom-call(s32[16]{0:T(128)} %dynamic-slice_bitcast_fusion.info.refs_0_, s32[6]{0:T(128)} %adapter.3, s32[8]{0:T(128)} %owner.3, ...), custom_call_target="tpu_custom_call" | custom-call | flops 1400000000 | tf_op jit(solution)/shard_map/tail/pallas_call | solution.py:672
  39.8 4.1 %halve.3 = (f32[4,16,4608]{2,1,0:T(8,128)}, bf16[4,16,4608]{2,1,0:T(8,128)(2,1)}) custom-call(s32[16]{0:T(128)} %dynamic-slice_bitcast_fusion.info.refs_0_, f32[4,2,16,4096]{3,2,1,0:T(8,128)} %bitcast.25, f32[4,2,16,512]{3,2,1,0:T(8,128)} %bitcast.30, f32[4,2,16,4096]{3,2,1,0:T(8,128)} %bitcast.8.refs_2_, f32[4,2,16,512]{3,2,1,0:T(8,128)} %bitcast.31, ...), custom_call_target="tpu_custom_call" | custom-call | flops 400000000 | tf_op jit(solution)/shard_map/halve/pallas_call | solution.py:711
  44.0 1.6 %collective-permute-start.14 = (bf16[352,1024]{1,0:T(8,128)(2,1)}, bf16[352,1024]{1,0:T(8,128)(2,1)}, u32[]{:S(2)}, u32[]{:S(2)}) collective-permute-start(bf16[352,1024]{1,0:T(8,128)(2,1)} %gate.10.refs_4_.refs_11_), channel_id=1, source_target_pairs={{0,4},{1,3},{4,8},{5,1},{8,12},{9,5},{12,14},{13,9},{14,10},{15,13... | collective-permute-start | bytes 2162696 | tf_op jit(solution)/shard_map/ppermute | solution.py:595
  45.6 1.6 %collective-permute-start.16 = (bf16[352,1024]{1,0:T(8,128)(2,1)}, bf16[352,1024]{1,0:T(8,128)(2,1)S(1)}, u32[]{:S(2)}, u32[]{:S(2)}) collective-permute-start(bf16[352,1024]{1,0:T(8,128)(2,1)} %gate.11.refs_12_), channel_id=1, source_target_pairs={{0,4},{1,3},{4,8},{5,1},{8,12},{9,5},{12,14},{13,9},{14,10},{15,13... | collective-permute-start | bytes 2162696 | tf_op jit(solution)/shard_map/ppermute | solution.py:595
  47.6 8.8 %weights.4 = (bf16[384,8192]{1,0:T(8,128)(2,1)}, f32[384,1024]{1,0:T(8,128)}, bf16[1024,1024]{1,0:T(8,128)(2,1)}) custom-call(s32[16]{0:T(128)} %dynamic-slice_bitcast_fusion.info.refs_0_, s32[3,3]{1,0:T(4,128)} %get-tuple-element.36.table.refs_1_, bf16[768,8192]{1,0:T(8,128)(2,1)} %refs_2_.7, bf16[384,4096]{1,0:T(8,128)(2,1)} %collective-permute-done.2.refs_3_, ...), custom_call_target="tpu_custom_call" | custom-call | flops 1400000000 | tf_op jit(solution)/shard_map/weights/pallas_call | solution.py:747
  56.5 5.4 %collective-permute-done.14.refs_0_ = bf16[352,1024]{1,0:T(8,128)(2,1)} collective-permute-done((bf16[352,1024]{1,0:T(8,128)(2,1)}, bf16[352,1024]{1,0:T(8,128)(2,1)}, u32[]{:S(2)}, u32[]{:S(2)}) %collective-permute-start.14) | collective-permute-done | bytes 720928 | tf_op jit(solution)/shard_map/ppermute | solution.py:595
  62.5 9.5 %weights.5 = (bf16[384,8192]{1,0:T(8,128)(2,1)}, f32[384,1024]{1,0:T(8,128)}, bf16[1024,1024]{1,0:T(8,128)(2,1)}) custom-call(s32[16]{0:T(128)} %dynamic-slice_bitcast_fusion.info.refs_0_, s32[3,3]{1,0:T(4,128)} %get-tuple-element.36.table.refs_1_, bf16[768,8192]{1,0:T(8,128)(2,1)} %refs_2_.7, ...), custom_call_target="tpu_custom_call", output_to_operand_aliasing={{0}: (9, {})} | custom-call | flops 1400000000 | tf_op jit(solution)/shard_map/weights/pallas_call | solution.py:747
  72.0 4.0 %collective-permute-done.17.refs_2_ = bf16[4,16,4608]{2,1,0:T(8,128)(2,1)} collective-permute-done((bf16[4,16,4608]{2,1,0:T(8,128)(2,1)}, bf16[4,16,4608]{2,1,0:T(8,128)(2,1)}, u32[]{:S(2)}, u32[]{:S(2)}) %collective-permute-start.17) | collective-permute-done | bytes 589856 | tf_op jit(solution)/shard_map/ppermute | solution.py:604
  76.9 2.2 %broadcast_select_fusion = bf16[352,1024]{1,0:T(8,128)(2,1)} fusion(bf16[352,1024]{1,0:T(8,128)(2,1)} %gate.12.refs_14_.refs_11_, bf16[352,1024]{1,0:T(8,128)(2,1)} %gate.13.refs_2_.refs_1_.refs_12_, pred[]{:T(512)S(6)} %eq.7), kind=kLoop, calls=%fused_computation | loop fusion | flops 360448 | bytes 2162689 | tf_op jit(solution)/shard_map/jit(_where)/select_n | solution.py:814
  80.1 2.9 %halve.4 = (f32[2,16,4608]{2,1,0:T(8,128)}, bf16[2,16,4608]{2,1,0:T(8,128)(2,1)}) custom-call(s32[16]{0:T(128)} %dynamic-slice_bitcast_fusion.info.refs_0_, f32[2,2,16,4608]{3,2,1,0:T(8,128)} %bitcast.26, bf16[2,2,16,4608]{3,2,1,0:T(8,128)(2,1)} %bitcast.11.refs_1_, bf16[352,1024]{1,0:T(8,128)(2,1)} %gate.13.refs_2_.refs_1_.refs_12_), custom_call_target="tpu_custom_call" | custom-call | flops 400000000 | tf_op jit(solution)/shard_map/halve/pallas_call | solution.py:711
  83.0 7.6 %collective-permute-done.22.refs_0_ = bf16[352,1024]{1,0:T(8,128)(2,1)} collective-permute-done((bf16[352,1024]{1,0:T(8,128)(2,1)}, bf16[352,1024]{1,0:T(8,128)(2,1)}, u32[]{:S(2)}, u32[]{:S(2)}) %collective-permute-start.22) | collective-permute-done | bytes 720928 | tf_op jit(solution)/shard_map/ppermute | solution.py:595
  90.7 2.7 %collective-permute-start.24 = (bf16[352,1024]{1,0:T(8,128)(2,1)}, bf16[352,1024]{1,0:T(8,128)(2,1)}, u32[]{:S(2)}, u32[]{:S(2)}) collective-permute-start(bf16[352,1024]{1,0:T(8,128)(2,1)} %gate.14.refs_17_.refs_13_.refs_14_), channel_id=1, source_target_pairs={{0,16},{2,18},{4,20},{6,22},{8,24},{10,26},{12,28},{14,30},{16,0},... | collective-permute-start | bytes 2162696 | tf_op jit(solution)/shard_map/ppermute | solution.py:802
  93.5 11.4 %weights.6 = (bf16[384,8192]{1,0:T(8,128)(2,1)}, f32[384,1024]{1,0:T(8,128)}) custom-call(s32[16]{0:T(128)} %dynamic-slice_bitcast_fusion.info.refs_0_, s32[3,3]{1,0:T(4,128)} %get-tuple-element.36.table.refs_1_, bf16[768,8192]{1,0:T(8,128)(2,1)} %refs_2_.7, bf16[384,4096]{1,0:T(8,128)(2,1)} %collective-permute-done.2.refs_3_, ...), custom_call_target="tpu_custom_call", output_to_operand_aliasing={{0}: (9, {})} | custom-call | flops 1400000000 | tf_op jit(solution)/shard_map/weights/pallas_call | solution.py:747
  104.9 2.6 %halve.5 = (f32[1,16,4608]{2,1,0:T(8,128)}, bf16[1,16,4608]{2,1,0:T(8,128)(2,1)}) custom-call(s32[16]{0:T(128)} %dynamic-slice_bitcast_fusion.info.refs_0_, f32[1,2,16,4608]{3,2,1,0:T(8,128)} %bitcast.29, bf16[1,2,16,4608]{3,2,1,0:T(8,128)(2,1)} %bitcast.13.refs_1_, f32[384,1024]{1,0:T(8,128)} %get-tuple-element.59.refs_2_.refs_1_.refs_11_), custom_call_target="tpu_custom_call" | custom-call | flops 400000000 | tf_op jit(solution)/shard_map/halve/pallas_call | solution.py:711
  108.5 2.0 %collective-permute-start.27 = (bf16[1,16,4608]{2,1,0:T(8,128)(2,1)S(1)}, bf16[1,16,4608]{2,1,0:T(8,128)(2,1)}, u32[]{:S(2)}, u32[]{:S(2)}) collective-permute-start(bf16[1,16,4608]{2,1,0:T(8,128)(2,1)S(1)} %copy-done.11), channel_id=1, source_target_pairs={{0,8},{2,10},{4,12},{6,14},{8,0},{10,2},{12,4},{14,6},{1,9},{3,11}... | collective-permute-start | bytes 442376 | tf_op jit(solution)/shard_map/ppermute | solution.py:604
  111.3 6.6 %weights.7 = (bf16[384,8192]{1,0:T(8,128)(2,1)}, bf16[384,1024]{1,0:T(8,128)(2,1)}) custom-call(s32[16]{0:T(128)} %dynamic-slice_bitcast_fusion.info.refs_0_, s32[3,3]{1,0:T(4,128)} %get-tuple-element.36.table.refs_1_, bf16[768,8192]{1,0:T(8,128)(2,1)} %refs_2_.7, ...), custom_call_target="tpu_custom_call", output_to_operand_aliasing={{0}: (12, {})} | custom-call | flops 800000000 | tf_op jit(solution)/shard_map/weights/pallas_call | solution.py:747
  118.8 1.8 %final.1 = (f32[16,4096]{1,0:T(8,128)}, f32[16,512]{1,0:T(8,128)}) custom-call(f32[16,4608]{1,0:T(8,128)} %bitcast.35, bf16[16,4608]{1,0:T(8,128)(2,1)} %bitcast.15.moved, bf16[384,1024]{1,0:T(8,128)(2,1)} %get-tuple-element.32.after), custom_call_target="tpu_custom_call" | custom-call | flops 400000000 | tf_op jit(solution)/shard_map/final/pallas_call | solution.py:835
  (78 shorter events, 13.1 us)
Async XLA Ops:
  0.7 8.7 %collective-permute-start.1 = (bf16[384,1024]{1,0:T(8,128)(2,1)}, bf16[384,1024]{1,0:T(8,128)(2,1)}, u32[]{:S(2)}, u32[]{:S(2)}) collective-permute-start(bf16[384,1024]{1,0:T(8,128)(2,1)} %grad.1), channel_id=1, source_target_pairs={{0,1},{1,0},{2,3},{3,2},{4,5},{5,4},{6,7},{7,6},{8,9},{9,8},{10,11... | collective-permute-start | bytes 2359304 | tf_op jit(solution)/shard_map/ppermute | solution.py:601
  3.8 16.6 %collective-permute-start.4 = (bf16[352,1024]{1,0:T(8,128)(2,1)}, bf16[352,1024]{1,0:T(8,128)(2,1)}, u32[]{:S(2)}, u32[]{:S(2)}) collective-permute-start(bf16[352,1024]{1,0:T(8,128)(2,1)} %get-tuple-element.68), channel_id=1, source_target_pairs={{0,4},{1,3},{4,8},{5,1},{8,12},{9,5},{12,14},{13,9},{14,10},{15,13... | collective-permute-start | bytes 2162696 | tf_op jit(solution)/shard_map/ppermute | solution.py:595
  6.6 16.9 %collective-permute-start.3 = (bf16[352,1024]{1,0:T(8,128)(2,1)}, bf16[352,1024]{1,0:T(8,128)(2,1)S(1)}, u32[]{:S(2)}, u32[]{:S(2)}) collective-permute-start(bf16[352,1024]{1,0:T(8,128)(2,1)} %get-tuple-element.69), channel_id=1, source_target_pairs={{0,4},{1,3},{4,8},{5,1},{8,12},{9,5},{12,14},{13,9},{14,10},{15,13... | collective-permute-start | bytes 2162696 | tf_op jit(solution)/shard_map/ppermute | solution.py:595
  20.3 15.7 %collective-permute-start.11 = (bf16[352,1024]{1,0:T(8,128)(2,1)}, bf16[352,1024]{1,0:T(8,128)(2,1)}, u32[]{:S(2)}, u32[]{:S(2)}) collective-permute-start(bf16[352,1024]{1,0:T(8,128)(2,1)} %gate.8.refs_1_.refs_9_), channel_id=1, source_target_pairs={{0,4},{1,3},{4,8},{5,1},{8,12},{9,5},{12,14},{13,9},{14,10},{15,13... | collective-permute-start | bytes 2162696 | tf_op jit(solution)/shard_map/ppermute | solution.py:595
  22.0 23.6 %collective-permute-start.7 = (bf16[352,1024]{1,0:T(8,128)(2,1)}, bf16[352,1024]{1,0:T(8,128)(2,1)}, u32[]{:S(2)}, u32[]{:S(2)}) collective-permute-start(bf16[352,1024]{1,0:T(8,128)(2,1)} %gate.8.refs_1_.refs_9_), channel_id=1, source_target_pairs={{0,16},{16,0},{1,17},{17,1},{2,18},{18,2},{3,19},{19,3},{4,20},{20... | collective-permute-start | bytes 2162696 | tf_op jit(solution)/shard_map/ppermute | solution.py:598
  23.5 23.7 %collective-permute-start.2 = (bf16[384,4096]{1,0:T(8,128)(2,1)}, bf16[384,4096]{1,0:T(8,128)(2,1)}, u32[]{:S(2)}, u32[]{:S(2)}) collective-permute-start(bf16[384,4096]{1,0:T(8,128)(2,1)} %get-tuple-element.37), channel_id=1, source_target_pairs={{0,1},{1,0},{2,3},{3,2},{4,5},{5,4},{6,7},{7,6},{8,9},{9,8},{10,11... | collective-permute-start | bytes 9437192 | tf_op jit(solution)/shard_map/ppermute | solution.py:601
  24.4 19.6 %collective-permute-start.8 = (bf16[352,1024]{1,0:T(8,128)(2,1)}, bf16[352,1024]{1,0:T(8,128)(2,1)S(1)}, u32[]{:S(2)}, u32[]{:S(2)}) collective-permute-start(bf16[352,1024]{1,0:T(8,128)(2,1)} %gate.9.after.refs_10_), channel_id=1, source_target_pairs={{0,4},{1,3},{4,8},{5,1},{8,12},{9,5},{12,14},{13,9},{14,10},{15,13... | collective-permute-start | bytes 2162696 | tf_op jit(solution)/shard_map/ppermute | solution.py:595
  26.4 11.9 %collective-permute-start.9 = (f32[128,4096]{1,0:T(8,128)}, f32[128,4096]{1,0:T(8,128)}, u32[]{:S(2)}, u32[]{:S(2)}) collective-permute-start(f32[128,4096]{1,0:T(8,128)} %get-tuple-element.48), channel_id=1, source_target_pairs={{0,1},{1,0},{2,3},{3,2},{4,5},{5,4},{6,7},{7,6},{8,9},{9,8},{10,11... | collective-permute-start | bytes 6291464 | tf_op jit(solution)/shard_map/ppermute | solution.py:601
  38.0 9.7 %collective-permute-start.5 = (bf16[384,4096]{1,0:T(8,128)(2,1)}, bf16[384,4096]{1,0:T(8,128)(2,1)}, u32[]{:S(2)}, u32[]{:S(2)}) collective-permute-start(bf16[384,4096]{1,0:T(8,128)(2,1)} %get-tuple-element.41), channel_id=1, source_target_pairs={{0,1},{1,0},{2,3},{3,2},{4,5},{5,4},{6,7},{7,6},{8,9},{9,8},{10,11... | collective-permute-start | bytes 9437192 | tf_op jit(solution)/shard_map/ppermute | solution.py:601
  38.3 24.2 %collective-permute-start.13 = (bf16[352,1024]{1,0:T(8,128)(2,1)}, bf16[352,1024]{1,0:T(8,128)(2,1)}, u32[]{:S(2)}, u32[]{:S(2)}) collective-permute-start(bf16[352,1024]{1,0:T(8,128)(2,1)} %gate.10.refs_4_.refs_11_), channel_id=1, source_target_pairs={{0,16},{16,0},{1,17},{17,1},{2,18},{18,2},{3,19},{19,3},{4,20},{20... | collective-permute-start | bytes 2162696 | tf_op jit(solution)/shard_map/ppermute | solution.py:598
  44.0 18.0 %collective-permute-start.14 = (bf16[352,1024]{1,0:T(8,128)(2,1)}, bf16[352,1024]{1,0:T(8,128)(2,1)}, u32[]{:S(2)}, u32[]{:S(2)}) collective-permute-start(bf16[352,1024]{1,0:T(8,128)(2,1)} %gate.10.refs_4_.refs_11_), channel_id=1, source_target_pairs={{0,4},{1,3},{4,8},{5,1},{8,12},{9,5},{12,14},{13,9},{14,10},{15,13... | collective-permute-start | bytes 2162696 | tf_op jit(solution)/shard_map/ppermute | solution.py:595
  45.6 30.4 %collective-permute-start.16 = (bf16[352,1024]{1,0:T(8,128)(2,1)}, bf16[352,1024]{1,0:T(8,128)(2,1)S(1)}, u32[]{:S(2)}, u32[]{:S(2)}) collective-permute-start(bf16[352,1024]{1,0:T(8,128)(2,1)} %gate.11.refs_12_), channel_id=1, source_target_pairs={{0,4},{1,3},{4,8},{5,1},{8,12},{9,5},{12,14},{13,9},{14,10},{15,13... | collective-permute-start | bytes 2162696 | tf_op jit(solution)/shard_map/ppermute | solution.py:595
  47.2 28.8 %collective-permute-start.17 = (bf16[4,16,4608]{2,1,0:T(8,128)(2,1)}, bf16[4,16,4608]{2,1,0:T(8,128)(2,1)}, u32[]{:S(2)}, u32[]{:S(2)}) collective-permute-start(bf16[4,16,4608]{2,1,0:T(8,128)(2,1)} %get-tuple-element.57), channel_id=1, source_target_pairs={{0,2},{2,0},{4,6},{6,4},{8,10},{10,8},{12,14},{14,12},{1,3},{3,1},... | collective-permute-start | bytes 1769480 | tf_op jit(solution)/shard_map/ppermute | solution.py:604
  56.4 6.1 %collective-permute-start.12 = (bf16[1024,1024]{1,0:T(8,128)(2,1)}, bf16[1024,1024]{1,0:T(8,128)(2,1)}, u32[]{:S(2)}, u32[]{:S(2)}) collective-permute-start(bf16[1024,1024]{1,0:T(8,128)(2,1)} %get-tuple-element.53), channel_id=1, source_target_pairs={{0,1},{1,0},{2,3},{3,2},{4,5},{5,4},{6,7},{7,6},{8,9},{9,8},{10,11... | collective-permute-start | bytes 6291464 | tf_op jit(solution)/shard_map/ppermute | solution.py:601
  62.0 17.1 %collective-permute-start.18 = (bf16[352,1024]{1,0:T(8,128)(2,1)}, bf16[352,1024]{1,0:T(8,128)(2,1)}, u32[]{:S(2)}, u32[]{:S(2)}) collective-permute-start(bf16[352,1024]{1,0:T(8,128)(2,1)} %gate.12.refs_14_.refs_11_), channel_id=1, source_target_pairs={{0,16},{16,0},{1,17},{17,1},{2,18},{18,2},{3,19},{19,3},{4,20},{20... | collective-permute-start | bytes 2162696 | tf_op jit(solution)/shard_map/ppermute | solution.py:598
  79.1 11.6 %collective-permute-start.22 = (bf16[352,1024]{1,0:T(8,128)(2,1)}, bf16[352,1024]{1,0:T(8,128)(2,1)}, u32[]{:S(2)}, u32[]{:S(2)}) collective-permute-start(bf16[352,1024]{1,0:T(8,128)(2,1)} %broadcast_select_fusion), channel_id=1, source_target_pairs={{0,4},{1,3},{4,8},{5,1},{8,12},{9,5},{12,14},{13,9},{14,10},{15,13... | collective-permute-start | bytes 2162696 | tf_op jit(solution)/shard_map/ppermute | solution.py:595
  79.1 14.3 %collective-permute-start.19 = (bf16[352,1024]{1,0:T(8,128)(2,1)}, bf16[352,1024]{1,0:T(8,128)(2,1)}, u32[]{:S(2)}, u32[]{:S(2)}) collective-permute-start(bf16[352,1024]{1,0:T(8,128)(2,1)} %gate.12.refs_14_.refs_11_), channel_id=1, source_target_pairs={{0,1},{1,0},{2,3},{3,2},{4,5},{5,4},{6,7},{7,6},{8,9},{9,8},{10,11... | collective-permute-start | bytes 2162696 | tf_op jit(solution)/shard_map/ppermute | solution.py:601
  79.1 14.3 %collective-permute-start.21 = (bf16[352,1024]{1,0:T(8,128)(2,1)}, bf16[352,1024]{1,0:T(8,128)(2,1)}, u32[]{:S(2)}, u32[]{:S(2)}) collective-permute-start(bf16[352,1024]{1,0:T(8,128)(2,1)} %collective-permute-done.18.refs_13_), channel_id=1, source_target_pairs={{0,1},{1,0},{2,3},{3,2},{4,5},{5,4},{6,7},{7,6},{8,9},{9,8},{10,11... | collective-permute-start | bytes 2162696 | tf_op jit(solution)/shard_map/ppermute | solution.py:601
  79.6 13.9 %collective-permute-start.20 = (bf16[352,1024]{1,0:T(8,128)(2,1)S(1)}, bf16[352,1024]{1,0:T(8,128)(2,1)}, u32[]{:S(2)}, u32[]{:S(2)}) collective-permute-start(bf16[352,1024]{1,0:T(8,128)(2,1)S(1)} %copy-done.2), channel_id=1, source_target_pairs={{0,1},{1,0},{2,3},{3,2},{4,5},{5,4},{6,7},{7,6},{8,9},{9,8},{10,11... | collective-permute-start | bytes 2162696 | tf_op jit(solution)/shard_map/ppermute | solution.py:601
  79.6 13.9 %collective-permute-start.15 = (bf16[1024,1024]{1,0:T(8,128)(2,1)}, bf16[1024,1024]{1,0:T(8,128)(2,1)}, u32[]{:S(2)}, u32[]{:S(2)}) collective-permute-start(bf16[1024,1024]{1,0:T(8,128)(2,1)} %get-tuple-element.56), channel_id=1, source_target_pairs={{0,1},{1,0},{2,3},{3,2},{4,5},{5,4},{6,7},{7,6},{8,9},{9,8},{10,11... | collective-permute-start | bytes 6291464 | tf_op jit(solution)/shard_map/ppermute | solution.py:601
  90.7 16.9 %collective-permute-start.24 = (bf16[352,1024]{1,0:T(8,128)(2,1)}, bf16[352,1024]{1,0:T(8,128)(2,1)}, u32[]{:S(2)}, u32[]{:S(2)}) collective-permute-start(bf16[352,1024]{1,0:T(8,128)(2,1)} %gate.14.refs_17_.refs_13_.refs_14_), channel_id=1, source_target_pairs={{0,16},{2,18},{4,20},{6,22},{8,24},{10,26},{12,28},{14,30},{16,0},... | collective-permute-start | bytes 2162696 | tf_op jit(solution)/shard_map/ppermute | solution.py:802
  93.3 11.6 %collective-permute-start.25 = (bf16[2,16,4608]{2,1,0:T(8,128)(2,1)}, bf16[2,16,4608]{2,1,0:T(8,128)(2,1)}, u32[]{:S(2)}, u32[]{:S(2)}) collective-permute-start(bf16[2,16,4608]{2,1,0:T(8,128)(2,1)} %get-tuple-element.61), channel_id=1, source_target_pairs={{0,4},{2,6},{4,0},{6,2},{8,12},{10,14},{12,8},{14,10},{1,5},{3,7},... | collective-permute-start | bytes 884744 | tf_op jit(solution)/shard_map/ppermute | solution.py:604
  93.4 17.0 %collective-permute-start.23 = (bf16[352,1024]{1,0:T(8,128)(2,1)}, bf16[352,1024]{1,0:T(8,128)(2,1)}, u32[]{:S(2)}, u32[]{:S(2)}) collective-permute-start(bf16[352,1024]{1,0:T(8,128)(2,1)} %gate.14.refs_17_.refs_13_.refs_14_), channel_id=1, source_target_pairs={{0,1},{1,0},{2,3},{3,2},{4,5},{5,4},{6,7},{7,6},{8,9},{9,8},{10,11... | collective-permute-start | bytes 2162696 | tf_op jit(solution)/shard_map/ppermute | solution.py:601
  108.5 10.4 %collective-permute-start.27 = (bf16[1,16,4608]{2,1,0:T(8,128)(2,1)S(1)}, bf16[1,16,4608]{2,1,0:T(8,128)(2,1)}, u32[]{:S(2)}, u32[]{:S(2)}) collective-permute-start(bf16[1,16,4608]{2,1,0:T(8,128)(2,1)S(1)} %copy-done.11), channel_id=1, source_target_pairs={{0,8},{2,10},{4,12},{6,14},{8,0},{10,2},{12,4},{14,6},{1,9},{3,11}... | collective-permute-start | bytes 442376 | tf_op jit(solution)/shard_map/ppermute | solution.py:604
  (16 other events, 38.3 us)
